TPU v7x, 512 devices: a whole 4x4x16 slice. The times are simulated.
512 devices in a mesh: dp: 128 (over z, y_lo, x), ctx: 4 (over y_hi, core).
Axes of the slice: x: 4, y: 4 (y_hi: 2, y_lo: 2; y = y_hi * 2 + y_lo), z: 16, core: 2. Of those that a mesh axis runs over, the one named last changes fastest.
Arguments:
- hidden: bfloat16 [65536, 1024], P(('dp', 'ctx')), may hold values from -80 to 80
- doc_len: int32 [128], P('dp'), may hold values from 256 to 512, as said below
- doc_keep: int32 [65536], P(('dp', 'ctx')), may hold values 0 or 1
- w_query: bfloat16 [1024, 512], replicated, may hold values from -1 to 1
- w_key: bfloat16 [1024, 512], replicated, may hold values from -1 to 1
- w_value: bfloat16 [1024, 512], replicated, may hold values from -0.1875 to 0.1875
- w_out: bfloat16 [512, 1024], replicated, may hold values from -0.25 to 0.25
- ln_gain: float32 [1024], replicated, may hold values from 0.5 to 2
- w_proj: bfloat16 [1024, 128], replicated, may hold values from -0.1875 to 0.1875
- queries: bfloat16 [512, 32, 128], P(('dp', 'ctx')), may hold values from -8.5 to 8.5
- query_mask: bfloat16 [512, 32], P(('dp', 'ctx')), may hold values from 0.19921875 to 1
- positive: int32 [512], P(('dp', 'ctx')), may hold values from 0 to 127
Outputs:
- d_hidden: bfloat16 [65536, 1024], P(('dp', 'ctx'))
- loss: float32 [], replicated
Inputs may be any that keep to these rules, and one draw needn't show every extreme that they name: `doc_len`: some document has exactly 512 valid tokens and some exactly 256.
All inputs are finite; a program needn't handle non-finite values. No bound on the sum of `doc_keep` on one device may be relied on, other than what follows from the above.
Results may differ from a plain program's by a relative error of at most 0.035.
The roundings to bfloat16 on the way count: a program that leaves them out, or rounds other values in their place, can miss the bound.
Values may be sent and summed in bfloat16 or wider, within the bound.
No kernel may reach another device: no remote copies, remote signals or barrier semaphores. Data moves between devices by JAX's collectives and lax.ppermute only.
A program may use at most 64 MiB of HBM per device.

v0:
```python
import math

import jax
import jax.numpy as jnp
from jax import lax
from jax.sharding import PartitionSpec as P

HD = 64


TAU = 0.05
GRAD_SCALE = 1024.0
NEG = -1e30


def dot32(left, right):
    return jnp.dot(left, right, preferred_element_type=jnp.float32)


def split_heads(t):
    return t.reshape(t.shape[0], -1, HD)


def soft_sums(qset, embed, mask):
    count, qlen, width = qset.shape
    block = math.gcd(count, 64)
    groups = qset.reshape(count // block, block, qlen, width)

    def one(group):
        close = jnp.einsum("bie,je->bij", group, embed, preferred_element_type=jnp.float32)
        return jnp.sum(jnp.exp(close / TAU) * mask, -1)

    return lax.map(one, groups).reshape(count, qlen)


def token_grads(qset, embed, mask, coef):
    count, qlen, width = qset.shape
    block = math.gcd(count, 64)
    groups = qset.reshape(count // block, block, qlen, width)
    coefs = coef.reshape(count // block, block, qlen)

    def step(carry, pair):
        group, factor = pair
        close = jnp.einsum("bie,je->bij", group, embed, preferred_element_type=jnp.float32)
        coupling = (jnp.exp(close / TAU) * mask * factor[..., None]).astype(jnp.bfloat16)
        return (
            carry + jnp.einsum("bij,bie->je", coupling, group, preferred_element_type=jnp.float32),
            None,
        )

    start = jnp.zeros((embed.shape[0], width), jnp.float32)
    total, unused = lax.scan(step, start, (groups, coefs))
    return total


def contrast(table, pos_set, mine):
    docs = table.shape[0]
    lse = jnp.log(jnp.sum(jnp.exp(table), 0))
    hit = jnp.arange(docs, dtype=jnp.int32)[:, None] == pos_set[None, :]
    target = jnp.sum(jnp.where(hit, table, 0.0), 0)
    total = jnp.sum(lse - target)
    row = lax.dynamic_index_in_dim(table, mine, 0, keepdims=False)
    dscore = GRAD_SCALE * (jnp.exp(row - lse) - (pos_set == mine).astype(jnp.float32))
    return (total, dscore)


def body(
    hidden,
    doc_len,
    doc_keep,
    w_query,
    w_key,
    w_value,
    w_out,
    ln_gain,
    w_proj,
    queries,
    query_mask,
    positive,
):
    rows = hidden.shape[0]
    width = rows * lax.axis_size("ctx")
    place = lax.axis_index("ctx") * rows + jnp.arange(rows, dtype=jnp.int32)
    length = doc_len[0]
    keep = jnp.where((place < length) & ((doc_keep == 1) | (place == 0)), 1.0, 0.0).astype(
        jnp.float32
    )
    query = dot32(hidden, w_query).astype(jnp.bfloat16)
    keyed_own = dot32(hidden, w_key).astype(jnp.bfloat16)
    value_own = dot32(hidden, w_value).astype(jnp.bfloat16)
    keyed, value = (
        lax.all_gather(keyed_own, "ctx", axis=0, tiled=True),
        lax.all_gather(value_own, "ctx", axis=0, tiled=True),
    )
    valid = jnp.arange(width, dtype=jnp.int32) < length
    scores = jnp.einsum(
        "rhc,jhc->hrj", split_heads(query), split_heads(keyed), preferred_element_type=jnp.float32
    ) * HD ** (-0.5)
    scores = jnp.where(valid[None, None, :], scores, NEG)
    top = jnp.max(scores, -1, keepdims=True)
    expo = jnp.exp(scores - top)
    denom = jnp.sum(expo, -1, keepdims=True)
    probs = expo / denom
    probs_b = probs.astype(jnp.bfloat16)
    attended = jnp.einsum(
        "hrj,jhc->rhc", probs_b, split_heads(value), preferred_element_type=jnp.float32
    )
    attended = attended.reshape(rows, -1).astype(jnp.bfloat16)
    mixed = hidden.astype(jnp.float32) + dot32(attended, w_out)
    centred = mixed - jnp.mean(mixed, -1, keepdims=True)
    inv = lax.rsqrt(jnp.mean(centred * centred, -1, keepdims=True) + 1e-05)
    unit = centred * inv
    normed = (unit * ln_gain).astype(jnp.bfloat16)
    proj = dot32(normed, w_proj)
    scale = lax.rsqrt(jnp.sum(proj * proj, -1, keepdims=True) + 1e-06)
    embed_f = proj * scale
    embed = embed_f.astype(jnp.bfloat16)
    qfull = queries.astype(jnp.float32)
    qn = (qfull * lax.rsqrt(jnp.sum(qfull * qfull, -1, keepdims=True) + 1e-06)).astype(jnp.bfloat16)
    mine = lax.axis_index("dp")
    qset, qmask_set, pos_set = (
        lax.all_gather(qn, ("dp", "ctx"), axis=0, tiled=True),
        lax.all_gather(query_mask, ("dp", "ctx"), axis=0, tiled=True),
        lax.all_gather(positive, ("dp", "ctx"), axis=0, tiled=True),
    )
    qmask_f = qmask_set.astype(jnp.float32)
    sums = lax.psum(soft_sums(qset, embed, keep), "ctx")
    column = jnp.sum(qmask_f * TAU * jnp.log(sums), -1)
    table = lax.all_gather(column[None, :], "dp", axis=0, tiled=True)
    loss, dscore = contrast(table, pos_set, mine)
    coef = dscore[:, None] * qmask_f / sums
    embed_grad = token_grads(qset, embed, keep, coef)
    proj_grad = (
        (embed_grad - embed_f * jnp.sum(embed_f * embed_grad, -1, keepdims=True)) * scale
    ).astype(jnp.bfloat16)
    normed_grad = dot32(proj_grad, w_proj.T)
    gained = normed_grad * ln_gain
    mixed_grad = inv * (
        gained
        - jnp.mean(gained, -1, keepdims=True)
        - unit * jnp.mean(gained * unit, -1, keepdims=True)
    )
    mixed_b = mixed_grad.astype(jnp.bfloat16)
    attended_grad = dot32(mixed_b, w_out.T).astype(jnp.bfloat16)
    delta = jnp.transpose(
        jnp.sum(
            split_heads(attended_grad).astype(jnp.float32)
            * split_heads(attended).astype(jnp.float32),
            -1,
        )
    )
    inner = jnp.einsum(
        "rhc,jhc->hrj",
        split_heads(attended_grad),
        split_heads(value),
        preferred_element_type=jnp.float32,
    )
    score_grad = (probs * (inner - delta[..., None]) * HD ** (-0.5)).astype(jnp.bfloat16)
    q_grad = jnp.einsum(
        "hrj,jhc->rhc", score_grad, split_heads(keyed), preferred_element_type=jnp.float32
    )
    q_grad = q_grad.reshape(rows, -1).astype(jnp.bfloat16)
    k_part = jnp.einsum(
        "hrj,rhc->jhc", score_grad, split_heads(query), preferred_element_type=jnp.float32
    ).reshape(width, -1)
    v_part = jnp.einsum(
        "hrj,rhc->jhc", probs_b, split_heads(attended_grad), preferred_element_type=jnp.float32
    ).reshape(width, -1)
    k_sum, v_sum = (
        lax.psum_scatter(
            k_part.astype(jnp.bfloat16), "ctx", scatter_dimension=0, tiled=True
        ).astype(jnp.float32),
        lax.psum_scatter(
            v_part.astype(jnp.bfloat16), "ctx", scatter_dimension=0, tiled=True
        ).astype(jnp.float32),
    )
    k_grad = k_sum.astype(jnp.bfloat16)
    v_grad = v_sum.astype(jnp.bfloat16)
    total = (
        mixed_grad + dot32(q_grad, w_query.T) + dot32(k_grad, w_key.T) + dot32(v_grad, w_value.T)
    )
    return (total.astype(jnp.bfloat16), loss)


def solution(mesh):
    placed = (
        P(("dp", "ctx"), None),
        P("dp"),
        P(("dp", "ctx")),
        P(),
        P(),
        P(),
        P(),
        P(),
        P(),
        P(("dp", "ctx"), None, None),
        P(("dp", "ctx"), None),
        P(("dp", "ctx")),
    )
    return jax.shard_map(
        body, mesh=mesh, in_specs=placed, out_specs=(P(("dp", "ctx"), None), P()), check_vma=False
    )
```

profile of v0, /device:TPU:1, one launch (start us, length us, event | category | flops | bytes accessed | tf_op | source)
XLA Modules:
  0.0 2065.6 jit_solution(10883637024428701219)
XLA Ops:
  7.2 1.0 fusion.38
  8.2 1.4 fusion.39
  9.7 1.7 convolution_convert_fusion.3
  11.4 15.2 all_gather.19
  26.6 2.1 copy.39
  28.6 1.0 convolution_convert_fusion.4
  29.6 1.1 copy.38
  31.7 8.9 all_gather.18
  40.8 2.2 fusion.43
  43.0 1.8 fusion.26
  47.2 774.7 %all-gather.5.cloned.1.call-done = bf16[512,32,128]{2,1,0:T(8,128)(2,1)} async-done(((bf16[1,32,128]{2,1,0:T(8,128)(2,1)}), bf16[512,32,128]{2,1,0:T(8,128)(2,1)}) %all-gather.5.cloned.1.call-update) | async-done | bytes 4194320 | tf_op jit(solution)/shard_map/all_gather | solution.py:122
  821.9 17.5 while.21
  821.9 1.6 fusion.81
  824.1 1.6 fusion.81
  826.3 1.5 fusion.81
  828.5 1.6 fusion.81
  830.6 1.6 fusion.81
  832.8 1.5 fusion.81
  835.0 1.6 fusion.81
  837.2 1.6 fusion.81
  840.0 680.7 %all-gather.1 = bf16[512,1,32]{2,1,0:T(2,128)(2,1)S(1)} all-gather(bf16[1,1,32]{2,1,0:T(2,128)(2,1)S(1)} %bitcast.125), channel_id=1, replica_groups=mesh['dp'=128,'ctx'=4] {'dp','ctx'}, dimensions={0}, use_global_device_ids=true | all-gather | bytes 32832 | tf_op jit(solution)/shard_map/all_gather | solution.py:123
  1521.8 99.7 %all-reduce = s32[512]{0:T(512)S(1)} all-reduce(s32[512]{0:T(512)S(1)} %dynamic-update-slice), channel_id=1, replica_groups=mesh['dp'=128,'ctx'=4] {'dp','ctx'}, use_global_device_ids=true, to_apply=%add | all-reduce | flops 512 | bytes 4096
  1621.5 1.1 multiply_reduce_fusion.3
  1622.6 249.2 %all-gather.2 = f32[128,1,512]{2,1,0:T(1,128)S(1)} all-gather(f32[1,1,512]{2,1,0:T(1,128)S(1)} %bitcast.122), channel_id=2, replica_groups=mesh['dp'=128,'ctx'=4] {'dp'}, dimensions={0}, use_global_device_ids=true | all-gather | bytes 264192 | tf_op jit(solution)/shard_map/all_gather | solution.py:129
  1872.5 1.1 multiply_divide_fusion
  1873.6 0.8 copy.43
  1874.4 33.0 %while.22 = (s32[]{:T(128)}, f32[128,128]{1,0:T(8,128)}, bf16[8,64,32,128]{3,2,1,0:T(8,128)(2,1)}, bf16[128,128]{1,0:T(8,128)(2,1)}, f32[128]{0:T(128)}, /*index=5*/f32[8,64,32]{1,2,0:T(8,128)}, s32[]{:T(128)}, s32[]{:T(128)}) while((s32[]{:T(128)}, f32[128,128]{1,0:T(8,128)}, bf16[8,64,32,128]{3,2,1,0:T(8,128)(2,1)}, ...), condition=%wide.region_13.14_spmd.clone, body=%wide.region_12.13_spmd.clone.sunk | while | flops 135299072 | bytes 1761895 | solution.py:52
  1874.4 1.1 constant_dynamic-slice_fusion.3
  1875.5 0.7 dynamic-slice_bitcast_fusion.2
  1876.3 2.2 fusion.83
  1878.5 1.1 constant_dynamic-slice_fusion.3
  1879.6 0.7 dynamic-slice_bitcast_fusion.2
  1880.3 2.3 fusion.83
  1882.6 1.1 constant_dynamic-slice_fusion.3
  1883.7 0.7 dynamic-slice_bitcast_fusion.2
  1884.4 2.3 fusion.83
  1886.8 1.1 constant_dynamic-slice_fusion.3
  1887.8 0.7 dynamic-slice_bitcast_fusion.2
  1888.6 2.3 fusion.83
  1890.9 1.1 constant_dynamic-slice_fusion.3
  1892.7 2.3 fusion.83
  1895.0 1.1 constant_dynamic-slice_fusion.3
  1896.8 2.3 fusion.83
  1899.2 1.1 constant_dynamic-slice_fusion.3
  1900.2 0.7 dynamic-slice_bitcast_fusion.2
  1901.0 2.3 fusion.83
  1903.3 1.1 constant_dynamic-slice_fusion.3
  1905.1 2.3 fusion.83
  1907.4 0.9 copy.45
  1909.0 0.9 multiply_reduce_fusion.4
  1909.9 1.2 fusion.42
  1911.1 1.1 convolution_convert_fusion.2
  1912.5 2.4 multiply_convert_fusion
  1914.9 1.0 copy-done.5
  1915.8 1.1 convolution_convert_fusion.1
  1916.9 2.1 copy.47
  1919.1 1.1 convolution_convert_fusion
  1920.2 2.2 copy.49
  1922.4 1.9 convolution_convert_fusion.6
  1924.3 1.3 convolution_add_fusion.2
  1925.6 85.0 %reduce-scatter.7.cloned.1.call-done = bf16[128,512]{1,0:T(8,128)(2,1)} async-done(((bf16[512,512]{1,0:T(8,128)(2,1)}), bf16[128,512]{1,0:T(8,128)(2,1)}) %reduce-scatter.7.cloned.1.call-update) | async-done | bytes 131088
  2010.6 1.9 convolution_add_fusion.1
  2012.5 44.5 %reduce-scatter.9.cloned.1.call-done = bf16[128,512]{1,0:T(8,128)(2,1)} async-done(((bf16[512,512]{1,0:T(8,128)(2,1)}), bf16[128,512]{1,0:T(8,128)(2,1)}) %reduce-scatter.9.cloned.1.call-update) | async-done | bytes 131088
  2057.0 2.1 fusion.22
  (98 shorter events, 12.7 us)
Async XLA Ops:
  7.2 38.1 %copy-start = (bf16[512,1024]{1,0:T(8,128)(2,1)S(1)}, bf16[512,1024]{1,0:T(8,128)(2,1)}, u32[]{:S(2)}) copy-start(bf16[512,1024]{1,0:T(8,128)(2,1)} %param.22) | copy-start | bytes 3145732
  7.2 21.5 %copy-start.6 = (bf16[128,1024]{1,0:T(8,128)(2,1)S(1)}, bf16[128,1024]{1,0:T(8,128)(2,1)}, u32[]{:S(2)}) copy-start(bf16[128,1024]{1,0:T(8,128)(2,1)} %param.16) | copy-start | bytes 786436
  7.2 21.5 %copy-start.1 = (bf16[1024,512]{1,0:T(8,128)(2,1)S(1)}, bf16[1024,512]{1,0:T(8,128)(2,1)}, u32[]{:S(2)}) copy-start(bf16[1024,512]{1,0:T(8,128)(2,1)} %param.19) | copy-start | bytes 3145732
  7.2 814.7 %all-gather.5.cloned.1.call-start = ((), (), s32[]{:S(2)}) async-start(), calls=%async_computation.2 | async-start | bytes 4202496 | tf_op jit(solution)/shard_map/all_gather | solution.py:122
  9.6 1611.9 %all-reduce.3.cloned.1.call-start = ((), (), s32[]{:S(2)}) async-start(), calls=%async_computation.3 | async-start | bytes 524288 | tf_op jit(solution)/shard_map/psum | solution.py:127
  9.7 21.7 %copy-start.3 = (bf16[1024,512]{1,0:T(8,128)(2,1)S(1)}, bf16[1024,512]{1,0:T(8,128)(2,1)}, u32[]{:S(2)}) copy-start(bf16[1024,512]{1,0:T(8,128)(2,1)} %param.21) | copy-start | bytes 3145732
  29.6 11.2 copy-start.7
  30.7 12.3 copy-start.13
  40.8 4.0 copy-start.8
  43.0 2.3 copy-start.22
  44.8 1.2 copy-start.9
  44.8 1.2 copy-start.16
  45.3 1.9 copy-start.25
  45.7 0.6 copy-start.17
  46.0 0.6 copy-start.19
  46.3 775.6 %copy-start.11 = (f32[128,128]{0,1:T(8,128)}, f32[128,128]{0,1:T(8,128)S(1)}, u32[]{:S(2)}) copy-start(f32[128,128]{0,1:T(8,128)S(1)} %get-tuple-element.150) | copy-start | bytes 196612
  46.6 0.5 copy-start.21
  821.9 18.1 copy-start.24
  839.4 0.6 copy-start.15
  839.4 0.6 copy-start.26
  839.4 1171.2 %reduce-scatter.7.cloned.1.call-start = ((), (), s32[]{:S(2)}) async-start(), calls=%async_computation.4 | async-start | bytes 655360
  1874.4 35.5 %copy-start.10 = (bf16[1024,128]{1,0:T(8,128)(2,1)S(1)}, bf16[1024,128]{1,0:T(8,128)(2,1)}, u32[]{:S(2)}) copy-start(bf16[1024,128]{1,0:T(8,128)(2,1)} %param.24) | copy-start | bytes 786436
  1908.4 0.6 copy-start.12
  1909.9 2.6 copy-start.23
  1912.5 3.4 copy-start.14
  1914.8 1.0 copy-start.5
  1919.0 5.2 copy-start.18
  1919.0 5.2 copy-start.20
  1919.1 137.9 %reduce-scatter.9.cloned.1.call-start = ((), (), s32[]{:S(2)}) async-start(), calls=%async_computation.5 | async-start | bytes 655360
  1920.2 4.1 copy-start.2
  1925.6 131.4 %copy-start.4 = (bf16[1024,512]{1,0:T(8,128)(2,1)S(1)}, bf16[1024,512]{1,0:T(8,128)(2,1)}, u32[]{:S(2)}) copy-start(bf16[1024,512]{1,0:T(8,128)(2,1)} %param.21) | copy-start | bytes 3145732
Sparse Core Ops, SparseCore 0:
  10.3 811.5 all-gather.4
  839.5 57.0 all-reduce.2
  1919.2 91.3 reduce-scatter.6
  2013.5 43.4 reduce-scatter.8
where the time goes:
time: 2070 us
  blocking collectives  1050 us (51%)
  waiting for transfers between devices  904 us (44%)
  matrix products  51.3 us (2%)
  local copies, waits for them, and re-layouts  32 us (2%)
    all_gather x1, waiting for transfers between devices, body(): lax.all_gather(qn, ('dp', 'ctx'), axis=0, tiled=True)  775 us
    all_gather x1, blocking collectives, body(): lax.all_gather(query_mask, ('dp', 'ctx'), axis=0, tiled=True)  681 us
    all_gather x1, blocking collectives, body(): table = lax.all_gather(column[None, :], 'dp', axis=0, tiled=True)  249 us
    unnamed x6, waiting for transfers between devices  130 us
    unnamed x1, blocking collectives  99.7 us
  transfers between devices with their start and end apart: 4, of which 3 were waited for; matrix products, arithmetic and copies ran while one was open for 1% of the time, Pallas kernels for 0%

commit v1 on v0

v1 whole, which is shorter than its diff:
```python
import jax
import jax.numpy as jnp
import numpy as np
from jax import lax
from jax.sharding import Mesh, PartitionSpec as P

HD = 64
TAU = 0.05
GRAD_SCALE = 1024.0
NEG = -1e30
AXES = ("z", "ylo", "x", "yhi", "core")
SIZES = (16, 2, 4, 2, 2)
DP = ("z", "ylo", "x")
SWAP = [(0, 1), (1, 0)]
bf16 = jnp.bfloat16
f32 = jnp.float32


def dot32(left, right):
    return jnp.dot(left, right, preferred_element_type=f32)


def split_heads(t):
    return t.reshape(t.shape[0], -1, HD)


def spread(x, axes, count):
    return lax.all_to_all(jnp.broadcast_to(x[None], (count,) + x.shape), axes, 0, 0)


def body(
    hidden,
    doc_len,
    doc_keep,
    w_query,
    w_key,
    w_value,
    w_out,
    ln_gain,
    w_proj,
    queries,
    query_mask,
    positive,
):
    rows = hidden.shape[0]
    length = doc_len[0]
    me = lax.axis_index("yhi") * 2 + lax.axis_index("core")
    mine = lax.axis_index(DP)

    keep_rows = jnp.zeros((16, hidden.shape[1]), bf16).at[0, :rows].set(doc_keep.astype(bf16))
    own = jnp.concatenate([hidden, keep_rows], 0)
    by_core = lax.ppermute(own, "core", SWAP)
    by_yhi = lax.ppermute(own, "yhi", SWAP)
    by_both = lax.ppermute(by_yhi, "core", SWAP)
    blocks = (own, by_core, by_yhi, by_both)
    x = jnp.concatenate([b[:rows] for b in blocks], 0)
    skip = jnp.stack([b[rows, :rows] for b in blocks])
    place = (me ^ jnp.arange(4, dtype=jnp.int32))[:, None] * rows + jnp.arange(
        rows, dtype=jnp.int32
    )
    valid = (place < length).reshape(-1)
    keep = ((place < length) & ((skip == 1) | (place == 0))).astype(f32).reshape(-1)

    qfull = queries[0].astype(f32)
    qn = (qfull * lax.rsqrt(jnp.sum(qfull * qfull, -1, keepdims=True) + 1e-06)).astype(bf16)
    qlen, width = qn.shape
    extra = jnp.concatenate(
        [
            jnp.tile(query_mask, (1, width // qlen)),
            jnp.broadcast_to(positive[:, None].astype(bf16), (1, width)),
            jnp.zeros((14, width), bf16),
        ],
        0,
    )
    line = spread(jnp.concatenate([qn, extra], 0), "z", 16)
    line = jnp.concatenate(
        [line[:, :qlen].reshape(-1, width), line[:, qlen], line[:, qlen + 1]], 0
    )
    plane = spread(line, ("ylo", "x"), 8)
    qset = plane[:, : 16 * qlen].reshape(-1, width)
    qmask = plane[:, 16 * qlen : 16 * qlen + 16, :qlen].reshape(-1, qlen).astype(f32)
    pos = plane[:, 16 * qlen + 16 :, 0].reshape(-1).astype(jnp.int32)
    count = pos.shape[0]

    query = dot32(x, w_query).astype(bf16)
    keyed = dot32(x, w_key).astype(bf16)
    value = dot32(x, w_value).astype(bf16)
    scores = jnp.einsum(
        "rhc,jhc->hrj", split_heads(query), split_heads(keyed), preferred_element_type=f32
    ) * HD ** (-0.5)
    scores = jnp.where(valid[None, None, :], scores, NEG)
    top = jnp.max(scores, -1, keepdims=True)
    expo = jnp.exp(scores - top)
    denom = jnp.sum(expo, -1, keepdims=True)
    probs = expo / denom
    probs_b = probs.astype(bf16)
    attended = jnp.einsum("hrj,jhc->rhc", probs_b, split_heads(value), preferred_element_type=f32)
    attended = attended.reshape(x.shape[0], -1).astype(bf16)
    mixed = x.astype(f32) + dot32(attended, w_out)
    centred = mixed - jnp.mean(mixed, -1, keepdims=True)
    inv = lax.rsqrt(jnp.mean(centred * centred, -1, keepdims=True) + 1e-05)
    unit = centred * inv
    normed = (unit * ln_gain).astype(bf16)
    proj = dot32(normed, w_proj)
    scale = lax.rsqrt(jnp.sum(proj * proj, -1, keepdims=True) + 1e-06)
    embed_f = proj * scale
    embed = embed_f.astype(bf16)

    close = lax.dot_general(embed, qset, (((1,), (1,)), ((), ())), preferred_element_type=f32)
    near = jnp.exp(close / TAU) * keep[:, None]
    sums = jnp.sum(near, 0).reshape(count, qlen)
    column = jnp.sum(qmask * TAU * jnp.log(sums), -1)
    table = spread(column, DP, 128)
    lse = jnp.log(jnp.sum(jnp.exp(table), 0))
    hit = jnp.arange(128, dtype=jnp.int32)[:, None] == pos[None, :]
    loss_part = jnp.sum(lse - jnp.sum(jnp.where(hit, table, 0.0), 0))
    dscore = GRAD_SCALE * (jnp.exp(column - lse) - (pos == mine).astype(f32))
    coef = (dscore[:, None] * qmask / sums).reshape(-1)
    coupling = (near * coef[None, :]).astype(bf16)
    partial = dot32(coupling, qset)

    sent = jnp.concatenate([partial, jnp.broadcast_to(loss_part, (8, width))], 0)

    def blocks_of(t, order):
        return jnp.concatenate([t[o * rows : (o + 1) * rows] for o in order] + [t[4 * rows :]], 0)

    sent = sent + blocks_of(lax.ppermute(sent, "core", SWAP), (1, 0, 3, 2))
    sent = sent + blocks_of(lax.ppermute(sent, "yhi", SWAP), (2, 3, 0, 1))
    embed_grad = sent[: 4 * rows]
    loss = sent[4 * rows, 0]

    proj_grad = (
        (embed_grad - embed_f * jnp.sum(embed_f * embed_grad, -1, keepdims=True)) * scale
    ).astype(bf16)
    normed_grad = dot32(proj_grad, w_proj.T)
    gained = normed_grad * ln_gain
    mixed_grad = inv * (
        gained
        - jnp.mean(gained, -1, keepdims=True)
        - unit * jnp.mean(gained * unit, -1, keepdims=True)
    )
    mixed_b = mixed_grad.astype(bf16)
    attended_grad = dot32(mixed_b, w_out.T).astype(bf16)
    delta = jnp.transpose(
        jnp.sum(
            split_heads(attended_grad).astype(f32) * split_heads(attended).astype(f32),
            -1,
        )
    )[..., None]

    def score_grads(left, right, prob, off):
        inner = jnp.einsum(
            "rhc,jhc->hrj", split_heads(left), split_heads(right), preferred_element_type=f32
        )
        return (prob * (inner - off) * HD ** (-0.5)).astype(bf16)

    by_row = score_grads(attended_grad[:rows], value, probs[:, :rows], delta[:, :rows])
    by_col = score_grads(attended_grad, value[:rows], probs[:, :, :rows], delta)
    q_grad = jnp.einsum("hrj,jhc->rhc", by_row, split_heads(keyed), preferred_element_type=f32)
    k_grad = jnp.einsum("hrj,rhc->jhc", by_col, split_heads(query), preferred_element_type=f32)
    v_grad = jnp.einsum(
        "hrj,rhc->jhc",
        probs_b[:, :, :rows],
        split_heads(attended_grad),
        preferred_element_type=f32,
    )
    q_grad, k_grad, v_grad = (t.reshape(rows, -1).astype(bf16) for t in (q_grad, k_grad, v_grad))
    total = (
        mixed_grad[:rows]
        + dot32(q_grad, w_query.T)
        + dot32(k_grad, w_key.T)
        + dot32(v_grad, w_value.T)
    )
    return (total.astype(bf16), loss)


def solution(mesh):
    fine = Mesh(np.asarray(mesh.devices).reshape(SIZES), AXES)
    placed = (
        P(AXES, None),
        P(DP),
        P(AXES),
        P(),
        P(),
        P(),
        P(),
        P(),
        P(),
        P(AXES, None, None),
        P(AXES, None),
        P(AXES),
    )
    return jax.shard_map(
        body, mesh=fine, in_specs=placed, out_specs=(P(AXES, None), P()), check_vma=False
    )
```

time: 2070 us -> 168 us (0.08)
  blocking collectives: 1050 us -> 0 us
  waiting for transfers between devices: 904 us -> 34.2 us
  starting transfers between devices: 0.16 us -> 52.7 us
    all_gather x4 -> x0, blocking collectives: 954 us -> none  [the longest x1 681 us: body(): lax.all_gather(query_mask, ('dp', 'ctx'), axis=0, tiled=True)]
    all_gather x1 -> x0, waiting for transfers between devices: 775 us -> none  [body(): lax.all_gather(qn, ('dp', 'ctx'), axis=0, tiled=True)]
    unnamed x6 -> x0, waiting for transfers between devices: 130 us -> none
    unnamed x1 -> x0, blocking collectives: 99.7 us -> none
    all_to_all x0 -> x3, starting transfers between devices: none -> 32 us  [spread(): lax.all_to_all(jnp.broadcast_to(x[None], (count,) + x.shape), axes, 0, 0)]
    all_to_all x0 -> x3, waiting for transfers between devices: none -> 24.2 us  [spread(): lax.all_to_all(jnp.broadcast_to(x[None], (count,) + x.shape), axes, 0, 0)]
    dot_general x30 -> x15, matrix products: 48.7 us -> 31.6 us  [the longest x11 19.3 us: dot32(): return jnp.dot(left, right, preferred_element_type=f32)]
  transfers between devices with their start and end apart: 4 -> 8, of which waited for: 3 -> 5; matrix products, arithmetic and copies ran while one was open for 1% -> 20% of each run, Pallas kernels for 0% -> 0%
where the time goes in v1:
time: 168 us; the launch traced here: 167 us
  starting transfers between devices  52.7 us (31%)
  matrix products  40.1 us (24%)
  waiting for transfers between devices  34.2 us (20%)
  other arithmetic  21.2 us (13%)
  local copies, waits for them, and re-layouts  15.7 us (9%)
  between operations  2.67 us (2%)
    all_to_all x3, starting transfers between devices, spread(): lax.all_to_all(jnp.broadcast_to(x[None], (count,) + x.shape), axes, 0, 0)  32 us
    all_to_all x3, waiting for transfers between devices, spread(): lax.all_to_all(jnp.broadcast_to(x[None], (count,) + x.shape), axes, 0, 0)  24.2 us
    dot_general x11, matrix products, dot32(): return jnp.dot(left, right, preferred_element_type=f32)  19.3 us
    convert_element_type x1, other arithmetic, body(): probs_b = probs.astype(bf16)  8.29 us
    ppermute x1, waiting for transfers between devices, body(): sent = sent + blocks_of(lax.ppermute(sent, 'yhi', SWAP), (2, 3, 0, 1))  7.73 us
    sub x1, matrix products, body(): expo = jnp.exp(scores - top)  7.73 us
    ppermute x1, starting transfers between devices, body(): by_yhi = lax.ppermute(own, 'yhi', SWAP)  5.65 us
    dot_general x1, matrix products, body(): lax.dot_general(embed, qset, (((1,), (1,)), ((), ())), preferred_element_...  5.11 us
  transfers between devices with their start and end apart: 8, of which 5 were waited for; matrix products, arithmetic and copies ran while one was open for 20% of the time, Pallas kernels for 0%

profile of v1, /device:TPU:1, one launch (start us, length us, event | category | flops | bytes accessed | tf_op | source)
XLA Modules:
  0.0 166.6 jit_solution(15599036808258910114)
XLA Ops:
  0.7 0.8 convert_bitcast_fusion
  1.4 1.0 fusion.29
  2.4 5.7 %collective-permute-start.1 = (bf16[144,1024]{1,0:T(8,128)(2,1)S(1)}, bf16[144,1024]{1,0:T(8,128)(2,1)S(1)}, u32[]{:S(2)}, u32[]{:S(2)}) collective-permute-start(bf16[144,1024]{1,0:T(8,128)(2,1)S(1)} %fusion.29), channel_id=1, source_target_pairs={{0,2},{2,0},{1,3},{3,1},{4,6},{6,4},{5,7},{7,5},{8,10},{10,8},{9,1... | collective-permute-start | bytes 884744 | tf_op jit(solution)/shard_map/ppermute | solution.py:53
  8.1 5.1 %collective-permute-start = (bf16[144,1024]{1,0:T(8,128)(2,1)S(1)}, bf16[144,1024]{1,0:T(8,128)(2,1)S(1)}, u32[]{:S(2)}, u32[]{:S(2)}) collective-permute-start(bf16[144,1024]{1,0:T(8,128)(2,1)S(1)} %fusion.29), channel_id=1, source_target_pairs={{0,1},{1,0},{2,3},{3,2},{4,5},{5,4},{6,7},{7,6},{8,9},{9,8},{10,11... | collective-permute-start | bytes 884744 | tf_op jit(solution)/shard_map/ppermute | solution.py:52
  13.1 0.8 fusion.35
  13.9 0.8 fusion.36
  14.7 0.7 tile.12
  15.4 0.1 tile.13
  16.4 0.7 broadcast_in_dim.34
  17.1 12.8 %all-to-all-start = ((bf16[16,48,128]{2,1,0:T(8,128)(2,1)}), bf16[16,48,128]{2,1,0:T(8,128)(2,1)}, u32[]{:S(2)}, u32[]{:S(2)}) async-start(bf16[16,48,128]{2,1,0:T(8,128)(2,1)} %broadcast_in_dim.34), calls=%async_computation | async-start | bytes 393216 | tf_op jit(solution)/shard_map/all_to_all | solution.py:28
  30.5 2.2 %collective-permute-start.2 = (bf16[144,1024]{1,0:T(8,128)(2,1)S(1)}, bf16[144,1024]{1,0:T(8,128)(2,1)S(1)}, u32[]{:S(2)}, u32[]{:S(2)}) collective-permute-start(bf16[144,1024]{1,0:T(8,128)(2,1)S(1)} %collective-permute-done.1), channel_id=1, source_target_pairs={{0,1},{1,0},{2,3},{3,2},{4,5},{5,4},{6,7},{7,6},{8,9},{9,8},{10,11... | collective-permute-start | bytes 884744 | tf_op jit(solution)/shard_map/ppermute | solution.py:54
  32.9 1.1 collective-permute-done.2
  34.0 0.7 copy-done.27
  34.7 2.9 %convolution_convert_fusion.2 = bf16[512,512]{0,1:T(8,128)(2,1)} fusion(bf16[1024,512]{1,0:T(8,128)(2,1)} %param.18, bf16[128,1024]{1,0:T(8,128)(2,1)S(1)} %slice.142, bf16[128,1024]{1,0:T(8,128)(2,1)S(1)} %slice.141, bf16[128,1024]{1,0:T(8,128)(2,1)S(1)} %slice.140, bf16[128,1024]{1,0:T(8,128)(2,1)S(1)} %copy-done.7), kind=kOutput, calls=%fused_computation.29 | convolution fusion | flops 541327360 | bytes 2621440 | tf_op jit(solution)/shard_map/dot_general | solution.py:20
  37.6 0.8 convolution_convert_fusion.3
  38.4 0.4 copy-done.24
  38.9 0.8 convolution_convert_fusion.4
  39.7 7.7 %fusion.55 = (f32[8,512]{1,0:T(8,128)S(1)}, f32[8,512,512]{1,2,0:T(8,128)}) fusion(pred[512]{0:T(512)(128)(4,1)S(1)} %fusion.39, bf16[512,8,64]{0,2,1:T(8,128)(2,1)S(1)} %bitcast.91, bf16[512,8,64]{0,2,1:T(8,128)(2,1)} %bitcast.93), kind=kOutput, calls=%fused_computation.116 | convolution fusion | flops 276824576 | bytes 9454080 | tf_op jit(solution)/shard_map/sub | solution.py:93
  47.4 8.3 %fusion.52 = (bf16[8,512,512]{1,2,0:T(8,128)(2,1)S(1)}, f32[8,512,512]{1,2,0:T(8,128)}) fusion(f32[8,512,512]{1,2,0:T(8,128)} %get-tuple-element.27, f32[8,512]{1,0:T(8,128)S(1)} %get-tuple-element.26), kind=kLoop, calls=%fused_computation.113 | loop fusion | flops 4194304 | bytes 20987904 | tf_op jit(solution)/shard_map/convert_element_type | solution.py:96
  55.7 0.8 convolution_convert_fusion
  56.6 1.1 copy-done.1
  57.7 0.7 slice.149
  58.4 0.8 fusion.51
  59.2 0.4 multiply_reduce_fusion.1
  59.7 0.9 fusion.54
  60.6 0.9 slice.143
  61.5 1.2 broadcast_in_dim.35
  62.7 4.4 %all-to-all-start.1 = ((bf16[8,544,128]{2,1,0:T(8,128)(2,1)}), bf16[8,544,128]{2,1,0:T(8,128)(2,1)}, u32[]{:S(2)}, u32[]{:S(2)}) async-start(bf16[8,544,128]{2,1,0:T(8,128)(2,1)} %broadcast_in_dim.35), calls=%async_computation.1 | async-start | bytes 2228224 | tf_op jit(solution)/shard_map/all_to_all | solution.py:28
  67.3 2.6 %multiply_reduce_fusion.5 = (f32[512]{0:T(512)S(1)}, f32[512,128]{0,1:T(8,128)}) fusion(bf16[1024,128]{1,0:T(8,128)(2,1)} %param.22, f32[1024]{0:T(1024)S(1)} %copy-done.36, f32[512]{0:T(512)S(1)} %add_rsqrt_fusion.1, f32[512]{0:T(512)S(1)} %broadcast_multiply_fusion.2, f32[512,1024]{1,0:T(8,128)S(1)} %get-tuple-element.29, ...), kind=kOutput, calls=%fused_computation.58 | convolution fusion | flops 141164032 | bytes 3680256 | tf_op jit(solution)/shard_map/dot_general | solution.py:20
  69.9 13.7 %all-to-all-done.1 = bf16[8,544,128]{2,1,0:T(8,128)(2,1)} async-done(((bf16[8,544,128]{2,1,0:T(8,128)(2,1)}), bf16[8,544,128]{2,1,0:T(8,128)(2,1)}, u32[]{:S(2)}, u32[]{:S(2)}) %all-to-all-start.1) | async-done | bytes 1114144 | tf_op jit(solution)/shard_map/all_to_all | solution.py:28
  83.6 1.3 slice.146
  85.0 5.1 %fusion.1 = (f32[4096]{0:T(1024)S(1)}, f32[512,4096]{1,0:T(8,128)}) fusion(f32[512]{0:T(512)S(1)} %fusion.43, bf16[4096,128]{1,0:T(8,128)(2,1)S(1)} %bitcast.83, f32[512,128]{0,1:T(8,128)S(1)} %copy-done.20, f32[512]{0:T(512)S(1)} %add_rsqrt_fusion), kind=kOutput, calls=%fused_computation.5 | convolution fusion | flops 543289344 | bytes 9719808 | tf_op jit(solution)/shard_map/dot_general | solution.py:109
  90.2 0.9 multiply_reduce_fusion.6
  91.1 0.7 broadcast_in_dim.36
  91.8 14.8 %all-to-all-start.2 = ((f32[128,1,128]{2,1,0:T(1,128)}), f32[128,1,128]{2,1,0:T(1,128)S(1)}, u32[]{:S(2)}, u32[]{:S(2)}) async-start(f32[128,1,128]{2,1,0:T(1,128)} %broadcast_in_dim.36), calls=%async_computation.2 | async-start | bytes 131072 | tf_op jit(solution)/shard_map/all_to_all | solution.py:28
  106.6 1.0 convert_reduce_fusion
  107.5 0.6 reshape.238
  108.1 0.8 slice_convert_fusion
  108.9 0.7 reshape.239
  109.6 10.4 %all-to-all-done.2 = f32[128,1,128]{2,1,0:T(1,128)S(1)} async-done(((f32[128,1,128]{2,1,0:T(1,128)}), f32[128,1,128]{2,1,0:T(1,128)S(1)}, u32[]{:S(2)}, u32[]{:S(2)}) %all-to-all-start.2) | async-done | bytes 65568 | tf_op jit(solution)/shard_map/all_to_all | solution.py:28
  120.0 0.7 select_reduce_fusion
  120.7 1.3 subtract_reduce_fusion
  122.2 0.7 multiply_divide_fusion
  122.9 5.6 %fusion.6 = f32[512,128]{0,1:T(8,128)S(1)} fusion(bf16[4096,128]{1,0:T(8,128)(2,1)} %bitcast.84, f32[512,4096]{1,0:T(8,128)} %get-tuple-element.33, f32[4096]{0:T(1024)S(1)} %multiply_divide_fusion, f32[512]{0:T(512)} %copy-done.30), kind=kOutput, calls=%fused_computation.11 | convolution fusion | flops 545259520 | bytes 9717760 | tf_op jit(solution)/shard_map/dot_general | solution.py:20
  128.5 0.7 concatenate.28
  129.3 4.1 %collective-permute-start.3 = (f32[520,128]{0,1:T(8,128)S(1)}, f32[520,128]{0,1:T(8,128)S(1)}, u32[]{:S(2)}, u32[]{:S(2)}) collective-permute-start(f32[520,128]{0,1:T(8,128)S(1)} %concatenate.28), channel_id=1, source_target_pairs={{0,1},{1,0},{2,3},{3,2},{4,5},{5,4},{6,7},{7,6},{8,9},{9,8},{10,11... | collective-permute-start | bytes 798728 | tf_op jit(solution)/shard_map/ppermute | solution.py:127
  133.5 1.2 collective-permute-done.3
  134.7 0.7 pad_add_fusion
  135.4 3.7 %collective-permute-start.4 = (f32[520,128]{0,1:T(8,128)S(1)}, f32[520,128]{0,1:T(8,128)S(1)}, u32[]{:S(2)}, u32[]{:S(2)}) collective-permute-start(f32[520,128]{0,1:T(8,128)S(1)} %pad_add_fusion), channel_id=1, source_target_pairs={{0,2},{2,0},{1,3},{3,1},{4,6},{6,4},{5,7},{7,5},{8,10},{10,8},{9,1... | collective-permute-start | bytes 798728 | tf_op jit(solution)/shard_map/ppermute | solution.py:128
  139.1 0.9 slice.166
  140.0 7.7 %collective-permute-done.4 = f32[520,128]{0,1:T(8,128)S(1)} collective-permute-done((f32[520,128]{0,1:T(8,128)S(1)}, f32[520,128]{0,1:T(8,128)S(1)}, u32[]{:S(2)}, u32[]{:S(2)}) %collective-permute-start.4) | collective-permute-done | bytes 266272 | tf_op jit(solution)/shard_map/ppermute | solution.py:128
  147.9 0.5 slice.168
  148.5 0.9 multiply_reduce_fusion.2
  149.4 2.8 %subtract_multiply_fusion = f32[512,1024]{1,0:T(8,128)S(1)} fusion(f32[512,1024]{1,0:T(8,128)S(1)} %get-tuple-element.34, f32[512]{0:T(512)S(1)} %broadcast_multiply_fusion, f32[512]{0:T(512)S(1)} %broadcast_multiply_fusion.1, f32[1024]{0:T(1024)S(1)} %copy-done.37, f32[512]{0:T(512)S(1)} %copy-done.34, f32[512]{0:T(512)S(1)} %copy-done.32, ...), kind=kLoop, calls=%fused_computation.18 | loop fusion | flops 8388608 | bytes 7352320 | tf_op jit(solution)/shard_map/mul | solution.py:137
  152.2 0.8 multiply_reduce_fusion.3
  153.0 0.8 copy-done.5
  153.8 0.6 slice_bitcast_fusion
  154.4 2.6 %fusion.15 = bf16[8,64,128]{2,1,0:T(8,128)(2,1)S(1)} fusion(bf16[512,8,64]{0,2,1:T(8,128)(2,1)} %bitcast.94, f32[8,512,512]{1,2,0:T(8,128)} %get-tuple-element.19, bf16[128,8,64]{0,2,1:T(8,128)(2,1)S(1)} %bitcast.98, bf16[512,8,64]{0,2,1:T(8,128)(2,1)} %bitcast.86, f32[8,128]{1,0:T(8,128)} %slice_bitcast_fusion), kind=kOutput, calls=%fused_computation.37 | convolution fusion | flops 136380416 | bytes 3411968 | tf_op jit(solution)/shard_map/hrj,jhc->rhc/dot_general | solution.py:159
  157.1 2.6 %convolution_add_fusion.2 = f32[128,1024]{1,0:T(8,128)} fusion(bf16[128,512]{0,1:T(8,128)(2,1)S(1)} %bitcast.96, bf16[1024,512]{1,0:T(8,128)(2,1)} %param.17, f32[512,1024]{1,0:T(8,128)S(1)} %subtract_multiply_fusion), kind=kOutput, calls=%fused_computation.34 | convolution fusion | flops 134348800 | bytes 2228224 | tf_op jit(solution)/shard_map/dot_general | solution.py:20
  159.6 1.7 %convolution_convert_fusion.5 = bf16[8,64,128]{2,1,0:T(8,128)(2,1)S(1)} fusion(bf16[512,8,64]{0,2,1:T(8,128)(2,1)S(1)} %bitcast.88, bf16[8,512,512]{1,2,0:T(8,128)(2,1)} %copy-done.1), kind=kOutput, calls=%fused_computation.38 | convolution fusion | flops 67174400 | bytes 1703936 | tf_op jit(solution)/shard_map/hrj,rhc->jhc/dot_general | solution.py:161
  161.3 2.8 %fusion.14 = bf16[8,64,128]{2,1,0:T(8,128)(2,1)S(1)} fusion(bf16[512,8,64]{0,2,1:T(8,128)(2,1)} %bitcast.92, f32[8,512,512]{1,2,0:T(8,128)} %get-tuple-element.19, bf16[512,8,64]{0,2,1:T(8,128)(2,1)} %bitcast.87, bf16[128,8,64]{0,2,1:T(8,128)(2,1)S(1)} %bitcast.97, f32[8,512]{1,0:T(8,128)S(1)} %bitcast.102), kind=kOutput, calls=%fused_computation.36 | convolution fusion | flops 136380416 | bytes 3424256 | tf_op jit(solution)/shard_map/hrj,rhc->jhc/dot_general | solution.py:160
  164.2 0.5 convolution_add_fusion.1
  164.7 0.7 copy-done.25
  165.4 1.2 fusion.13
  (111 shorter events, 1.2 us)
Async XLA Ops:
  0.6 57.7 %copy-start = (bf16[512,1024]{1,0:T(8,128)(2,1)S(1)}, bf16[512,1024]{1,0:T(8,128)(2,1)}, u32[]{:S(2)}) copy-start(bf16[512,1024]{1,0:T(8,128)(2,1)} %param.20) | copy-start | bytes 3145732
  0.6 34.1 %copy-start.7 = (bf16[128,1024]{1,0:T(8,128)(2,1)S(1)}, bf16[128,1024]{1,0:T(8,128)(2,1)}, u32[]{:S(2)}) copy-start(bf16[128,1024]{1,0:T(8,128)(2,1)} %param.14) | copy-start | bytes 786436
  2.4 28.1 %collective-permute-start.1 = (bf16[144,1024]{1,0:T(8,128)(2,1)S(1)}, bf16[144,1024]{1,0:T(8,128)(2,1)S(1)}, u32[]{:S(2)}, u32[]{:S(2)}) collective-permute-start(bf16[144,1024]{1,0:T(8,128)(2,1)S(1)} %fusion.29), channel_id=1, source_target_pairs={{0,2},{2,0},{1,3},{3,1},{4,6},{6,4},{5,7},{7,5},{8,10},{10,8},{9,1... | collective-permute-start | bytes 884744 | tf_op jit(solution)/shard_map/ppermute | solution.py:53
  8.1 24.8 %collective-permute-start = (bf16[144,1024]{1,0:T(8,128)(2,1)S(1)}, bf16[144,1024]{1,0:T(8,128)(2,1)S(1)}, u32[]{:S(2)}, u32[]{:S(2)}) collective-permute-start(bf16[144,1024]{1,0:T(8,128)(2,1)S(1)} %fusion.29), channel_id=1, source_target_pairs={{0,1},{1,0},{2,3},{3,2},{4,5},{5,4},{6,7},{7,6},{8,9},{9,8},{10,11... | collective-permute-start | bytes 884744 | tf_op jit(solution)/shard_map/ppermute | solution.py:52
  17.1 42.6 %all-to-all-start = ((bf16[16,48,128]{2,1,0:T(8,128)(2,1)}), bf16[16,48,128]{2,1,0:T(8,128)(2,1)}, u32[]{:S(2)}, u32[]{:S(2)}) async-start(bf16[16,48,128]{2,1,0:T(8,128)(2,1)} %broadcast_in_dim.34), calls=%async_computation | async-start | bytes 393216 | tf_op jit(solution)/shard_map/all_to_all | solution.py:28
  30.5 3.5 %collective-permute-start.2 = (bf16[144,1024]{1,0:T(8,128)(2,1)S(1)}, bf16[144,1024]{1,0:T(8,128)(2,1)S(1)}, u32[]{:S(2)}, u32[]{:S(2)}) collective-permute-start(bf16[144,1024]{1,0:T(8,128)(2,1)S(1)} %collective-permute-done.1), channel_id=1, source_target_pairs={{0,1},{1,0},{2,3},{3,2},{4,5},{5,4},{6,7},{7,6},{8,9},{9,8},{10,11... | collective-permute-start | bytes 884744 | tf_op jit(solution)/shard_map/ppermute | solution.py:54
  32.8 5.6 %copy-start.8 = (bf16[128,1024]{1,0:T(8,128)(2,1)}, bf16[128,1024]{1,0:T(8,128)(2,1)S(1)}, u32[]{:S(2)}) copy-start(bf16[128,1024]{1,0:T(8,128)(2,1)S(1)} %slice.141) | copy-start | bytes 786436
  32.9 5.5 %copy-start.11 = (bf16[128,1024]{1,0:T(8,128)(2,1)}, bf16[128,1024]{1,0:T(8,128)(2,1)S(1)}, u32[]{:S(2)}) copy-start(bf16[128,1024]{1,0:T(8,128)(2,1)S(1)} %slice.140) | copy-start | bytes 786436
  34.0 0.7 copy-start.27
  34.7 3.7 %copy-start.14 = (bf16[128,1024]{1,0:T(8,128)(2,1)}, bf16[128,1024]{1,0:T(8,128)(2,1)S(1)}, u32[]{:S(2)}) copy-start(bf16[128,1024]{1,0:T(8,128)(2,1)S(1)} %slice.142) | copy-start | bytes 786436
  34.7 2.9 %copy-start.22 = (bf16[1024,512]{1,0:T(8,128)(2,1)S(1)}, bf16[1024,512]{1,0:T(8,128)(2,1)}, u32[]{:S(2)}) copy-start(bf16[1024,512]{1,0:T(8,128)(2,1)} %param.17) | copy-start | bytes 3145732
  37.6 1.2 copy-start.24
  38.9 0.8 copy-start.26
  39.6 16.1 %copy-start.4 = (bf16[512,512]{0,1:T(8,128)(2,1)}, bf16[512,512]{0,1:T(8,128)(2,1)S(1)}, u32[]{:S(2)}) copy-start(bf16[512,512]{0,1:T(8,128)(2,1)S(1)} %convolution_convert_fusion.4) | copy-start | bytes 1572868
  55.7 1.9 %copy-start.1 = (bf16[8,512,512]{1,2,0:T(8,128)(2,1)}, bf16[8,512,512]{1,2,0:T(8,128)(2,1)S(1)}, u32[]{:S(2)}) copy-start(bf16[8,512,512]{1,2,0:T(8,128)(2,1)S(1)} %get-tuple-element.18) | copy-start | bytes 12582916
  55.7 2.6 %copy-start.9 = (bf16[128,1024]{1,0:T(8,128)(2,1)S(1)}, bf16[128,1024]{1,0:T(8,128)(2,1)}, u32[]{:S(2)}) copy-start(bf16[128,1024]{1,0:T(8,128)(2,1)} %copy-done.8) | copy-start | bytes 786436
  55.7 2.6 %copy-start.12 = (bf16[128,1024]{1,0:T(8,128)(2,1)S(1)}, bf16[128,1024]{1,0:T(8,128)(2,1)}, u32[]{:S(2)}) copy-start(bf16[128,1024]{1,0:T(8,128)(2,1)} %copy-done.11) | copy-start | bytes 786436
  55.7 2.6 %copy-start.15 = (bf16[128,1024]{1,0:T(8,128)(2,1)S(1)}, bf16[128,1024]{1,0:T(8,128)(2,1)}, u32[]{:S(2)}) copy-start(bf16[128,1024]{1,0:T(8,128)(2,1)} %copy-done.14) | copy-start | bytes 786436
  57.7 1.5 copy-start.18
  59.2 89.2 %copy-start.2 = (f32[512,1024]{1,0:T(8,128)}, f32[512,1024]{1,0:T(8,128)S(1)}, u32[]{:S(2)}) copy-start(f32[512,1024]{1,0:T(8,128)S(1)} %get-tuple-element.29) | copy-start | bytes 6291460
  59.2 8.1 %copy-start.31 = (f32[512]{0:T(512)}, f32[512]{0:T(512)S(1)}, u32[]{:S(2)}) copy-start(f32[512]{0:T(512)S(1)} %broadcast_multiply_fusion.2) | copy-start | bytes 6148
  59.6 7.6 %copy-start.36 = (f32[1024]{0:T(1024)S(1)}, f32[1024]{0:T(1024)}, u32[]{:S(2)}) copy-start(f32[1024]{0:T(1024)} %param.21) | copy-start | bytes 12292
  62.7 20.8 %all-to-all-start.1 = ((bf16[8,544,128]{2,1,0:T(8,128)(2,1)}), bf16[8,544,128]{2,1,0:T(8,128)(2,1)}, u32[]{:S(2)}, u32[]{:S(2)}) async-start(bf16[8,544,128]{2,1,0:T(8,128)(2,1)} %broadcast_in_dim.35), calls=%async_computation.1 | async-start | bytes 2228224 | tf_op jit(solution)/shard_map/all_to_all | solution.py:28
  67.3 17.7 %copy-start.30 = (f32[512]{0:T(512)}, f32[512]{0:T(512)S(1)}, u32[]{:S(2)}) copy-start(f32[512]{0:T(512)S(1)} %fusion.43) | copy-start | bytes 6148
  67.3 2.6 %copy-start.33 = (f32[512]{0:T(512)}, f32[512]{0:T(512)S(1)}, u32[]{:S(2)}) copy-start(f32[512]{0:T(512)S(1)} %add_rsqrt_fusion.1) | copy-start | bytes 6148
  69.9 20.2 %copy-start.28 = (f32[512]{0:T(512)}, f32[512]{0:T(512)S(1)}, u32[]{:S(2)}) copy-start(f32[512]{0:T(512)S(1)} %add_rsqrt_fusion) | copy-start | bytes 6148
  83.6 1.4 copy-start.20
  84.9 5.1 %copy-start.3 = (bf16[8,512,128]{2,1,0:T(8,128)(2,1)}, bf16[8,512,128]{2,1,0:T(8,128)(2,1)S(1)}, u32[]{:S(2)}) copy-start(bf16[8,512,128]{2,1,0:T(8,128)(2,1)S(1)} %slice.146) | copy-start | bytes 3145732
  91.1 0.7 copy-start.35
  91.8 28.2 %all-to-all-start.2 = ((f32[128,1,128]{2,1,0:T(1,128)}), f32[128,1,128]{2,1,0:T(1,128)S(1)}, u32[]{:S(2)}, u32[]{:S(2)}) async-start(f32[128,1,128]{2,1,0:T(1,128)} %broadcast_in_dim.36), calls=%async_computation.2 | async-start | bytes 131072 | tf_op jit(solution)/shard_map/all_to_all | solution.py:28
  128.5 19.3 %copy-start.21 = (f32[512,128]{0,1:T(8,128)S(1)}, f32[512,128]{0,1:T(8,128)}, u32[]{:S(2)}) copy-start(f32[512,128]{0,1:T(8,128)} %get-tuple-element.31) | copy-start | bytes 786436
  128.5 19.3 %copy-start.29 = (f32[512]{0:T(512)S(1)}, f32[512]{0:T(512)}, u32[]{:S(2)}) copy-start(f32[512]{0:T(512)} %copy-done.28) | copy-start | bytes 6148
  129.3 19.2 %copy-start.10 = (bf16[128,1024]{1,0:T(8,128)(2,1)S(1)}, bf16[128,1024]{1,0:T(8,128)(2,1)}, u32[]{:S(2)}) copy-start(bf16[128,1024]{1,0:T(8,128)(2,1)} %copy-done.8) | copy-start | bytes 786436
  129.3 19.2 %copy-start.13 = (bf16[128,1024]{1,0:T(8,128)(2,1)S(1)}, bf16[128,1024]{1,0:T(8,128)(2,1)}, u32[]{:S(2)}) copy-start(bf16[128,1024]{1,0:T(8,128)(2,1)} %copy-done.11) | copy-start | bytes 786436
  129.3 19.2 %copy-start.16 = (bf16[128,1024]{1,0:T(8,128)(2,1)S(1)}, bf16[128,1024]{1,0:T(8,128)(2,1)}, u32[]{:S(2)}) copy-start(bf16[128,1024]{1,0:T(8,128)(2,1)} %copy-done.14) | copy-start | bytes 786436
  129.3 19.1 %copy-start.32 = (f32[512]{0:T(512)S(1)}, f32[512]{0:T(512)}, u32[]{:S(2)}) copy-start(f32[512]{0:T(512)} %copy-done.31) | copy-start | bytes 6148
  129.3 19.1 %copy-start.34 = (f32[512]{0:T(512)S(1)}, f32[512]{0:T(512)}, u32[]{:S(2)}) copy-start(f32[512]{0:T(512)} %copy-done.33) | copy-start | bytes 6148
  129.3 19.1 %copy-start.37 = (f32[1024]{0:T(1024)S(1)}, f32[1024]{0:T(1024)}, u32[]{:S(2)}) copy-start(f32[1024]{0:T(1024)} %param.21) | copy-start | bytes 12292
  129.3 19.1 %copy-start.38 = (bf16[1024,128]{1,0:T(8,128)(2,1)S(1)}, bf16[1024,128]{1,0:T(8,128)(2,1)}, u32[]{:S(2)}) copy-start(bf16[1024,128]{1,0:T(8,128)(2,1)} %param.22) | copy-start | bytes 786436
  129.3 5.4 %collective-permute-start.3 = (f32[520,128]{0,1:T(8,128)S(1)}, f32[520,128]{0,1:T(8,128)S(1)}, u32[]{:S(2)}, u32[]{:S(2)}) collective-permute-start(f32[520,128]{0,1:T(8,128)S(1)} %concatenate.28), channel_id=1, source_target_pairs={{0,1},{1,0},{2,3},{3,2},{4,5},{5,4},{6,7},{7,6},{8,9},{9,8},{10,11... | collective-permute-start | bytes 798728 | tf_op jit(solution)/shard_map/ppermute | solution.py:127
  135.4 12.3 %collective-permute-start.4 = (f32[520,128]{0,1:T(8,128)S(1)}, f32[520,128]{0,1:T(8,128)S(1)}, u32[]{:S(2)}, u32[]{:S(2)}) collective-permute-start(f32[520,128]{0,1:T(8,128)S(1)} %pad_add_fusion), channel_id=1, source_target_pairs={{0,2},{2,0},{1,3},{3,1},{4,6},{6,4},{5,7},{7,5},{8,10},{10,8},{9,1... | collective-permute-start | bytes 798728 | tf_op jit(solution)/shard_map/ppermute | solution.py:128
  149.4 2.8 %copy-start.19 = (bf16[8,64,512]{2,1,0:T(8,128)(2,1)S(1)}, bf16[8,64,512]{2,1,0:T(8,128)(2,1)}, u32[]{:S(2)}) copy-start(bf16[8,64,512]{2,1,0:T(8,128)(2,1)} %copy-done.18) | copy-start | bytes 1572868
  153.0 0.8 copy-start.5
  157.0 2.6 %copy-start.6 = (bf16[512,512]{0,1:T(8,128)(2,1)S(1)}, bf16[512,512]{0,1:T(8,128)(2,1)}, u32[]{:S(2)}) copy-start(bf16[512,512]{0,1:T(8,128)(2,1)} %copy-done.5) | copy-start | bytes 1572868
  161.3 2.9 %copy-start.17 = (f32[128,1024]{1,0:T(8,128)S(1)}, f32[128,1024]{1,0:T(8,128)}, u32[]{:S(2)}) copy-start(f32[128,1024]{1,0:T(8,128)} %convolution_add_fusion.2) | copy-start | bytes 1572868
  161.3 2.9 %copy-start.23 = (bf16[1024,512]{1,0:T(8,128)(2,1)S(1)}, bf16[1024,512]{1,0:T(8,128)(2,1)}, u32[]{:S(2)}) copy-start(bf16[1024,512]{1,0:T(8,128)(2,1)} %param.18) | copy-start | bytes 3145732
  164.2 1.2 copy-start.25

commit v2 on v1

v2 whole, which is shorter than its diff:
```python
import jax
import jax.numpy as jnp
import numpy as np
from jax import lax
from jax.experimental import pallas as pl
from jax.experimental.pallas import tpu as pltpu
from jax.sharding import Mesh, PartitionSpec as P

D = 1024
HEADS = 8
HD = 64
E = 128
QLEN = 32
L = 512
ROWS = 128
DOCS = 128
QSET = 128
AUX = 16
TAU = 0.05
GRAD_SCALE = 1024.0
NEG = -1e30
AXES = ("z", "ylo", "x", "yhi", "core")
SIZES = (16, 2, 4, 2, 2)
DP = ("z", "ylo", "x")
LINE = 16
PLANE = 8
CHUNK = LINE * QLEN
SWAP = [(0, 1), (1, 0)]
bf16 = jnp.bfloat16
f32 = jnp.float32
i32 = jnp.int32
VMEM = pl.BlockSpec(memory_space=pltpu.VMEM)
SMEM = pl.BlockSpec(memory_space=pltpu.SMEM)
NN = (((1,), (0,)), ((), ()))
NT = (((1,), (1,)), ((), ()))
TN = (((0,), (0,)), ((), ()))


def dot(left, right, dims=NN):
    return lax.dot_general(left, right, dims, preferred_element_type=f32)


def iota(shape, dim):
    return lax.broadcasted_iota(i32, shape, dim)


def select(x, choice):
    choice = choice.astype(bf16)
    high = x.astype(bf16)
    rest = x - high.astype(f32)
    middle = rest.astype(bf16)
    low = (rest - middle.astype(f32)).astype(bf16)
    return dot(high, choice) + (dot(middle, choice) + dot(low, choice))


def call(kernel, outs, ins, scratch=(), flops=0, limit=40):
    return pl.pallas_call(
        kernel,
        out_shape=outs,
        in_specs=ins,
        out_specs=jax.tree.map(lambda _: VMEM, outs),
        scratch_shapes=list(scratch),
        compiler_params=pltpu.CompilerParams(vmem_limit_bytes=limit * 2**20),
        cost_estimate=pl.CostEstimate(flops=flops, bytes_accessed=8 * 2**20, transcendentals=0),
    )


def shape(dims, kind):
    return jax.ShapeDtypeStruct(dims, kind)


def pack_kernel(pos_ref, queries_ref, mask_ref, hidden_ref, skip_ref, query_out, own_out):
    q = queries_ref[...].astype(f32)
    qn = (q * lax.rsqrt(jnp.sum(q * q, -1, keepdims=True) + 1e-06)).astype(bf16)
    repeat = (iota((QLEN, E), 1) % QLEN == iota((QLEN, E), 0)).astype(bf16)
    weights = dot(jnp.broadcast_to(mask_ref[...], (AUX, QLEN)), repeat)
    target = pos_ref[0].astype(f32)
    row = iota((AUX, E), 0)
    aux = jnp.where(row == 0, weights, jnp.where(row == 1, target, 0.0)).astype(bf16)
    for z in range(LINE):
        query_out[z, :QLEN, :] = qn
        query_out[z, QLEN:, :] = aux
    own_out[:ROWS, :] = hidden_ref[...]
    own_out[ROWS:, :] = jnp.zeros((AUX, D), bf16)
    own_out[ROWS:, :ROWS] = jnp.broadcast_to(skip_ref[...], (AUX, ROWS)).astype(f32).astype(bf16)


def pack(positive, queries, query_mask, hidden, doc_keep):
    return call(
        pack_kernel,
        (shape((LINE, QLEN + AUX, E), bf16), shape((ROWS + AUX, D), bf16)),
        [SMEM, VMEM, VMEM, VMEM, VMEM],
    )(positive, queries[0], query_mask, hidden, doc_keep[None])


def repack_kernel(line_ref, out_ref):
    aux = line_ref[:, QLEN:, :].astype(f32)
    weights = aux[:, 0, :].astype(bf16)
    target = aux[:, 1, :].astype(bf16)
    for p in range(PLANE):
        for z in range(LINE):
            out_ref[p, z * QLEN : (z + 1) * QLEN, :] = line_ref[z, :QLEN, :]
        out_ref[p, CHUNK : CHUNK + LINE, :] = weights
        out_ref[p, CHUNK + LINE :, :] = target


def repack(line):
    return call(repack_kernel, shape((PLANE, CHUNK + 2 * LINE, E), bf16), [VMEM])(line)


def forward_kernel(
    scalar_ref,
    x0_ref,
    x1_ref,
    x2_ref,
    x3_ref,
    wq_ref,
    wk_ref,
    wv_ref,
    wo_ref,
    gain_ref,
    wp_ref,
    q_ref,
    k_ref,
    v_ref,
    att_ref,
    prow_ref,
    pcol_ref,
    unit_ref,
    inv_ref,
    proj_ref,
    embed_ref,
    keep_ref,
    x_ref,
):
    length = scalar_ref[0]
    me = scalar_ref[1]
    sources = (x0_ref, x1_ref, x2_ref, x3_ref)
    bias = []
    for b, source in enumerate(sources):
        rows = slice(b * ROWS, (b + 1) * ROWS)
        x_ref[rows, :] = source[:ROWS, :]
        start = jnp.bitwise_xor(me, b) * ROWS
        skip = source[ROWS:, :ROWS].astype(f32)[0:1, :]
        place = start + iota((1, ROWS), 1)
        valid = place < length
        bias.append(jnp.where(valid, 0.0, NEG))
        kept = jnp.where(valid & ((skip == 1.0) | (place == 0)), 1.0, 0.0)
        diagonal = iota((ROWS, ROWS), 0) == iota((ROWS, ROWS), 1)
        column = jnp.sum(jnp.where(diagonal, kept, 0.0), -1, keepdims=True)
        keep_ref[rows, :] = jnp.broadcast_to(column, (ROWS, E))
    bias = jnp.concatenate(bias, 1)
    x = x_ref[...]
    k_ref[...] = dot(x, wk_ref[...]).astype(bf16)
    q_ref[...] = dot(x, wq_ref[...]).astype(bf16)
    v_ref[...] = dot(x, wv_ref[...]).astype(bf16)
    first = iota((ROWS, 2 * HD), 1) < HD
    for pair in range(HEADS // 2):
        lanes = slice(pair * 2 * HD, (pair + 1) * 2 * HD)
        kp = k_ref[:, lanes]
        vp = v_ref[:, lanes]
        for b in range(4):
            rows = slice(b * ROWS, (b + 1) * ROWS)
            qp = q_ref[rows, lanes] * jnp.array(HD**-0.5, bf16)
            mixes = []
            for half in range(2):
                head = 2 * pair + half
                own = first if half == 0 else ~first
                scores = dot(jnp.where(own, qp, jnp.zeros_like(qp)), kp, NT) + bias
                expo = jnp.exp(scores - jnp.max(scores, -1, keepdims=True))
                probs = expo * (1.0 / jnp.sum(expo, -1, keepdims=True))
                if b == 0:
                    prow_ref[head] = probs
                pcol_ref[head, rows, :] = probs[:, :ROWS]
                mixes.append(dot(probs.astype(bf16), vp))
            att_ref[rows, lanes] = jnp.where(first, mixes[0], mixes[1]).astype(bf16)
    unit_ref[...] = dot(att_ref[...], wo_ref[...])
    for c in range(8):
        rows = slice(c * 64, (c + 1) * 64)
        mixed = x_ref[rows, :].astype(f32) + unit_ref[rows, :]
        centred = mixed - jnp.mean(mixed, -1, keepdims=True)
        inv = lax.rsqrt(jnp.mean(centred * centred, -1, keepdims=True) + 1e-05)
        unit = centred * inv
        unit_ref[rows, :] = unit
        inv_ref[rows, :] = jnp.broadcast_to(inv, (64, E))
        x_ref[rows, :] = (unit * gain_ref[...]).astype(bf16)
    proj = dot(x_ref[...], wp_ref[...])
    proj_ref[...] = proj
    scale = lax.rsqrt(jnp.sum(proj * proj, -1, keepdims=True) + 1e-06)
    embed_ref[...] = (proj * scale).astype(bf16)


def forward(scalars, blocks, w_query, w_key, w_value, w_out, ln_gain, w_proj):
    square = shape((L, HEADS * HD), bf16)
    return call(
        forward_kernel,
        (
            square,
            square,
            square,
            square,
            shape((HEADS, ROWS, L), f32),
            shape((HEADS, L, ROWS), f32),
            shape((L, D), f32),
            shape((L, E), f32),
            shape((L, E), f32),
            shape((L, E), bf16),
            shape((L, E), f32),
        ),
        [SMEM] + [VMEM] * 10,
        [pltpu.VMEM((L, D), bf16)],
        flops=4 * 10**9,
    )(scalars, *blocks, w_query, w_key, w_value, w_out, ln_gain[None], w_proj)


def sums_kernel(plane_ref, embed_ref, keep_ref, send_ref, sums_ref, weight_ref):
    for c in range(PLANE):
        total = jnp.zeros((8, CHUNK), f32)
        for b in range(4):
            rows = slice(b * ROWS, (b + 1) * ROWS)
            close = dot(embed_ref[rows, :], plane_ref[c, :CHUNK, :], NT)
            near = jnp.exp(close * (1.0 / TAU)) * keep_ref[rows, 0:1]
            total += jnp.sum(near.reshape(ROWS // 8, 8, CHUNK), 0)
        total = jnp.sum(total, 0, keepdims=True)
        for j in range(4):
            sums_ref[4 * c + j : 4 * c + j + 1, :] = total[:, j * E : (j + 1) * E]
    weights = jnp.concatenate([plane_ref[c, CHUNK : CHUNK + LINE, :] for c in range(PLANE)], 0)
    row, col = iota((QLEN, QSET), 0), iota((QLEN, QSET), 1)
    weight = jnp.zeros((QLEN, E), f32)
    for g in range(4):
        picked = dot((col == 4 * row + g).astype(bf16), weights)
        weight = jnp.where(col // QLEN == g, picked, weight)
    weight_ref[...] = weight
    parts = weight * TAU * jnp.log(sums_ref[...])
    source, place = iota((E, QSET), 0), iota((E, QSET), 1)
    table = select(parts, source // QLEN == place % 4)
    table = jnp.sum(jnp.where(col // 4 == row, table, 0.0), 0, keepdims=True)
    send_ref[...] = jnp.broadcast_to(table, (DOCS, QSET))


def sums_call(plane, embed, keep):
    return call(
        sums_kernel,
        (shape((DOCS, QSET), f32), shape((QLEN, E), f32), shape((QLEN, E), f32)),
        [VMEM] * 3,
        flops=10**9,
    )(plane, embed, keep)


def grads_kernel(mine_ref, table_ref, plane_ref, embed_ref, keep_ref, sums_ref, weight_ref, out_ref):
    mine = mine_ref[0]
    table = table_ref[...]
    lse = jnp.log(jnp.sum(jnp.exp(table), 0, keepdims=True))
    targets = jnp.concatenate(
        [plane_ref[c, CHUNK + LINE :, :] for c in range(PLANE)], 0
    ).astype(f32)
    row, col = iota((QSET, QSET), 0), iota((QSET, QSET), 1)
    target = jnp.sum(jnp.where(row == col, targets, 0.0), 0, keepdims=True).astype(i32)
    hit = row == target
    gap = lse - jnp.sum(jnp.where(hit, table, 0.0), 0, keepdims=True)
    loss = jnp.sum(gap, -1, keepdims=True)
    own = jnp.sum(jnp.where(row == mine, table, 0.0), 0, keepdims=True)
    dscore = GRAD_SCALE * (jnp.exp(own - lse) - jnp.where(target == mine, 1.0, 0.0))
    group = iota((QLEN, QSET), 1) // 4 == iota((QLEN, QSET), 0)
    wide = select(jnp.where(group, dscore, 0.0), row % 4 == col // QLEN)
    coef = wide * weight_ref[...] / sums_ref[...]
    for b in range(4):
        rows = slice(b * ROWS, (b + 1) * ROWS)
        total = jnp.zeros((ROWS, E), f32)
        for c in range(PLANE):
            queries = plane_ref[c, :CHUNK, :]
            close = dot(embed_ref[rows, :], queries, NT)
            factor = jnp.concatenate([coef[4 * c + j : 4 * c + j + 1, :] for j in range(4)], 1)
            coupling = (jnp.exp(close * (1.0 / TAU)) * factor).astype(bf16)
            total += dot(coupling, queries)
        out_ref[rows, :] = total * keep_ref[rows, :]
    out_ref[L:, :] = jnp.broadcast_to(loss, (8, E))


def grads_call(mine, table, plane, embed, keep, sums, weight):
    return call(grads_kernel, shape((L + 8, E), f32), [SMEM] + [VMEM] * 6, flops=2 * 10**9)(
        mine, table, plane, embed, keep, sums, weight
    )


def add_kernel(own_ref, got_ref, sum_ref, send_ref):
    for b in range(4):
        rows = slice(b * ROWS, (b + 1) * ROWS)
        other = (b ^ 1) * ROWS
        total = own_ref[rows, :] + got_ref[other : other + ROWS, :]
        sum_ref[rows, :] = total
        send_ref[rows, :] = total.astype(bf16)
    loss = own_ref[L:, :] + got_ref[L:, :]
    sum_ref[L:, :] = loss
    high = loss.astype(bf16).astype(f32)
    middle = (loss - high).astype(bf16).astype(f32)
    low = loss - high - middle
    send_ref[L : L + 16, :] = jnp.concatenate([high, middle], 0).astype(bf16)
    send_ref[L + 16 :, :] = jnp.concatenate([low, low], 0).astype(bf16)


def add_call(own, got):
    return call(add_kernel, (shape((L + 8, E), f32), shape((L + 32, E), bf16)), [VMEM] * 2)(own, got)


def backward_kernel(
    sum_ref,
    got_ref,
    proj_ref,
    unit_ref,
    inv_ref,
    gain_ref,
    wp_ref,
    wo_ref,
    att_ref,
    q_ref,
    k_ref,
    v_ref,
    prow_ref,
    pcol_ref,
    wq_ref,
    wk_ref,
    wv_ref,
    out_ref,
    loss_ref,
    wide_ref,
    mixed_ref,
    ag_ref,
    qg_ref,
    kg_ref,
    vg_ref,
):
    tail = got_ref[L:, :].astype(f32)
    loss_ref[...] = sum_ref[L:, :] + (tail[0:8] + tail[8:16] + tail[16:24])
    got = got_ref[:L, :].astype(f32)
    grad = sum_ref[:L, :] + jnp.concatenate([got[2 * ROWS :], got[: 2 * ROWS]], 0)
    proj = proj_ref[...]
    scale = lax.rsqrt(jnp.sum(proj * proj, -1, keepdims=True) + 1e-06)
    embed = proj * scale
    proj_grad = ((grad - embed * jnp.sum(embed * grad, -1, keepdims=True)) * scale).astype(bf16)
    wide_ref[...] = dot(proj_grad, wp_ref[...], NT)
    for c in range(8):
        rows = slice(c * 64, (c + 1) * 64)
        gained = wide_ref[rows, :] * gain_ref[...]
        unit = unit_ref[rows, :]
        along = jnp.mean(gained * unit, -1, keepdims=True)
        mixed = inv_ref[rows, 0:1] * (gained - jnp.mean(gained, -1, keepdims=True) - unit * along)
        if c < 2:
            wide_ref[rows, :] = mixed
        mixed_ref[rows, :] = mixed.astype(bf16)
    ag_ref[...] = dot(mixed_ref[...], wo_ref[...], NT).astype(bf16)
    first = iota((ROWS, 2 * HD), 1) < HD
    for pair in range(HEADS // 2):
        lanes = slice(pair * 2 * HD, (pair + 1) * 2 * HD)
        kp = k_ref[:, lanes]
        vp = v_ref[:, lanes]
        grads = [[], [], []]
        for half in range(2):
            head = 2 * pair + half
            own = first if half == 0 else ~first
            kg = jnp.zeros((ROWS, 2 * HD), f32)
            vg = jnp.zeros((ROWS, 2 * HD), f32)
            for b in range(4):
                rows = slice(b * ROWS, (b + 1) * ROWS)
                agp = ag_ref[rows, lanes]
                part = jnp.where(own, agp, jnp.zeros_like(agp))
                delta = jnp.sum(
                    part.astype(f32) * att_ref[rows, lanes].astype(f32), -1, keepdims=True
                )
                if b == 0:
                    inner = dot(part, vp, NT)
                    score = (prow_ref[head] * ((inner - delta) * HD**-0.5)).astype(bf16)
                    grads[0].append(dot(score, kp))
                    inner = inner[:, :ROWS]
                    score = score[:, :ROWS]
                else:
                    inner = dot(part, vp[:ROWS], NT)
                    score = (pcol_ref[head, rows, :] * ((inner - delta) * HD**-0.5)).astype(bf16)
                kg += dot(score, q_ref[rows, lanes], TN)
                vg += dot(pcol_ref[head, rows, :].astype(bf16), agp, TN)
            grads[1].append(kg)
            grads[2].append(vg)
        for ref, (even, odd) in zip((qg_ref, kg_ref, vg_ref), grads):
            ref[:, lanes] = jnp.where(first, even, odd).astype(bf16)
    total = wide_ref[:ROWS, :]
    total += dot(qg_ref[...], wq_ref[...], NT)
    total += dot(kg_ref[...], wk_ref[...], NT)
    total += dot(vg_ref[...], wv_ref[...], NT)
    out_ref[...] = total.astype(bf16)


def backward(summed, got, kept, ln_gain, w_proj, w_out, w_query, w_key, w_value):
    q, k, v, att, prow, pcol, unit, inv, proj = kept
    width = HEADS * HD
    return call(
        backward_kernel,
        (shape((ROWS, D), bf16), shape((8, E), f32)),
        [VMEM] * 17,
        [
            pltpu.VMEM((L, D), f32),
            pltpu.VMEM((L, D), bf16),
            pltpu.VMEM((L, width), bf16),
            pltpu.VMEM((ROWS, width), bf16),
            pltpu.VMEM((ROWS, width), bf16),
            pltpu.VMEM((ROWS, width), bf16),
        ],
        flops=3 * 10**9,
    )(
        summed, got, proj, unit, inv, ln_gain[None], w_proj, w_out, att, q, k, v, prow, pcol,
        w_query, w_key, w_value,
    )


def spread(x, axes):
    return lax.all_to_all(x, axes, 0, 0)


def body(
    hidden,
    doc_len,
    doc_keep,
    w_query,
    w_key,
    w_value,
    w_out,
    ln_gain,
    w_proj,
    queries,
    query_mask,
    positive,
):
    me = lax.axis_index("yhi") * 2 + lax.axis_index("core")
    mine = lax.axis_index(DP)
    query_send, own = pack(positive, queries, query_mask, hidden, doc_keep)
    by_core = lax.ppermute(own, "core", SWAP)
    by_yhi = lax.ppermute(own, "yhi", SWAP)
    line = spread(query_send, "z")
    by_both = lax.ppermute(by_yhi, "core", SWAP)
    plane = spread(repack(line), ("ylo", "x"))
    scalars = jnp.stack([doc_len[0], me])
    *kept, embed, keep = forward(
        scalars, (own, by_core, by_yhi, by_both), w_query, w_key, w_value, w_out, ln_gain, w_proj
    )
    send, sums, weight = sums_call(plane, embed, keep)
    table = spread(send, DP)
    partial = grads_call(mine[None], table, plane, embed, keep, sums, weight)
    summed, half = add_call(partial, lax.ppermute(partial, "core", SWAP))
    got = lax.ppermute(half, "yhi", SWAP)
    out, loss = backward(summed, got, kept, ln_gain, w_proj, w_out, w_query, w_key, w_value)
    return (out, loss[0, 0])


def solution(mesh):
    fine = Mesh(np.asarray(mesh.devices).reshape(SIZES), AXES)
    placed = (
        P(AXES, None),
        P(DP),
        P(AXES),
        P(),
        P(),
        P(),
        P(),
        P(),
        P(),
        P(AXES, None, None),
        P(AXES, None),
        P(AXES),
    )
    return jax.shard_map(
        body, mesh=fine, in_specs=placed, out_specs=(P(AXES, None), P()), check_vma=False
    )
```

time: 168 us -> 170 us (1.012)
  matrix products: 40.1 us -> 0 us
  Pallas kernels: 0 us -> 33.4 us
  blocking collectives: 0 us -> 28.1 us
  other arithmetic: 21.2 us -> 0.08 us
  local copies, waits for them, and re-layouts: 15.7 us -> 34.9 us
  starting transfers between devices: 52.7 us -> 42.1 us
  waiting for transfers between devices: 34.2 us -> 28.1 us
    pallas_call x0 -> x7, Pallas kernels: none -> 33.4 us  [the longest x1 16.5 us: forward(): call(forward_kernel, (square, square, square, square, shape((HEADS, ROWS,...]
    dot_general x16 -> x0, matrix products: 32.4 us -> none  [the longest x11 19.3 us: dot32(): return jnp.dot(left, right, preferred_element_type=f32)]
    unnamed x82 -> x96, local copies, waits for them, and re-layouts: 3.97 us -> 34.4 us
    all_to_all x0 -> x1, blocking collectives: none -> 28.1 us  [spread(): return lax.all_to_all(x, axes, 0, 0)]
    all_to_all x3 -> x2, starting transfers between devices: 32 us -> 18.6 us  [spread(): return lax.all_to_all(x, axes, 0, 0)]
    convert_element_type x5 -> x0, other arithmetic: 10.9 us -> none  [the longest x1 8.29 us: body(): probs_b = probs.astype(bf16)]
    all_to_all x3 -> x2, waiting for transfers between devices: 24.2 us -> 13.4 us  [spread(): return lax.all_to_all(x, axes, 0, 0)]
    ppermute x1, waiting for transfers between devices: 0.01 us -> 8.7 us  [body(): by_yhi = lax.ppermute(own, 'yhi', SWAP)]
  transfers between devices with their start and end apart: 8 -> 7, of which waited for: 5 -> 4; matrix products, arithmetic and copies ran while one was open for 20% -> 0% of each run, Pallas kernels for 0% -> 10%
where the time goes in v2:
time: 170 us; the launch traced here: 169 us
  starting transfers between devices  42.1 us (25%)
  local copies, waits for them, and re-layouts  34.9 us (21%)
  Pallas kernels  33.4 us (20%)
  blocking collectives  28.1 us (17%)
  waiting for transfers between devices  28.1 us (17%)
  between operations  2.13 us (1%)
    unnamed x96, local copies, waits for them, and re-layouts  34.4 us
    all_to_all x1, blocking collectives, spread(): return lax.all_to_all(x, axes, 0, 0)  28.1 us
    all_to_all x2, starting transfers between devices, spread(): return lax.all_to_all(x, axes, 0, 0)  18.6 us
    pallas_call x1, Pallas kernels, forward(): call(forward_kernel, (square, square, square, square, shape((HEADS, ROWS,...  16.5 us
    all_to_all x2, waiting for transfers between devices, spread(): return lax.all_to_all(x, axes, 0, 0)  13.4 us
    ppermute x1, waiting for transfers between devices, body(): by_yhi = lax.ppermute(own, 'yhi', SWAP)  8.7 us
    pallas_call x1, Pallas kernels, backward(): call(backward_kernel, (shape((ROWS, D), bf16), shape((8, E), f32)), [VMEM...  8.41 us
    ppermute x1, starting transfers between devices, body(): by_core = lax.ppermute(own, 'core', SWAP)  7.3 us
  transfers between devices with their start and end apart: 7, of which 4 were waited for; matrix products, arithmetic and copies ran while one was open for 0% of the time, Pallas kernels for 10%

profile of v2, /device:TPU:1, one launch (start us, length us, event | category | flops | bytes accessed | tf_op | source)
XLA Modules:
  0.0 168.8 jit_solution(4583553109014775638)
XLA Ops:
  1.3 0.9 copy-done.19
  2.2 0.7 copy-done.26
  2.9 0.7 copy-done.28
  3.6 0.7 copy-done.29
  4.2 0.1 shard_map.131
  4.4 28.1 %all_to_all.21.line_ref = bf16[16,48,128]{2,1,0:T(8,128)(2,1)S(1)} all-to-all(bf16[16,48,128]{2,1,0:T(8,128)(2,1)S(1)} %get-tuple-element.22), channel_id=1, replica_groups=mesh['z'=16,'ylo'=2,'x'=4,'yhi'=2,'core'=2] {'z'}, dimensions={0} | all-to-all | bytes 393216 | tf_op jit(solution)/shard_map/all_to_all | solution.py:415
  32.5 1.2 shard_map.132
  33.6 5.0 %all-to-all-start.1 = ((bf16[8,544,128]{2,1,0:T(8,128)(2,1)}), bf16[8,544,128]{2,1,0:T(8,128)(2,1)S(1)}, u32[]{:S(2)}, u32[]{:S(2)}) async-start(bf16[8,544,128]{2,1,0:T(8,128)(2,1)} %shard_map.132), calls=%async_computation.1 | async-start | bytes 2228224 | tf_op jit(solution)/shard_map/all_to_all | solution.py:415
  38.7 4.5 %collective-permute-start.1 = (bf16[144,1024]{1,0:T(8,128)(2,1)S(1)}, bf16[144,1024]{1,0:T(8,128)(2,1)S(1)}, u32[]{:S(2)}, u32[]{:S(2)}) collective-permute-start(bf16[144,1024]{1,0:T(8,128)(2,1)S(1)} %get-tuple-element.23.x0_ref), channel_id=1, source_target_pairs={{0,2},{2,0},{1,3},{3,1},{4,6},{6,4},{5,7},{7,5},{8,10},{10,8},{9,1... | collective-permute-start | bytes 884744 | tf_op jit(solution)/shard_map/ppermute | solution.py:436
  43.2 7.3 %collective-permute-start = (bf16[144,1024]{1,0:T(8,128)(2,1)S(1)}, bf16[144,1024]{1,0:T(8,128)(2,1)S(1)}, u32[]{:S(2)}, u32[]{:S(2)}) collective-permute-start(bf16[144,1024]{1,0:T(8,128)(2,1)S(1)} %get-tuple-element.23.x0_ref), channel_id=1, source_target_pairs={{0,1},{1,0},{2,3},{3,2},{4,5},{5,4},{6,7},{7,6},{8,9},{9,8},{10,11... | collective-permute-start | bytes 884744 | tf_op jit(solution)/shard_map/ppermute | solution.py:435
  50.5 8.7 %collective-permute-done.1.x2_ref = bf16[144,1024]{1,0:T(8,128)(2,1)S(1)} collective-permute-done((bf16[144,1024]{1,0:T(8,128)(2,1)S(1)}, bf16[144,1024]{1,0:T(8,128)(2,1)S(1)}, u32[]{:S(2)}, u32[]{:S(2)}) %collective-permute-start.1) | collective-permute-done | bytes 294944 | tf_op jit(solution)/shard_map/ppermute | solution.py:436
  59.2 4.6 %collective-permute-start.2 = (bf16[144,1024]{1,0:T(8,128)(2,1)S(1)}, bf16[144,1024]{1,0:T(8,128)(2,1)S(1)}, u32[]{:S(2)}, u32[]{:S(2)}) collective-permute-start(bf16[144,1024]{1,0:T(8,128)(2,1)S(1)} %collective-permute-done.1.x2_ref), channel_id=1, source_target_pairs={{0,1},{1,0},{2,3},{3,2},{4,5},{5,4},{6,7},{7,6},{8,9},{9,8},{10,11... | collective-permute-start | bytes 884744 | tf_op jit(solution)/shard_map/ppermute | solution.py:438
  63.8 0.7 copy-done.32
  65.2 0.1 pad_add_fusion.scalar_ref
  65.3 0.0 collective-permute-done.x1_ref
  65.3 0.7 copy-done.34
  66.0 0.0 collective-permute-done.2.x3_ref
  66.0 0.7 copy-done.36
  66.7 1.2 copy-done.3
  68.0 1.2 copy-done.5
  69.2 1.2 copy-done.7
  70.4 1.2 copy-done.9
  71.6 1.0 copy-done.31
  72.6 1.0 copy-done.33
  73.6 1.0 copy-done.35
  74.5 1.0 copy-done.37
  75.5 16.5 %shard_map.133 = (bf16[512,512]{1,0:T(8,128)(2,1)S(1)}, bf16[512,512]{1,0:T(8,128)(2,1)S(1)}, bf16[512,512]{1,0:T(8,128)(2,1)S(1)}, bf16[512,512]{1,0:T(8,128)(2...) custom-call(s32[2]{0:T(128)S(1)} %pad_add_fusion.scalar_ref, ...), custom_call_target="tpu_custom_call" | custom-call | flops 4000000000 | bytes 8388608 | tf_op jit(solution)/shard_map/pallas_call | solution.py:195
  92.0 1.4 copy-done
  93.3 0.8 copy-done.11
  94.2 0.8 copy-done.13
  94.9 0.8 copy-done.15
  95.7 0.8 copy-done.17
  96.5 0.7 copy-done.21
  97.2 0.7 copy-done.23
  98.0 0.7 copy-done.38
  98.7 0.6 copy-done.41
  99.3 0.9 copy-done.39
  100.3 0.9 copy-done.42
  101.2 1.8 %shard_map.134 = (f32[128,128]{1,0:T(8,128)S(1)}, f32[32,128]{1,0:T(8,128)S(1)}, f32[32,128]{1,0:T(8,128)S(1)}) custom-call(bf16[8,544,128]{2,1,0:T(8,128)(2,1)S(1)} %all-to-all-done.1.plane_ref, bf16[512,128]{1,0:T(8,128)(2,1)S(1)} %copy-done.42, f32[512,128]{1,0:T(8,128)S(1)} %copy-done.39), custom_call_target="tpu_custom_call" | custom-call | flops 1000000000 | bytes 8388608 | tf_op jit(solution)/shard_map/pallas_call | solution.py:242
  103.0 0.6 copy-done.25
  103.6 0.6 copy-done.44
  104.2 0.6 copy-done.46
  104.9 13.6 %all-to-all-start.2 = ((f32[128,1,128]{2,1,0:T(1,128)}), f32[128,1,128]{2,1,0:T(1,128)S(1)}, u32[]{:S(2)}, u32[]{:S(2)}) async-start(f32[128,1,128]{2,1,0:T(1,128)} %bitcast.11), calls=%async_computation.2 | async-start | bytes 131072 | tf_op jit(solution)/shard_map/all_to_all | solution.py:415
  118.4 13.4 %all-to-all-done.2 = f32[128,1,128]{2,1,0:T(1,128)S(1)} async-done(((f32[128,1,128]{2,1,0:T(1,128)}), f32[128,1,128]{2,1,0:T(1,128)S(1)}, u32[]{:S(2)}, u32[]{:S(2)}) %all-to-all-start.2) | async-done | bytes 65568 | tf_op jit(solution)/shard_map/all_to_all | solution.py:415
  131.9 0.9 copy-done.40
  132.8 0.9 copy-done.43
  133.7 0.7 copy-done.45
  134.4 0.7 copy-done.47
  135.2 0.0 copy-start.8
  135.2 5.3 %shard_map.135.own_ref = f32[520,128]{1,0:T(8,128)S(1)} custom-call(s32[1]{0:T(128)} %bitcast.mine_ref, f32[128,128]{1,0:T(8,128)S(1)} %bitcast.10, bf16[8,544,128]{2,1,0:T(8,128)(2,1)S(1)} %all-to-all-done.1.plane_ref, bf16[512,128]{1,0:T(8,128)(2,1)S(1)} %copy-done.43, f32[512,128]{1,0:T(8,128)S(1)} %copy-done.40, f32[32,128]{1,0:T(8,128)S(1)} %copy-done.45, ...), custom_call_target="tpu_custom_call" | custom-call | flops 2000000000 | bytes 8388608 | tf_op jit(solution)/shard_map/pallas_call | solution.py:281
  140.5 3.6 %collective-permute-start.3 = (f32[520,128]{1,0:T(8,128)S(1)}, f32[520,128]{1,0:T(8,128)S(1)}, u32[]{:S(2)}, u32[]{:S(2)}) collective-permute-start(f32[520,128]{1,0:T(8,128)S(1)} %shard_map.135.own_ref), channel_id=1, source_target_pairs={{0,1},{1,0},{2,3},{3,2},{4,5},{5,4},{6,7},{7,6},{8,9},{9,8},{10,11... | collective-permute-start | bytes 798728 | tf_op jit(solution)/shard_map/ppermute | solution.py:447
  144.1 1.1 collective-permute-done.3.got_ref
  145.3 0.1 shard_map.136
  145.3 3.5 %collective-permute-start.4 = (bf16[544,128]{1,0:T(8,128)(2,1)S(1)}, bf16[544,128]{1,0:T(8,128)(2,1)S(1)}, u32[]{:S(2)}, u32[]{:S(2)}) collective-permute-start(bf16[544,128]{1,0:T(8,128)(2,1)S(1)} %get-tuple-element.30), channel_id=1, source_target_pairs={{0,2},{2,0},{1,3},{3,1},{4,6},{6,4},{5,7},{7,5},{8,10},{10,8},{9,1... | collective-permute-start | bytes 417800 | tf_op jit(solution)/shard_map/ppermute | solution.py:448
  148.8 4.8 %collective-permute-done.4.got_ref = bf16[544,128]{1,0:T(8,128)(2,1)S(1)} collective-permute-done((bf16[544,128]{1,0:T(8,128)(2,1)S(1)}, bf16[544,128]{1,0:T(8,128)(2,1)S(1)}, u32[]{:S(2)}, u32[]{:S(2)}) %collective-permute-start.4) | collective-permute-done | bytes 139296 | tf_op jit(solution)/shard_map/ppermute | solution.py:448
  153.6 0.0 copy-start.10
  153.7 1.2 copy-done.10
  154.9 1.0 copy-done.14
  155.9 1.0 copy-done.16
  157.0 1.0 copy-done.18
  158.0 0.9 copy-done.22
  159.0 0.9 copy-done.24
  159.9 8.4 %shard_map.137 = (bf16[128,1024]{1,0:T(8,128)(2,1)}, f32[8,128]{1,0:T(8,128)S(1)}) custom-call(f32[520,128]{1,0:T(8,128)S(1)} %get-tuple-element.29.sum_ref, bf16[544,128]{1,0:T(8,128)(2,1)S(1)} %collective-permute-done.4.got_ref, f32[512,128]{1,0:T(8,128)S(1)} %copy-done.24, f32[512,1024]{1,0:T(8,128)S(1)} %copy-done.2, f32[512,128]{1,0:T(8,128)S(1)} %copy-done.22, ...), custom_call_target="tpu_custom_call" | custom-call | flops 3000000000 | bytes 8388608 | tf_op jit(solution)/shard_map/pallas_call | solution.py:395
  168.3 0.5 slice.3
  (56 shorter events, 0.1 us)
Async XLA Ops:
  1.3 1.0 copy-start.19
  2.2 0.7 copy-start.26
  2.9 0.7 copy-start.28
  3.6 0.7 copy-start.29
  4.2 62.5 %copy-start.20 = (bf16[1024,128]{1,0:T(8,128)(2,1)S(1)}, bf16[1024,128]{1,0:T(8,128)(2,1)}, u32[]{:S(2)}) copy-start(bf16[1024,128]{1,0:T(8,128)(2,1)} %wp_ref.3) | copy-start | bytes 786436
  4.2 62.5 %copy-start.27 = (f32[1024]{0:T(1024)S(1)}, f32[1024]{0:T(1024)}, u32[]{:S(2)}) copy-start(f32[1024]{0:T(1024)} %param.19) | copy-start | bytes 12292
  4.4 61.6 %copy-start.30 = (bf16[144,1024]{1,0:T(8,128)(2,1)}, bf16[144,1024]{1,0:T(8,128)(2,1)S(1)}, u32[]{:S(2)}) copy-start(bf16[144,1024]{1,0:T(8,128)(2,1)S(1)} %get-tuple-element.23.x0_ref) | copy-start | bytes 884740
  33.6 65.7 %all-to-all-start.1 = ((bf16[8,544,128]{2,1,0:T(8,128)(2,1)}), bf16[8,544,128]{2,1,0:T(8,128)(2,1)S(1)}, u32[]{:S(2)}, u32[]{:S(2)}) async-start(bf16[8,544,128]{2,1,0:T(8,128)(2,1)} %shard_map.132), calls=%async_computation.1 | async-start | bytes 2228224 | tf_op jit(solution)/shard_map/all_to_all | solution.py:415
  38.7 20.5 %collective-permute-start.1 = (bf16[144,1024]{1,0:T(8,128)(2,1)S(1)}, bf16[144,1024]{1,0:T(8,128)(2,1)S(1)}, u32[]{:S(2)}, u32[]{:S(2)}) collective-permute-start(bf16[144,1024]{1,0:T(8,128)(2,1)S(1)} %get-tuple-element.23.x0_ref), channel_id=1, source_target_pairs={{0,2},{2,0},{1,3},{3,1},{4,6},{6,4},{5,7},{7,5},{8,10},{10,8},{9,1... | collective-permute-start | bytes 884744 | tf_op jit(solution)/shard_map/ppermute | solution.py:436
  43.2 22.1 %collective-permute-start = (bf16[144,1024]{1,0:T(8,128)(2,1)S(1)}, bf16[144,1024]{1,0:T(8,128)(2,1)S(1)}, u32[]{:S(2)}, u32[]{:S(2)}) collective-permute-start(bf16[144,1024]{1,0:T(8,128)(2,1)S(1)} %get-tuple-element.23.x0_ref), channel_id=1, source_target_pairs={{0,1},{1,0},{2,3},{3,2},{4,5},{5,4},{6,7},{7,6},{8,9},{9,8},{10,11... | collective-permute-start | bytes 884744 | tf_op jit(solution)/shard_map/ppermute | solution.py:435
  59.2 6.8 %collective-permute-start.2 = (bf16[144,1024]{1,0:T(8,128)(2,1)S(1)}, bf16[144,1024]{1,0:T(8,128)(2,1)S(1)}, u32[]{:S(2)}, u32[]{:S(2)}) collective-permute-start(bf16[144,1024]{1,0:T(8,128)(2,1)S(1)} %collective-permute-done.1.x2_ref), channel_id=1, source_target_pairs={{0,1},{1,0},{2,3},{3,2},{4,5},{5,4},{6,7},{7,6},{8,9},{9,8},{10,11... | collective-permute-start | bytes 884744 | tf_op jit(solution)/shard_map/ppermute | solution.py:438
  63.8 0.7 copy-start.32
  65.3 0.7 copy-start.34
  66.0 0.7 copy-start.36
  66.7 1.2 copy-start.3
  68.0 1.2 copy-start.5
  69.2 1.2 copy-start.7
  70.4 1.2 copy-start.9
  71.6 1.0 copy-start.31
  72.6 1.0 copy-start.33
  73.6 1.0 copy-start.35
  74.5 1.0 copy-start.37
  92.0 1.4 copy-start
  93.3 0.8 copy-start.11
  94.1 0.8 copy-start.13
  94.9 0.8 copy-start.15
  95.7 0.8 copy-start.17
  96.5 0.7 copy-start.21
  97.2 0.7 copy-start.23
  98.0 0.7 copy-start.38
  98.7 0.6 copy-start.41
  99.3 1.0 copy-start.39
  100.3 0.9 copy-start.42
  103.0 0.6 copy-start.25
  103.6 0.6 copy-start.44
  104.2 0.6 copy-start.46
  104.9 27.0 %all-to-all-start.2 = ((f32[128,1,128]{2,1,0:T(1,128)}), f32[128,1,128]{2,1,0:T(1,128)S(1)}, u32[]{:S(2)}, u32[]{:S(2)}) async-start(f32[128,1,128]{2,1,0:T(1,128)} %bitcast.11), calls=%async_computation.2 | async-start | bytes 131072 | tf_op jit(solution)/shard_map/all_to_all | solution.py:415
  131.9 1.0 copy-start.40
  132.8 0.9 copy-start.43
  133.7 0.7 copy-start.45
  134.4 0.7 copy-start.47
  135.2 18.4 %copy-start.1 = (f32[8,512,128]{2,1,0:T(8,128)S(1)}, f32[8,512,128]{2,1,0:T(8,128)}, u32[]{:S(2)}) copy-start(f32[8,512,128]{2,1,0:T(8,128)} %copy-done) | copy-start | bytes 6291460
  135.2 18.4 %copy-start.2 = (f32[512,1024]{1,0:T(8,128)S(1)}, f32[512,1024]{1,0:T(8,128)}, u32[]{:S(2)}) copy-start(f32[512,1024]{1,0:T(8,128)} %get-tuple-element.32.unit_ref) | copy-start | bytes 6291460
  135.2 18.4 %copy-start.4 = (bf16[1024,512]{1,0:T(8,128)(2,1)S(1)}, bf16[1024,512]{1,0:T(8,128)(2,1)}, u32[]{:S(2)}) copy-start(bf16[1024,512]{1,0:T(8,128)(2,1)} %wq_ref.3) | copy-start | bytes 3145732
  135.2 18.5 %copy-start.6 = (bf16[1024,512]{1,0:T(8,128)(2,1)S(1)}, bf16[1024,512]{1,0:T(8,128)(2,1)}, u32[]{:S(2)}) copy-start(bf16[1024,512]{1,0:T(8,128)(2,1)} %wk_ref.3) | copy-start | bytes 3145732
  135.2 18.5 %copy-start.8 = (bf16[1024,512]{1,0:T(8,128)(2,1)S(1)}, bf16[1024,512]{1,0:T(8,128)(2,1)}, u32[]{:S(2)}) copy-start(bf16[1024,512]{1,0:T(8,128)(2,1)} %wv_ref.3) | copy-start | bytes 3145732
  135.2 18.5 %copy-start.12 = (bf16[512,512]{1,0:T(8,128)(2,1)S(1)}, bf16[512,512]{1,0:T(8,128)(2,1)}, u32[]{:S(2)}) copy-start(bf16[512,512]{1,0:T(8,128)(2,1)} %copy-done.11) | copy-start | bytes 1572868
  140.5 4.7 %collective-permute-start.3 = (f32[520,128]{1,0:T(8,128)S(1)}, f32[520,128]{1,0:T(8,128)S(1)}, u32[]{:S(2)}, u32[]{:S(2)}) collective-permute-start(f32[520,128]{1,0:T(8,128)S(1)} %shard_map.135.own_ref), channel_id=1, source_target_pairs={{0,1},{1,0},{2,3},{3,2},{4,5},{5,4},{6,7},{7,6},{8,9},{9,8},{10,11... | collective-permute-start | bytes 798728 | tf_op jit(solution)/shard_map/ppermute | solution.py:447
  145.3 8.3 %collective-permute-start.4 = (bf16[544,128]{1,0:T(8,128)(2,1)S(1)}, bf16[544,128]{1,0:T(8,128)(2,1)S(1)}, u32[]{:S(2)}, u32[]{:S(2)}) collective-permute-start(bf16[544,128]{1,0:T(8,128)(2,1)S(1)} %get-tuple-element.30), channel_id=1, source_target_pairs={{0,2},{2,0},{1,3},{3,1},{4,6},{6,4},{5,7},{7,5},{8,10},{10,8},{9,1... | collective-permute-start | bytes 417800 | tf_op jit(solution)/shard_map/ppermute | solution.py:448
  153.6 1.2 copy-start.10
  154.9 1.0 copy-start.14
  155.9 1.0 copy-start.16
  157.0 1.0 copy-start.18
  158.0 0.9 copy-start.22
  159.0 0.9 copy-start.24

commit v3 on v2

--- a/solution.py
+++ b/solution.py
@@ -25,11 +25,13 @@
 LINE = 16
 PLANE = 8
 CHUNK = LINE * QLEN
+STRIP = 64
 SWAP = [(0, 1), (1, 0)]
 bf16 = jnp.bfloat16
 f32 = jnp.float32
 i32 = jnp.int32
-VMEM = pl.BlockSpec(memory_space=pltpu.VMEM)
+BLOCK = pl.BlockSpec()
+ANY = pl.BlockSpec(memory_space=pl.ANY)
 SMEM = pl.BlockSpec(memory_space=pltpu.SMEM)
 NN = (((1,), (0,)), ((), ()))
 NT = (((1,), (1,)), ((), ()))
@@ -53,16 +55,31 @@
     return dot(high, choice) + (dot(middle, choice) + dot(low, choice))
 
 
-def call(kernel, outs, ins, scratch=(), flops=0, limit=40):
+def position():
+    return lax.axis_index("yhi") * 2 + lax.axis_index("core"), lax.axis_index(DP)
+
+
+def call(kernel, outs, ins, out_specs=None, scratch=(), flops=0):
     return pl.pallas_call(
         kernel,
         out_shape=outs,
         in_specs=ins,
-        out_specs=jax.tree.map(lambda _: VMEM, outs),
+        out_specs=jax.tree.map(lambda _: BLOCK, outs) if out_specs is None else out_specs,
         scratch_shapes=list(scratch),
-        compiler_params=pltpu.CompilerParams(vmem_limit_bytes=limit * 2**20),
-        cost_estimate=pl.CostEstimate(flops=flops, bytes_accessed=8 * 2**20, transcendentals=0),
+        compiler_params=pltpu.CompilerParams(vmem_limit_bytes=56 * 2**20),
+        cost_estimate=pl.CostEstimate(flops=flops, bytes_accessed=4 * 2**20, transcendentals=0),
     )
+
+
+class Moves:
+    def __init__(self, sems):
+        self.sems, self.used = sems, 0
+
+    def start(self, source, target):
+        copy = pltpu.make_async_copy(source, target, self.sems.at[self.used])
+        self.used += 1
+        copy.start()
+        return copy
 
 
 def shape(dims, kind):
@@ -89,11 +106,11 @@
     return call(
         pack_kernel,
         (shape((LINE, QLEN + AUX, E), bf16), shape((ROWS + AUX, D), bf16)),
-        [SMEM, VMEM, VMEM, VMEM, VMEM],
+        [SMEM] + [BLOCK] * 4,
     )(positive, queries[0], query_mask, hidden, doc_keep[None])
 
 
-def repack_kernel(line_ref, out_ref):
+def repack_kernel(line_ref, after_ref, out_ref):
     aux = line_ref[:, QLEN:, :].astype(f32)
     weights = aux[:, 0, :].astype(bf16)
     target = aux[:, 1, :].astype(bf16)
@@ -104,16 +121,36 @@
         out_ref[p, CHUNK + LINE :, :] = target
 
 
-def repack(line):
-    return call(repack_kernel, shape((PLANE, CHUNK + 2 * LINE, E), bf16), [VMEM])(line)
+def repack(line, after):
+    out = shape((PLANE, CHUNK + 2 * LINE, E), bf16)
+    return call(repack_kernel, out, [BLOCK, ANY])(line, after)
 
 
 def forward_kernel(
-    scalar_ref,
-    x0_ref,
-    x1_ref,
-    x2_ref,
-    x3_ref,
+    length_ref,
+    x0_any,
+    x1_any,
+    x2_any,
+    x3_any,
+    wq_any,
+    wk_any,
+    wv_any,
+    wo_any,
+    gain_any,
+    wp_any,
+    q_any,
+    k_any,
+    v_any,
+    att_any,
+    prow_any,
+    pcol_any,
+    unit_any,
+    inv_any,
+    proj_any,
+    embed_any,
+    keep_any,
+    x_ref,
+    skip_ref,
     wq_ref,
     wk_ref,
     wv_ref,
@@ -131,86 +168,141 @@
     proj_ref,
     embed_ref,
     keep_ref,
-    x_ref,
+    score_ref,
+    prob_ref,
+    sems,
 ):
-    length = scalar_ref[0]
-    me = scalar_ref[1]
-    sources = (x0_ref, x1_ref, x2_ref, x3_ref)
+    moves = Moves(sems)
+    blocks = [
+        moves.start(source.at[pl.ds(0, ROWS)], x_ref.at[pl.ds(b * ROWS, ROWS)])
+        for b, source in enumerate((x0_any, x1_any, x2_any, x3_any))
+    ]
+    at_k = moves.start(wk_any, wk_ref)
+    skips = [
+        moves.start(source.at[pl.ds(ROWS, AUX), pl.ds(0, ROWS)], skip_ref.at[b])
+        for b, source in enumerate((x0_any, x1_any, x2_any, x3_any))
+    ]
+    at_q = moves.start(wq_any, wq_ref)
+    at_v = moves.start(wv_any, wv_ref)
+    at_o = moves.start(wo_any, wo_ref)
+    at_gain = moves.start(gain_any, gain_ref)
+    at_p = moves.start(wp_any, wp_ref)
+    ends = []
+    length = length_ref[0]
+    me, _ = position()
+    for copy in blocks:
+        copy.wait()
+    at_k.wait()
+    k_ref[...] = dot(x_ref[...], wk_ref[...]).astype(bf16)
+    ends.append(moves.start(k_ref, k_any))
+    at_q.wait()
+    q_ref[...] = dot(x_ref[...], wq_ref[...]).astype(bf16)
+    ends.append(moves.start(q_ref, q_any))
+    at_v.wait()
+    v_ref[...] = dot(x_ref[...], wv_ref[...]).astype(bf16)
+    ends.append(moves.start(v_ref, v_any))
     bias = []
-    for b, source in enumerate(sources):
-        rows = slice(b * ROWS, (b + 1) * ROWS)
-        x_ref[rows, :] = source[:ROWS, :]
+    for b in range(4):
+        skips[b].wait()
         start = jnp.bitwise_xor(me, b) * ROWS
-        skip = source[ROWS:, :ROWS].astype(f32)[0:1, :]
+        skip = skip_ref[b].astype(f32)[0:1, :]
         place = start + iota((1, ROWS), 1)
         valid = place < length
         bias.append(jnp.where(valid, 0.0, NEG))
         kept = jnp.where(valid & ((skip == 1.0) | (place == 0)), 1.0, 0.0)
         diagonal = iota((ROWS, ROWS), 0) == iota((ROWS, ROWS), 1)
         column = jnp.sum(jnp.where(diagonal, kept, 0.0), -1, keepdims=True)
-        keep_ref[rows, :] = jnp.broadcast_to(column, (ROWS, E))
+        keep_ref[b * ROWS : (b + 1) * ROWS, :] = jnp.broadcast_to(column, (ROWS, E))
+    ends.append(moves.start(keep_ref, keep_any))
     bias = jnp.concatenate(bias, 1)
-    x = x_ref[...]
-    k_ref[...] = dot(x, wk_ref[...]).astype(bf16)
-    q_ref[...] = dot(x, wq_ref[...]).astype(bf16)
-    v_ref[...] = dot(x, wv_ref[...]).astype(bf16)
-    first = iota((ROWS, 2 * HD), 1) < HD
+    first = iota((L, 2 * HD), 1) < HD
     for pair in range(HEADS // 2):
         lanes = slice(pair * 2 * HD, (pair + 1) * 2 * HD)
-        kp = k_ref[:, lanes]
-        vp = v_ref[:, lanes]
-        for b in range(4):
-            rows = slice(b * ROWS, (b + 1) * ROWS)
-            qp = q_ref[rows, lanes] * jnp.array(HD**-0.5, bf16)
-            mixes = []
-            for half in range(2):
-                head = 2 * pair + half
-                own = first if half == 0 else ~first
-                scores = dot(jnp.where(own, qp, jnp.zeros_like(qp)), kp, NT) + bias
+        qp = q_ref[:, lanes] * jnp.array(HD**-0.5, bf16)
+        mixes = []
+        for half in range(2):
+            head = 2 * pair + half
+            own = first if half == 0 else ~first
+            score_ref[half] = dot(jnp.where(own, qp, jnp.zeros_like(qp)), k_ref[:, lanes], NT)
+            for c in range(L // STRIP):
+                rows = slice(c * STRIP, (c + 1) * STRIP)
+                scores = score_ref[half, rows, :] + bias
                 expo = jnp.exp(scores - jnp.max(scores, -1, keepdims=True))
                 probs = expo * (1.0 / jnp.sum(expo, -1, keepdims=True))
-                if b == 0:
-                    prow_ref[head] = probs
+                if (c + 1) * STRIP <= ROWS:
+                    prow_ref[head, rows, :] = probs
                 pcol_ref[head, rows, :] = probs[:, :ROWS]
-                mixes.append(dot(probs.astype(bf16), vp))
-            att_ref[rows, lanes] = jnp.where(first, mixes[0], mixes[1]).astype(bf16)
+                prob_ref[half, rows, :] = probs.astype(bf16)
+            mixes.append(dot(prob_ref[half], v_ref[:, lanes]))
+        att_ref[:, lanes] = jnp.where(first, mixes[0], mixes[1]).astype(bf16)
+        two = pl.ds(2 * pair, 2)
+        ends.append(moves.start(prow_ref.at[two], prow_any.at[two]))
+        ends.append(moves.start(pcol_ref.at[two], pcol_any.at[two]))
+    ends.append(moves.start(att_ref, att_any))
+    at_o.wait()
     unit_ref[...] = dot(att_ref[...], wo_ref[...])
-    for c in range(8):
-        rows = slice(c * 64, (c + 1) * 64)
+    at_gain.wait()
+    for c in range(L // STRIP):
+        rows = slice(c * STRIP, (c + 1) * STRIP)
         mixed = x_ref[rows, :].astype(f32) + unit_ref[rows, :]
         centred = mixed - jnp.mean(mixed, -1, keepdims=True)
         inv = lax.rsqrt(jnp.mean(centred * centred, -1, keepdims=True) + 1e-05)
         unit = centred * inv
         unit_ref[rows, :] = unit
-        inv_ref[rows, :] = jnp.broadcast_to(inv, (64, E))
+        inv_ref[rows, :] = jnp.broadcast_to(inv, (STRIP, E))
         x_ref[rows, :] = (unit * gain_ref[...]).astype(bf16)
+    ends.append(moves.start(unit_ref, unit_any))
+    ends.append(moves.start(inv_ref, inv_any))
+    at_p.wait()
     proj = dot(x_ref[...], wp_ref[...])
     proj_ref[...] = proj
+    ends.append(moves.start(proj_ref, proj_any))
     scale = lax.rsqrt(jnp.sum(proj * proj, -1, keepdims=True) + 1e-06)
     embed_ref[...] = (proj * scale).astype(bf16)
-
-
-def forward(scalars, blocks, w_query, w_key, w_value, w_out, ln_gain, w_proj):
-    square = shape((L, HEADS * HD), bf16)
+    ends.append(moves.start(embed_ref, embed_any))
+    for copy in ends:
+        copy.wait()
+
+
+def forward(doc_len, blocks, w_query, w_key, w_value, w_out, ln_gain, w_proj):
+    width = HEADS * HD
+    square = shape((L, width), bf16)
+    outs = (
+        square,
+        square,
+        square,
+        square,
+        shape((HEADS, ROWS, L), f32),
+        shape((HEADS, L, ROWS), f32),
+        shape((L, D), f32),
+        shape((L, E), f32),
+        shape((L, E), f32),
+        shape((L, E), bf16),
+        shape((L, E), f32),
+    )
+    ins = [
+        pltpu.VMEM((L, D), bf16),
+        pltpu.VMEM((4, AUX, ROWS), bf16),
+        pltpu.VMEM((D, width), bf16),
+        pltpu.VMEM((D, width), bf16),
+        pltpu.VMEM((D, width), bf16),
+        pltpu.VMEM((width, D), bf16),
+        pltpu.VMEM((1, D), f32),
+        pltpu.VMEM((D, E), bf16),
+    ]
+    work = [
+        pltpu.VMEM((2, L, L), f32),
+        pltpu.VMEM((2, L, L), bf16),
+        pltpu.SemaphoreType.DMA((32,)),
+    ]
     return call(
         forward_kernel,
-        (
-            square,
-            square,
-            square,
-            square,
-            shape((HEADS, ROWS, L), f32),
-            shape((HEADS, L, ROWS), f32),
-            shape((L, D), f32),
-            shape((L, E), f32),
-            shape((L, E), f32),
-            shape((L, E), bf16),
-            shape((L, E), f32),
-        ),
-        [SMEM] + [VMEM] * 10,
-        [pltpu.VMEM((L, D), bf16)],
+        outs,
+        [SMEM] + [ANY] * 10,
+        tuple(ANY for _ in outs),
+        ins + [pltpu.VMEM(o.shape, o.dtype) for o in outs] + work,
         flops=4 * 10**9,
-    )(scalars, *blocks, w_query, w_key, w_value, w_out, ln_gain[None], w_proj)
+    )(doc_len, *blocks, w_query, w_key, w_value, w_out, ln_gain[None], w_proj)
 
 
 def sums_kernel(plane_ref, embed_ref, keep_ref, send_ref, sums_ref, weight_ref):
@@ -242,13 +334,13 @@
     return call(
         sums_kernel,
         (shape((DOCS, QSET), f32), shape((QLEN, E), f32), shape((QLEN, E), f32)),
-        [VMEM] * 3,
+        [BLOCK] * 3,
         flops=10**9,
     )(plane, embed, keep)
 
 
-def grads_kernel(mine_ref, table_ref, plane_ref, embed_ref, keep_ref, sums_ref, weight_ref, out_ref):
-    mine = mine_ref[0]
+def grads_kernel(table_ref, plane_ref, embed_ref, keep_ref, sums_ref, weight_ref, out_ref):
+    _, mine = position()
     table = table_ref[...]
     lse = jnp.log(jnp.sum(jnp.exp(table), 0, keepdims=True))
     targets = jnp.concatenate(
@@ -277,9 +369,9 @@
     out_ref[L:, :] = jnp.broadcast_to(loss, (8, E))
 
 
-def grads_call(mine, table, plane, embed, keep, sums, weight):
-    return call(grads_kernel, shape((L + 8, E), f32), [SMEM] + [VMEM] * 6, flops=2 * 10**9)(
-        mine, table, plane, embed, keep, sums, weight
+def grads_call(table, plane, embed, keep, sums, weight):
+    return call(grads_kernel, shape((L + 8, E), f32), [BLOCK] * 6, flops=2 * 10**9)(
+        table, plane, embed, keep, sums, weight
     )
 
 
@@ -300,36 +392,66 @@
 
 
 def add_call(own, got):
-    return call(add_kernel, (shape((L + 8, E), f32), shape((L + 32, E), bf16)), [VMEM] * 2)(own, got)
+    return call(add_kernel, (shape((L + 8, E), f32), shape((L + 32, E), bf16)), [BLOCK] * 2)(own, got)
 
 
 def backward_kernel(
     sum_ref,
     got_ref,
     proj_ref,
-    unit_ref,
+    wp_ref,
     inv_ref,
     gain_ref,
-    wp_ref,
+    unit_any,
+    wo_any,
+    att_any,
+    v_any,
+    k_any,
+    q_any,
+    prow_any,
+    pcol_any,
+    wq_any,
+    wk_any,
+    wv_any,
+    out_ref,
+    loss_ref,
+    unit_ref,
     wo_ref,
     att_ref,
+    v_ref,
+    k_ref,
     q_ref,
-    k_ref,
-    v_ref,
     prow_ref,
     pcol_ref,
     wq_ref,
     wk_ref,
     wv_ref,
-    out_ref,
-    loss_ref,
     wide_ref,
     mixed_ref,
     ag_ref,
     qg_ref,
     kg_ref,
     vg_ref,
+    sems,
 ):
+    moves = Moves(sems)
+    at_unit = moves.start(unit_any, unit_ref)
+    at_out = moves.start(wo_any, wo_ref)
+    at_att = [
+        moves.start(source, target)
+        for source, target in (
+            (att_any, att_ref),
+            (v_any, v_ref),
+            (k_any, k_ref),
+            (q_any, q_ref),
+            (prow_any, prow_ref),
+            (pcol_any, pcol_ref),
+        )
+    ]
+    at_weights = [
+        moves.start(source, target)
+        for source, target in ((wq_any, wq_ref), (wk_any, wk_ref), (wv_any, wv_ref))
+    ]
     tail = got_ref[L:, :].astype(f32)
     loss_ref[...] = sum_ref[L:, :] + (tail[0:8] + tail[8:16] + tail[16:24])
     got = got_ref[:L, :].astype(f32)
@@ -339,6 +461,7 @@
     embed = proj * scale
     proj_grad = ((grad - embed * jnp.sum(embed * grad, -1, keepdims=True)) * scale).astype(bf16)
     wide_ref[...] = dot(proj_grad, wp_ref[...], NT)
+    at_unit.wait()
     for c in range(8):
         rows = slice(c * 64, (c + 1) * 64)
         gained = wide_ref[rows, :] * gain_ref[...]
@@ -348,7 +471,10 @@
         if c < 2:
             wide_ref[rows, :] = mixed
         mixed_ref[rows, :] = mixed.astype(bf16)
+    at_out.wait()
     ag_ref[...] = dot(mixed_ref[...], wo_ref[...], NT).astype(bf16)
+    for copy in at_att:
+        copy.wait()
     first = iota((ROWS, 2 * HD), 1) < HD
     for pair in range(HEADS // 2):
         lanes = slice(pair * 2 * HD, (pair + 1) * 2 * HD)
@@ -382,6 +508,8 @@
             grads[2].append(vg)
         for ref, (even, odd) in zip((qg_ref, kg_ref, vg_ref), grads):
             ref[:, lanes] = jnp.where(first, even, odd).astype(bf16)
+    for copy in at_weights:
+        copy.wait()
     total = wide_ref[:ROWS, :]
     total += dot(qg_ref[...], wq_ref[...], NT)
     total += dot(kg_ref[...], wk_ref[...], NT)
@@ -392,23 +520,23 @@
 def backward(summed, got, kept, ln_gain, w_proj, w_out, w_query, w_key, w_value):
     q, k, v, att, prow, pcol, unit, inv, proj = kept
     width = HEADS * HD
+    moved = (unit, w_out, att, v, k, q, prow, pcol, w_query, w_key, w_value)
     return call(
         backward_kernel,
         (shape((ROWS, D), bf16), shape((8, E), f32)),
-        [VMEM] * 17,
-        [
+        [BLOCK] * 6 + [ANY] * len(moved),
+        scratch=[pltpu.VMEM(m.shape, m.dtype) for m in moved]
+        + [
             pltpu.VMEM((L, D), f32),
             pltpu.VMEM((L, D), bf16),
             pltpu.VMEM((L, width), bf16),
             pltpu.VMEM((ROWS, width), bf16),
             pltpu.VMEM((ROWS, width), bf16),
             pltpu.VMEM((ROWS, width), bf16),
+            pltpu.SemaphoreType.DMA((len(moved),)),
         ],
         flops=3 * 10**9,
-    )(
-        summed, got, proj, unit, inv, ln_gain[None], w_proj, w_out, att, q, k, v, prow, pcol,
-        w_query, w_key, w_value,
-    )
+    )(summed, got, proj, w_proj, inv, ln_gain[None], *moved)
 
 
 def spread(x, axes):
@@ -429,21 +557,18 @@
     query_mask,
     positive,
 ):
-    me = lax.axis_index("yhi") * 2 + lax.axis_index("core")
-    mine = lax.axis_index(DP)
     query_send, own = pack(positive, queries, query_mask, hidden, doc_keep)
     by_core = lax.ppermute(own, "core", SWAP)
     by_yhi = lax.ppermute(own, "yhi", SWAP)
     line = spread(query_send, "z")
     by_both = lax.ppermute(by_yhi, "core", SWAP)
-    plane = spread(repack(line), ("ylo", "x"))
-    scalars = jnp.stack([doc_len[0], me])
+    plane = spread(repack(line, by_both), ("ylo", "x"))
     *kept, embed, keep = forward(
-        scalars, (own, by_core, by_yhi, by_both), w_query, w_key, w_value, w_out, ln_gain, w_proj
+        doc_len, (own, by_core, by_yhi, by_both), w_query, w_key, w_value, w_out, ln_gain, w_proj
     )
     send, sums, weight = sums_call(plane, embed, keep)
     table = spread(send, DP)
-    partial = grads_call(mine[None], table, plane, embed, keep, sums, weight)
+    partial = grads_call(table, plane, embed, keep, sums, weight)
     summed, half = add_call(partial, lax.ppermute(partial, "core", SWAP))
     got = lax.ppermute(half, "yhi", SWAP)
     out, loss = backward(summed, got, kept, ln_gain, w_proj, w_out, w_query, w_key, w_value)

time: 170 us -> 133 us (0.78)
  local copies, waits for them, and re-layouts: 34.9 us -> 5.67 us
  waiting for transfers between devices: 28.1 us -> 14.4 us
  Pallas kernels: 33.4 us -> 39.9 us
    unnamed x96 -> x16, local copies, waits for them, and re-layouts: 34.4 us -> 4.48 us
    all_to_all x2, waiting for transfers between devices: 13.4 us -> 0.98 us  [spread(): return lax.all_to_all(x, axes, 0, 0)]
    ppermute x1, starting transfers between devices: 7.3 us -> 2.74 us  [body(): by_core = lax.ppermute(own, 'core', SWAP)]
    pallas_call x5, Pallas kernels: 31.5 us -> 34.3 us  [the longest x1 12.2 us: backward(): call(backward_kernel, (shape((ROWS, D), bf16), shape((8, E), f32)), [BLOC...]
    ppermute x1, waiting for transfers between devices: 8.7 us -> 6.34 us  [body(): by_yhi = lax.ppermute(own, 'yhi', SWAP)]
    all_to_all x2, starting transfers between devices: 18.6 us -> 20.9 us  [spread(): return lax.all_to_all(x, axes, 0, 0)]
    pallas_call x1, Pallas kernels: 1.84 us -> 3.84 us  [sums_call(): call(sums_kernel, (shape((DOCS, QSET), f32), shape((QLEN, E), f32), shape...]
  transfers between devices with their start and end apart: 7 -> 7, of which waited for: 4 -> 6; matrix products, arithmetic and copies ran while one was open for 0% -> 0% of each run, Pallas kernels for 10% -> 8%
where the time goes in v3:
time: 133 us; the launch traced here: 132 us
  starting transfers between devices  40.9 us (31%)
  Pallas kernels  39.9 us (30%)
  blocking collectives  29.7 us (22%)
  waiting for transfers between devices  14.4 us (11%)
  local copies, waits for them, and re-layouts  5.67 us (4%)
  between operations  2.01 us (2%)
    all_to_all x1, blocking collectives, spread(): return lax.all_to_all(x, axes, 0, 0)  29.7 us
    all_to_all x2, starting transfers between devices, spread(): return lax.all_to_all(x, axes, 0, 0)  20.9 us
    pallas_call x1, Pallas kernels, backward(): call(backward_kernel, (shape((ROWS, D), bf16), shape((8, E), f32)), [BLOC...  12.2 us
    pallas_call x1, Pallas kernels, forward(): call(forward_kernel, outs, [SMEM] + [ANY] * 10, tuple((ANY for _ in outs)...  10.9 us
    pallas_call x1, Pallas kernels, grads_call(): call(grads_kernel, shape((L + 8, E), f32), [BLOCK] * 6, flops=2 * 10 ** 9)  7.37 us
    ppermute x1, waiting for transfers between devices, body(): by_yhi = lax.ppermute(own, 'yhi', SWAP)  6.34 us
    ppermute x1, starting transfers between devices, body(): by_yhi = lax.ppermute(own, 'yhi', SWAP)  4.82 us
    ppermute x1, starting transfers between devices, body(): got = lax.ppermute(half, 'yhi', SWAP)  4.52 us
  transfers between devices with their start and end apart: 7, of which 6 were waited for; matrix products, arithmetic and copies ran while one was open for 0% of the time, Pallas kernels for 8%

profile of v3, /device:TPU:1, one launch (start us, length us, event | category | flops | bytes accessed | tf_op | source)
XLA Modules:
  0.0 132.5 jit_solution(3721692861140885884)
XLA Ops:
  1.3 1.8 %shard_map.131 = (bf16[16,48,128]{2,1,0:T(8,128)(2,1)}, bf16[144,1024]{1,0:T(8,128)(2,1)}) custom-call(s32[1]{0:T(128)S(6)} %copy.16.pos_ref, bf16[32,128]{1,0:T(8,128)(2,1)} %bitcast.10, bf16[1,32]{1,0:T(2,128)(2,1)} %mask_ref.1, bf16[128,1024]{1,0:T(8,128)(2,1)} %hidden_ref.1, s32[1,128]{1,0:T(1,128)} %bitcast.13), custom_call_target="tpu_custom_call" | custom-call | bytes 4194304 | tf_op jit(solution)/shard_map/pallas_call | solution.py:106
  3.1 0.0 copy-start.5
  3.1 15.9 %all-to-all-start = ((bf16[16,48,128]{2,1,0:T(8,128)(2,1)}), bf16[16,48,128]{2,1,0:T(8,128)(2,1)S(1)}, u32[]{:S(2)}, u32[]{:S(2)}) async-start(bf16[16,48,128]{2,1,0:T(8,128)(2,1)} %get-tuple-element.22), calls=%async_computation | async-start | bytes 393216 | tf_op jit(solution)/shard_map/all_to_all | solution.py:543
  19.0 4.8 %collective-permute-start = (bf16[144,1024]{1,0:T(8,128)(2,1)}, bf16[144,1024]{1,0:T(8,128)(2,1)S(1)}, u32[]{:S(2)}, u32[]{:S(2)}) collective-permute-start(bf16[144,1024]{1,0:T(8,128)(2,1)} %get-tuple-element.23.x0_any), channel_id=1, source_target_pairs={{0,2},{2,0},{1,3},{3,1},{4,6},{6,4},{5,7},{7,5},{8,10},{10,8},{9,1... | collective-permute-start | bytes 884744 | tf_op jit(solution)/shard_map/ppermute | solution.py:562
  23.8 6.3 %collective-permute-done.x2_any = bf16[144,1024]{1,0:T(8,128)(2,1)S(1)} collective-permute-done((bf16[144,1024]{1,0:T(8,128)(2,1)}, bf16[144,1024]{1,0:T(8,128)(2,1)S(1)}, u32[]{:S(2)}, u32[]{:S(2)}) %collective-permute-start) | collective-permute-done | bytes 294944 | tf_op jit(solution)/shard_map/ppermute | solution.py:562
  30.1 0.0 copy-start.6
  30.1 3.8 %collective-permute-start.1 = (bf16[144,1024]{1,0:T(8,128)(2,1)S(1)}, bf16[144,1024]{1,0:T(8,128)(2,1)S(1)}, u32[]{:S(2)}, u32[]{:S(2)}) collective-permute-start(bf16[144,1024]{1,0:T(8,128)(2,1)S(1)} %collective-permute-done.x2_any), channel_id=1, source_target_pairs={{0,1},{1,0},{2,3},{3,2},{4,5},{5,4},{6,7},{7,6},{8,9},{9,8},{10,11... | collective-permute-start | bytes 884744 | tf_op jit(solution)/shard_map/ppermute | solution.py:564
  33.9 1.2 collective-permute-done.1.after_ref.x3_any
  35.1 0.0 copy-start.2
  35.1 0.0 all-to-all-done.line_ref
  35.1 0.7 copy-done.2
  35.8 0.0 copy-start.1
  35.8 0.7 copy-done.1
  36.5 2.1 %shard_map.132 = bf16[8,544,128]{2,1,0:T(8,128)(2,1)} custom-call(bf16[16,48,128]{2,1,0:T(8,128)(2,1)} %copy-done.1, bf16[144,1024]{1,0:T(8,128)(2,1)} %copy-done.2), custom_call_target="tpu_custom_call" | custom-call | bytes 4194304 | tf_op jit(solution)/shard_map/pallas_call | solution.py:126
  38.5 5.0 %all-to-all-start.1 = ((bf16[8,544,128]{2,1,0:T(8,128)(2,1)}), bf16[8,544,128]{2,1,0:T(8,128)(2,1)S(1)}, u32[]{:S(2)}, u32[]{:S(2)}) async-start(bf16[8,544,128]{2,1,0:T(8,128)(2,1)} %shard_map.132), calls=%async_computation.1 | async-start | bytes 2228224 | tf_op jit(solution)/shard_map/all_to_all | solution.py:543
  43.6 0.0 copy-done.5
  43.6 2.7 %collective-permute-start.2 = (bf16[144,1024]{1,0:T(8,128)(2,1)S(1)}, bf16[144,1024]{1,0:T(8,128)(2,1)S(1)}, u32[]{:S(2)}, u32[]{:S(2)}) collective-permute-start(bf16[144,1024]{1,0:T(8,128)(2,1)S(1)} %copy-done.5), channel_id=1, source_target_pairs={{0,1},{1,0},{2,3},{3,2},{4,5},{5,4},{6,7},{7,6},{8,9},{9,8},{10,11... | collective-permute-start | bytes 884744 | tf_op jit(solution)/shard_map/ppermute | solution.py:561
  47.0 0.5 collective-permute-done.2.x1_any
  47.5 0.0 copy-start.7
  47.5 0.0 copy-done.6
  47.5 0.7 copy-done.7
  48.3 10.9 %shard_map.133 = (bf16[512,512]{1,0:T(8,128)(2,1)}, bf16[512,512]{1,0:T(8,128)(2,1)}, bf16[512,512]{1,0:T(8,128)(2,1)}, bf16[512,512]{1,0:T(8,128)(2,1)}, f32[8,...) custom-call(s32[1]{0:T(128)S(6)} %copy.15.length_ref, ...), custom_call_target="tpu_custom_call" | custom-call | flops 4000000000 | bytes 4194304 | tf_op jit(solution)/shard_map/pallas_call | solution.py:298
  59.1 1.0 all-to-all-done.1.plane_ref
  60.1 0.0 copy-start
  60.1 1.0 copy-done
  61.1 3.8 %shard_map.134 = (f32[128,128]{1,0:T(8,128)}, f32[32,128]{1,0:T(8,128)}, f32[32,128]{1,0:T(8,128)}) custom-call(bf16[8,544,128]{2,1,0:T(8,128)(2,1)} %copy-done, bf16[512,128]{1,0:T(8,128)(2,1)} %get-tuple-element.24.embed_ref, f32[512,128]{1,0:T(8,128)} %get-tuple-element.25.keep_ref), custom_call_target="tpu_custom_call" | custom-call | flops 1000000000 | bytes 4194304 | tf_op jit(solution)/shard_map/pallas_call | solution.py:334
  65.0 29.7 %all_to_all.21 = f32[128,1,128]{2,1,0:T(1,128)} all-to-all(f32[128,1,128]{2,1,0:T(1,128)} %bitcast.9), channel_id=1, replica_groups=mesh['z'=16,'ylo'=2,'x'=4,'yhi'=2,'core'=2] {'z','ylo','x'}, dimensions={0} | all-to-all | bytes 131072 | tf_op jit(solution)/shard_map/all_to_all | solution.py:543
  94.6 7.4 %shard_map.135.own_ref = f32[520,128]{1,0:T(8,128)} custom-call(f32[128,128]{1,0:T(8,128)} %bitcast.8, bf16[8,544,128]{2,1,0:T(8,128)(2,1)} %copy-done, bf16[512,128]{1,0:T(8,128)(2,1)} %get-tuple-element.24.embed_ref, f32[512,128]{1,0:T(8,128)} %get-tuple-element.25.keep_ref, f32[32,128]{1,0:T(8,128)} %get-tuple-element.27.sums_ref, ...), custom_call_target="tpu_custom_call" | custom-call | flops 2000000000 | bytes 4194304 | tf_op jit(solution)/shard_map/pallas_call | solution.py:373
  102.0 4.1 %collective-permute-start.3 = (f32[520,128]{1,0:T(8,128)}, f32[520,128]{1,0:T(8,128)S(1)}, u32[]{:S(2)}, u32[]{:S(2)}) collective-permute-start(f32[520,128]{1,0:T(8,128)} %shard_map.135.own_ref), channel_id=1, source_target_pairs={{0,1},{1,0},{2,3},{3,2},{4,5},{5,4},{6,7},{7,6},{8,9},{9,8},{10,11... | collective-permute-start | bytes 798728 | tf_op jit(solution)/shard_map/ppermute | solution.py:572
  106.1 1.4 %collective-permute-done.3.got_ref = f32[520,128]{1,0:T(8,128)S(1)} collective-permute-done((f32[520,128]{1,0:T(8,128)}, f32[520,128]{1,0:T(8,128)S(1)}, u32[]{:S(2)}, u32[]{:S(2)}) %collective-permute-start.3) | collective-permute-done | bytes 266272 | tf_op jit(solution)/shard_map/ppermute | solution.py:572
  107.5 0.0 copy-start.3
  107.5 0.7 copy-done.3
  108.2 1.8 %shard_map.136 = (f32[520,128]{1,0:T(8,128)}, bf16[544,128]{1,0:T(8,128)(2,1)}) custom-call(f32[520,128]{1,0:T(8,128)} %shard_map.135.own_ref, f32[520,128]{1,0:T(8,128)} %copy-done.3), custom_call_target="tpu_custom_call" | custom-call | bytes 4194304 | tf_op jit(solution)/shard_map/pallas_call | solution.py:395
  110.0 4.5 %collective-permute-start.4 = (bf16[544,128]{1,0:T(8,128)(2,1)}, bf16[544,128]{1,0:T(8,128)(2,1)S(1)}, u32[]{:S(2)}, u32[]{:S(2)}) collective-permute-start(bf16[544,128]{1,0:T(8,128)(2,1)} %get-tuple-element.30), channel_id=1, source_target_pairs={{0,2},{2,0},{1,3},{3,1},{4,6},{6,4},{5,7},{7,5},{8,10},{10,8},{9,1... | collective-permute-start | bytes 417800 | tf_op jit(solution)/shard_map/ppermute | solution.py:573
  114.5 4.0 %collective-permute-done.4.got_ref = bf16[544,128]{1,0:T(8,128)(2,1)S(1)} collective-permute-done((bf16[544,128]{1,0:T(8,128)(2,1)}, bf16[544,128]{1,0:T(8,128)(2,1)S(1)}, u32[]{:S(2)}, u32[]{:S(2)}) %collective-permute-start.4) | collective-permute-done | bytes 139296 | tf_op jit(solution)/shard_map/ppermute | solution.py:573
  118.4 0.0 copy-start.4
  118.4 0.7 copy-done.4
  119.1 12.2 %shard_map.137 = (bf16[128,1024]{1,0:T(8,128)(2,1)}, f32[8,128]{1,0:T(8,128)}) custom-call(f32[520,128]{1,0:T(8,128)} %get-tuple-element.29.sum_ref, bf16[544,128]{1,0:T(8,128)(2,1)} %copy-done.4, f32[512,128]{1,0:T(8,128)} %get-tuple-element.31.proj_ref, bf16[1024,128]{1,0:T(8,128)(2,1)} %wp_ref.1, f32[512,128]{1,0:T(8,128)} %get-tuple-element.32.inv_ref, ...), custom_call_target="tpu_custom_call" | custom-call | flops 3000000000 | bytes 4194304 | tf_op jit(solution)/shard_map/pallas_call | solution.py:524
  131.3 1.2 slice.3
Async XLA Ops:
  3.1 40.5 %copy-start.5 = (bf16[144,1024]{1,0:T(8,128)(2,1)S(1)}, bf16[144,1024]{1,0:T(8,128)(2,1)}, u32[]{:S(2)}) copy-start(bf16[144,1024]{1,0:T(8,128)(2,1)} %get-tuple-element.23.x0_any) | copy-start | bytes 884740
  3.1 32.0 %all-to-all-start = ((bf16[16,48,128]{2,1,0:T(8,128)(2,1)}), bf16[16,48,128]{2,1,0:T(8,128)(2,1)S(1)}, u32[]{:S(2)}, u32[]{:S(2)}) async-start(bf16[16,48,128]{2,1,0:T(8,128)(2,1)} %get-tuple-element.22), calls=%async_computation | async-start | bytes 393216 | tf_op jit(solution)/shard_map/all_to_all | solution.py:543
  19.0 11.2 %collective-permute-start = (bf16[144,1024]{1,0:T(8,128)(2,1)}, bf16[144,1024]{1,0:T(8,128)(2,1)S(1)}, u32[]{:S(2)}, u32[]{:S(2)}) collective-permute-start(bf16[144,1024]{1,0:T(8,128)(2,1)} %get-tuple-element.23.x0_any), channel_id=1, source_target_pairs={{0,2},{2,0},{1,3},{3,1},{4,6},{6,4},{5,7},{7,5},{8,10},{10,8},{9,1... | collective-permute-start | bytes 884744 | tf_op jit(solution)/shard_map/ppermute | solution.py:562
  30.1 17.4 %copy-start.6 = (bf16[144,1024]{1,0:T(8,128)(2,1)}, bf16[144,1024]{1,0:T(8,128)(2,1)S(1)}, u32[]{:S(2)}) copy-start(bf16[144,1024]{1,0:T(8,128)(2,1)S(1)} %collective-permute-done.x2_any) | copy-start | bytes 884740
  30.1 5.0 %collective-permute-start.1 = (bf16[144,1024]{1,0:T(8,128)(2,1)S(1)}, bf16[144,1024]{1,0:T(8,128)(2,1)S(1)}, u32[]{:S(2)}, u32[]{:S(2)}) collective-permute-start(bf16[144,1024]{1,0:T(8,128)(2,1)S(1)} %collective-permute-done.x2_any), channel_id=1, source_target_pairs={{0,1},{1,0},{2,3},{3,2},{4,5},{5,4},{6,7},{7,6},{8,9},{9,8},{10,11... | collective-permute-start | bytes 884744 | tf_op jit(solution)/shard_map/ppermute | solution.py:564
  35.1 0.7 copy-start.2
  35.8 0.7 copy-start.1
  38.5 21.6 %all-to-all-start.1 = ((bf16[8,544,128]{2,1,0:T(8,128)(2,1)}), bf16[8,544,128]{2,1,0:T(8,128)(2,1)S(1)}, u32[]{:S(2)}, u32[]{:S(2)}) async-start(bf16[8,544,128]{2,1,0:T(8,128)(2,1)} %shard_map.132), calls=%async_computation.1 | async-start | bytes 2228224 | tf_op jit(solution)/shard_map/all_to_all | solution.py:543
  43.6 3.9 %collective-permute-start.2 = (bf16[144,1024]{1,0:T(8,128)(2,1)S(1)}, bf16[144,1024]{1,0:T(8,128)(2,1)S(1)}, u32[]{:S(2)}, u32[]{:S(2)}) collective-permute-start(bf16[144,1024]{1,0:T(8,128)(2,1)S(1)} %copy-done.5), channel_id=1, source_target_pairs={{0,1},{1,0},{2,3},{3,2},{4,5},{5,4},{6,7},{7,6},{8,9},{9,8},{10,11... | collective-permute-start | bytes 884744 | tf_op jit(solution)/shard_map/ppermute | solution.py:561
  47.5 0.7 copy-start.7
  60.1 1.0 copy-start
  102.0 5.5 %collective-permute-start.3 = (f32[520,128]{1,0:T(8,128)}, f32[520,128]{1,0:T(8,128)S(1)}, u32[]{:S(2)}, u32[]{:S(2)}) collective-permute-start(f32[520,128]{1,0:T(8,128)} %shard_map.135.own_ref), channel_id=1, source_target_pairs={{0,1},{1,0},{2,3},{3,2},{4,5},{5,4},{6,7},{7,6},{8,9},{9,8},{10,11... | collective-permute-start | bytes 798728 | tf_op jit(solution)/shard_map/ppermute | solution.py:572
  107.5 0.7 copy-start.3
  110.0 8.5 %collective-permute-start.4 = (bf16[544,128]{1,0:T(8,128)(2,1)}, bf16[544,128]{1,0:T(8,128)(2,1)S(1)}, u32[]{:S(2)}, u32[]{:S(2)}) collective-permute-start(bf16[544,128]{1,0:T(8,128)(2,1)} %get-tuple-element.30), channel_id=1, source_target_pairs={{0,2},{2,0},{1,3},{3,1},{4,6},{6,4},{5,7},{7,5},{8,10},{10,8},{9,1... | collective-permute-start | bytes 417800 | tf_op jit(solution)/shard_map/ppermute | solution.py:573
  118.4 0.7 copy-start.4

commit v4 on v3

v4 whole, which is shorter than its diff:
```python
import jax
import jax.numpy as jnp
import numpy as np
from jax import lax
from jax.experimental import pallas as pl
from jax.experimental.pallas import tpu as pltpu
from jax.sharding import Mesh, PartitionSpec as P

D = 1024
HEADS = 8
HD = 64
E = 128
QLEN = 32
L = 512
ROWS = 128
DOCS = 128
QSET = 128
AUX = 16
TAU = 0.05
GRAD_SCALE = 1024.0
NEG = -1e30
AXES = ("z", "ylo", "x", "yhi", "core")
SIZES = (16, 2, 4, 2, 2)
DP = ("z", "ylo", "x")
LINE = 16
PLANE = 8
CHUNK = LINE * QLEN
STRIP = 64
THIN = 32
MARKS_FLOPS = 3 * 10**9
LOG2E = 1.4426950408889634
SWAP = [(0, 1), (1, 0)]
bf16 = jnp.bfloat16
f32 = jnp.float32
i32 = jnp.int32
BLOCK = pl.BlockSpec()
VMEM = pl.BlockSpec(memory_space=pltpu.VMEM)
ANY = pl.BlockSpec(memory_space=pl.ANY)
HBM = pl.BlockSpec(memory_space=pltpu.MemorySpace.HBM)
SMEM = pl.BlockSpec(memory_space=pltpu.SMEM)
NN = (((1,), (0,)), ((), ()))
NT = (((1,), (1,)), ((), ()))
TN = (((0,), (0,)), ((), ()))


def dot(left, right, dims=NN):
    return lax.dot_general(left, right, dims, preferred_element_type=f32)


def iota(shape, dim):
    return lax.broadcasted_iota(i32, shape, dim)


def select(x, choice):
    choice = choice.astype(bf16)
    high = x.astype(bf16)
    rest = x - high.astype(f32)
    middle = rest.astype(bf16)
    low = (rest - middle.astype(f32)).astype(bf16)
    return dot(high, choice) + (dot(middle, choice) + dot(low, choice))


def position():
    return lax.axis_index("yhi") * 2 + lax.axis_index("core"), lax.axis_index(DP)


def call(kernel, outs, ins, out_specs=None, scratch=(), flops=0, limit=12):
    return pl.pallas_call(
        kernel,
        out_shape=outs,
        in_specs=ins,
        out_specs=jax.tree.map(lambda _: BLOCK, outs) if out_specs is None else out_specs,
        scratch_shapes=list(scratch),
        compiler_params=pltpu.CompilerParams(vmem_limit_bytes=limit * 2**20),
        cost_estimate=pl.CostEstimate(flops=flops, bytes_accessed=4 * 2**20, transcendentals=0),
    )


class Moves:
    def __init__(self, sems):
        self.sems, self.used = sems, 0

    def start(self, source, target):
        copy = pltpu.make_async_copy(source, target, self.sems.at[self.used])
        self.used += 1
        copy.start()
        return copy


def shape(dims, kind):
    return jax.ShapeDtypeStruct(dims, kind)


def pack_hidden_kernel(hidden_ref, skip_ref, own_out):
    own_out[:ROWS, :] = hidden_ref[...]
    own_out[ROWS:, :] = jnp.zeros((AUX, D), bf16)
    own_out[ROWS:, :ROWS] = jnp.broadcast_to(skip_ref[...], (AUX, ROWS)).astype(f32).astype(bf16)


def pack_hidden(hidden, doc_keep):
    return call(pack_hidden_kernel, shape((ROWS + AUX, D), bf16), [BLOCK] * 2, limit=56)(
        hidden, doc_keep[None]
    )


def pack_query_kernel(pos_ref, queries_ref, mask_ref, after_ref, query_out):
    q = queries_ref[...].astype(f32)
    qn = (q * lax.rsqrt(jnp.sum(q * q, -1, keepdims=True) + 1e-06)).astype(bf16)
    repeat = (iota((QLEN, E), 1) % QLEN == iota((QLEN, E), 0)).astype(bf16)
    weights = dot(jnp.broadcast_to(mask_ref[...], (AUX, QLEN)), repeat)
    target = pos_ref[0].astype(f32)
    row = iota((AUX, E), 0)
    aux = jnp.where(row == 0, weights, jnp.where(row == 1, target, 0.0)).astype(bf16)
    for z in range(LINE):
        query_out[z, :QLEN, :] = qn
        query_out[z, QLEN:, :] = aux


def pack_query(positive, queries, query_mask, after):
    return call(
        pack_query_kernel,
        shape((LINE, QLEN + AUX, E), bf16),
        [SMEM, BLOCK, BLOCK, ANY],
        limit=56,
    )(positive, queries[0], query_mask, after)


def repack_kernel(line_ref, after_ref, out_ref):
    aux = line_ref[:, QLEN:, :].astype(f32)
    weights = aux[:, 0, :].astype(bf16)
    target = aux[:, 1, :].astype(bf16)
    for p in range(PLANE):
        for z in range(LINE):
            out_ref[p, z * QLEN : (z + 1) * QLEN, :] = line_ref[z, :QLEN, :]
        out_ref[p, CHUNK : CHUNK + LINE, :] = weights
        out_ref[p, CHUNK + LINE :, :] = target


def repack(line, after):
    out = shape((PLANE, CHUNK + 2 * LINE, E), bf16)
    return call(repack_kernel, out, [BLOCK, ANY])(line, after)


def marks_kernel(length_ref, x0_any, x1_any, x2_any, x3_any, keep_ref, bias_ref, skip_ref, sems):
    moves = Moves(sems)
    skips = [
        moves.start(source.at[pl.ds(ROWS, AUX), pl.ds(0, ROWS)], skip_ref.at[b])
        for b, source in enumerate((x0_any, x1_any, x2_any, x3_any))
    ]
    length = length_ref[0]
    me, _ = position()
    for b in range(4):
        skips[b].wait()
        start = jnp.bitwise_xor(me, b) * ROWS
        skip = skip_ref[b].astype(f32)[0:1, :]
        place = start + iota((1, ROWS), 1)
        valid = place < length
        bias = jnp.where(valid, 0.0, NEG)
        bias_ref[:, b * ROWS : (b + 1) * ROWS] = jnp.broadcast_to(bias, (8, ROWS))
        kept = jnp.where(valid & ((skip == 1.0) | (place == 0)), 1.0, 0.0)
        diagonal = iota((ROWS, ROWS), 0) == iota((ROWS, ROWS), 1)
        column = jnp.sum(jnp.where(diagonal, kept, 0.0), -1, keepdims=True)
        keep_ref[b * ROWS : (b + 1) * ROWS, :] = jnp.broadcast_to(column, (ROWS, E)).astype(bf16)


def marks_call(doc_len, blocks):
    return call(
        marks_kernel,
        (shape((L, E), bf16), shape((8, L), f32)),
        [SMEM] + [ANY] * 4,
        scratch=[pltpu.VMEM((4, AUX, ROWS), bf16), pltpu.SemaphoreType.DMA((4,))],
        flops=MARKS_FLOPS,
        limit=4,
    )(doc_len, *blocks)


def forward_kernel(
    keep_any,
    bias_any,
    x0_any,
    x1_any,
    x2_any,
    x3_any,
    wq_any,
    wk_any,
    wv_any,
    wo_any,
    gain_any,
    wp_any,
    q_any,
    k_any,
    v_any,
    att_any,
    prow_any,
    pcol_any,
    unit_any,
    inv_any,
    proj_any,
    embed_any,
    x_ref,
    bias_ref,
    wq_ref,
    wk_ref,
    wv_ref,
    wo_ref,
    gain_ref,
    wp_ref,
    q_ref,
    k_ref,
    v_ref,
    att_ref,
    prow_ref,
    pcol_ref,
    unit_ref,
    inv_ref,
    proj_ref,
    embed_ref,
    score_ref,
    prob_ref,
    sems,
):
    moves = Moves(sems)
    blocks = [
        moves.start(source.at[pl.ds(0, ROWS)], x_ref.at[pl.ds(b * ROWS, ROWS)])
        for b, source in enumerate((x0_any, x1_any, x2_any, x3_any))
    ]
    at_k = moves.start(wk_any, wk_ref)
    at_keep = moves.start(keep_any, embed_ref.at[pl.ds(L, L)])
    at_bias = moves.start(bias_any, bias_ref)
    at_q = moves.start(wq_any, wq_ref)
    at_v = moves.start(wv_any, wv_ref)
    at_o = moves.start(wo_any, wo_ref)
    at_gain = moves.start(gain_any, gain_ref)
    at_p = moves.start(wp_any, wp_ref)
    ends = []
    for copy in blocks:
        copy.wait()
    at_k.wait()
    k_ref[...] = dot(x_ref[...], wk_ref[...]).astype(bf16)
    ends.append(moves.start(k_ref, k_any))
    at_q.wait()
    q_ref[...] = dot(x_ref[...], wq_ref[...]).astype(bf16)
    ends.append(moves.start(q_ref, q_any))
    at_v.wait()
    v_ref[...] = dot(x_ref[...], wv_ref[...]).astype(bf16)
    ends.append(moves.start(v_ref, v_any))
    at_keep.wait()
    at_bias.wait()
    bias = bias_ref[0:1, :]
    first = iota((L, 2 * HD), 1) < HD
    for pair in range(HEADS // 2):
        lanes = slice(pair * 2 * HD, (pair + 1) * 2 * HD)
        qp = q_ref[:, lanes] * jnp.array(HD**-0.5, bf16)
        mixes = []
        for half in range(2):
            head = 2 * pair + half
            own = first if half == 0 else ~first
            score_ref[half] = dot(jnp.where(own, qp, jnp.zeros_like(qp)), k_ref[:, lanes], NT)
            for c in range(L // STRIP):
                rows = slice(c * STRIP, (c + 1) * STRIP)
                scores = score_ref[half, rows, :] + bias
                expo = jnp.exp(scores - jnp.max(scores, -1, keepdims=True))
                probs = expo * (1.0 / jnp.sum(expo, -1, keepdims=True))
                prob_ref[half, rows, :] = probs.astype(bf16)
            prow_ref[head] = prob_ref[half, :ROWS, :]
            pcol_ref[head] = jnp.transpose(prob_ref[half, :, :ROWS])
            mixes.append(dot(prob_ref[half], v_ref[:, lanes]))
        att_ref[:, lanes] = jnp.where(first, mixes[0], mixes[1]).astype(bf16)
        two = pl.ds(2 * pair, 2)
        ends.append(moves.start(prow_ref.at[two], prow_any.at[two]))
        ends.append(moves.start(pcol_ref.at[two], pcol_any.at[two]))
    ends.append(moves.start(att_ref, att_any))
    at_o.wait()
    unit_ref[...] = dot(att_ref[...], wo_ref[...])
    at_gain.wait()
    for c in range(L // THIN):
        rows = slice(c * THIN, (c + 1) * THIN)
        mixed = x_ref[rows, :].astype(f32) + unit_ref[rows, :]
        centred = mixed - jnp.mean(mixed, -1, keepdims=True)
        inv = lax.rsqrt(jnp.mean(centred * centred, -1, keepdims=True) + 1e-05)
        unit = centred * inv
        unit_ref[rows, :] = unit
        inv_ref[rows, :] = jnp.broadcast_to(inv, (THIN, E))
        x_ref[rows, :] = (unit * gain_ref[...]).astype(bf16)
    ends.append(moves.start(unit_ref, unit_any))
    ends.append(moves.start(inv_ref, inv_any))
    at_p.wait()
    proj = dot(x_ref[...], wp_ref[...])
    proj_ref[...] = proj
    ends.append(moves.start(proj_ref, proj_any))
    scale = lax.rsqrt(jnp.sum(proj * proj, -1, keepdims=True) + 1e-06)
    embed_ref[:L, :] = (proj * scale).astype(bf16)
    ends.append(moves.start(embed_ref, embed_any))
    for copy in ends:
        copy.wait()


def forward(keep, bias, blocks, w_query, w_key, w_value, w_out, ln_gain, w_proj):
    width = HEADS * HD
    square = shape((L, width), bf16)
    outs = (
        square,
        square,
        square,
        square,
        shape((HEADS, ROWS, L), bf16),
        shape((HEADS, ROWS, L), bf16),
        shape((L, D), f32),
        shape((L, E), f32),
        shape((L, E), f32),
        shape((2 * L, E), bf16),
    )
    ins = [
        pltpu.VMEM((L, D), bf16),
        pltpu.VMEM((8, L), f32),
        pltpu.VMEM((D, width), bf16),
        pltpu.VMEM((D, width), bf16),
        pltpu.VMEM((D, width), bf16),
        pltpu.VMEM((width, D), bf16),
        pltpu.VMEM((1, D), f32),
        pltpu.VMEM((D, E), bf16),
    ]
    work = [
        pltpu.VMEM((2, L, L), f32),
        pltpu.VMEM((2, L, L), bf16),
        pltpu.SemaphoreType.DMA((32,)),
    ]
    return call(
        forward_kernel,
        outs,
        [ANY] * 6 + [HBM] * 6,
        tuple(HBM for _ in outs),
        ins + [pltpu.VMEM(o.shape, o.dtype) for o in outs] + work,
        flops=4 * 10**9,
        limit=56,
    )(keep, bias, *blocks, w_query, w_key, w_value, w_out, ln_gain[None], w_proj)


def sums_kernel(plane_ref, embed_ref, send_ref, sums_ref, weight_ref, keep_ref):
    keep_ref[...] = embed_ref[L:, :].astype(f32)
    for c in range(PLANE):
        total = jnp.zeros((8, CHUNK), f32)
        for b in range(4):
            rows = slice(b * ROWS, (b + 1) * ROWS)
            close = dot(embed_ref[rows, :], plane_ref[c, :CHUNK, :], NT)
            near = jnp.exp2(close * (LOG2E / TAU)) * keep_ref[rows, 0:1]
            total += jnp.sum(near.reshape(ROWS // 8, 8, CHUNK), 0)
        total = jnp.sum(total, 0, keepdims=True)
        for j in range(4):
            sums_ref[4 * c + j : 4 * c + j + 1, :] = total[:, j * E : (j + 1) * E]
    weights = jnp.concatenate([plane_ref[c, CHUNK : CHUNK + LINE, :] for c in range(PLANE)], 0)
    row, col = iota((QLEN, QSET), 0), iota((QLEN, QSET), 1)
    weight = jnp.zeros((QLEN, E), f32)
    for g in range(4):
        picked = dot((col == 4 * row + g).astype(bf16), weights)
        weight = jnp.where(col // QLEN == g, picked, weight)
    weight_ref[...] = weight
    parts = weight * TAU * jnp.log(sums_ref[...])
    source, place = iota((E, QSET), 0), iota((E, QSET), 1)
    table = select(parts, source // QLEN == place % 4)
    table = jnp.sum(jnp.where(col // 4 == row, table, 0.0), 0, keepdims=True)
    send_ref[...] = jnp.broadcast_to(table, (DOCS, QSET))


def sums_call(plane, embed):
    return call(
        sums_kernel,
        (shape((DOCS, QSET), f32), shape((QLEN, E), f32), shape((QLEN, E), f32)),
        [VMEM] * 2,
        (VMEM, VMEM, VMEM),
        [pltpu.VMEM((L, E), f32)],
        flops=10**9,
    )(plane, embed)


def grads_kernel(
    table_ref, sums_ref, weight_ref, plane_ref, embed_ref, out_ref, score_ref, couple_ref
):
    _, mine = position()
    table = table_ref[...]
    lse = jnp.log(jnp.sum(jnp.exp(table), 0, keepdims=True))
    targets = jnp.concatenate(
        [plane_ref[c, CHUNK + LINE :, :] for c in range(PLANE)], 0
    ).astype(f32)
    row, col = iota((QSET, QSET), 0), iota((QSET, QSET), 1)
    target = jnp.sum(jnp.where(row == col, targets, 0.0), 0, keepdims=True).astype(i32)
    hit = row == target
    gap = lse - jnp.sum(jnp.where(hit, table, 0.0), 0, keepdims=True)
    loss = jnp.sum(gap, -1, keepdims=True)
    own = jnp.sum(jnp.where(row == mine, table, 0.0), 0, keepdims=True)
    dscore = GRAD_SCALE * (jnp.exp(own - lse) - jnp.where(target == mine, 1.0, 0.0))
    group = iota((QLEN, QSET), 1) // 4 == iota((QLEN, QSET), 0)
    wide = select(jnp.where(group, dscore, 0.0), row % 4 == col // QLEN)
    coef = wide * weight_ref[...] / sums_ref[...]
    for c in range(PLANE):
        queries = plane_ref[c, :CHUNK, :]
        score_ref[c % 2] = dot(embed_ref[:L, :], queries, NT)
        factor = jnp.concatenate([coef[4 * c + j : 4 * c + j + 1, :] for j in range(4)], 1)
        for b in range(L // STRIP):
            rows = slice(b * STRIP, (b + 1) * STRIP)
            near = jnp.exp2(score_ref[c % 2, rows, :] * (LOG2E / TAU))
            couple_ref[c % 2, rows, :] = (near * factor).astype(bf16)
        part = dot(couple_ref[c % 2], queries)
        if c == 0:
            out_ref[:L, :] = part
        else:
            out_ref[:L, :] += part
    out_ref[:L, :] = out_ref[:L, :] * embed_ref[L:, :].astype(f32)
    out_ref[L:, :] = jnp.broadcast_to(loss, (8, E))


def grads_call(table, plane, embed, sums, weight):
    return call(
        grads_kernel,
        shape((L + 8, E), f32),
        [VMEM] * 5,
        VMEM,
        [pltpu.VMEM((2, L, CHUNK), f32), pltpu.VMEM((2, L, CHUNK), bf16)],
        flops=2 * 10**9,
    )(table, sums, weight, plane, embed)


def add_kernel(own_ref, got_ref, sum_ref, send_ref):
    for b in range(4):
        rows = slice(b * ROWS, (b + 1) * ROWS)
        other = (b ^ 1) * ROWS
        total = own_ref[rows, :] + got_ref[other : other + ROWS, :]
        sum_ref[rows, :] = total
        send_ref[rows, :] = total.astype(bf16)
    loss = own_ref[L:, :] + got_ref[L:, :]
    sum_ref[L:, :] = loss
    high = loss.astype(bf16).astype(f32)
    middle = (loss - high).astype(bf16).astype(f32)
    low = loss - high - middle
    send_ref[L : L + 16, :] = jnp.concatenate([high, middle], 0).astype(bf16)
    send_ref[L + 16 :, :] = jnp.concatenate([low, low], 0).astype(bf16)


def add_call(own, got):
    return call(add_kernel, (shape((L + 8, E), f32), shape((L + 32, E), bf16)), [VMEM] * 2, (VMEM, VMEM), limit=4)(own, got)


def backward_kernel(
    sum_ref,
    got_ref,
    proj_ref,
    wp_ref,
    inv_ref,
    gain_ref,
    unit_ref,
    wo_ref,
    att_ref,
    v_ref,
    k_ref,
    q_ref,
    prow_ref,
    pcol_ref,
    wq_ref,
    wk_ref,
    wv_ref,
    out_ref,
    loss_ref,
    wide_ref,
    mixed_ref,
    ag_ref,
    qg_ref,
    kg_ref,
    vg_ref,
    delta_ref,
    inner_ref,
    score_ref,
):
    tail = got_ref[L:, :].astype(f32)
    loss = sum_ref[L:, :] + (tail[0:8] + tail[8:16] + tail[16:24])
    loss_ref[0] = loss[0, 0]
    got = got_ref[:L, :].astype(f32)
    grad = sum_ref[:L, :] + jnp.concatenate([got[2 * ROWS :], got[: 2 * ROWS]], 0)
    proj = proj_ref[...]
    scale = lax.rsqrt(jnp.sum(proj * proj, -1, keepdims=True) + 1e-06)
    embed = proj * scale
    proj_grad = ((grad - embed * jnp.sum(embed * grad, -1, keepdims=True)) * scale).astype(bf16)
    wide_ref[...] = dot(proj_grad, wp_ref[...], NT)
    for c in range(L // THIN):
        rows = slice(c * THIN, (c + 1) * THIN)
        gained = wide_ref[rows, :] * gain_ref[...]
        unit = unit_ref[rows, :]
        along = jnp.mean(gained * unit, -1, keepdims=True)
        mixed = inv_ref[rows, 0:1] * (gained - jnp.mean(gained, -1, keepdims=True) - unit * along)
        if (c + 1) * THIN <= ROWS:
            wide_ref[rows, :] = mixed
        mixed_ref[rows, :] = mixed.astype(bf16)
    ag_ref[...] = dot(mixed_ref[...], wo_ref[...], NT).astype(bf16)
    product = ag_ref[...].astype(f32) * att_ref[...].astype(f32)
    high = product.astype(bf16)
    low = (product - high.astype(f32)).astype(bf16)
    heads = (iota((HEADS * HD, E), 0) // HD == iota((HEADS * HD, E), 1)).astype(bf16)
    delta = dot(high, heads) + dot(low, heads)
    delta_ref[...] = jnp.transpose(delta)
    first = iota((ROWS, 2 * HD), 1) < HD

    def halves(t):
        none = jnp.zeros_like(t)
        return jnp.concatenate([jnp.where(first, t, none), jnp.where(first, none, t)], 0)

    def joined(t):
        return jnp.where(first, t[:ROWS], t[ROWS:]).astype(bf16)

    for pair in range(HEADS // 2):
        lanes = slice(pair * 2 * HD, (pair + 1) * 2 * HD)
        kp, qp, vp, agp = k_ref[:, lanes], q_ref[:, lanes], v_ref[:, lanes], ag_ref[:, lanes]
        inner_ref[0] = dot(halves(vp[:ROWS]), agp, NT)
        inner_ref[1] = dot(halves(agp[:ROWS]), vp, NT)
        for half in range(2):
            head = 2 * pair + half
            for c in range(ROWS // STRIP):
                rows = slice(c * STRIP, (c + 1) * STRIP)
                place = slice(half * ROWS + c * STRIP, half * ROWS + (c + 1) * STRIP)
                off = inner_ref[0, place, :] - delta_ref[head : head + 1, :]
                prob = pcol_ref[head, rows, :].astype(f32)
                score_ref[0, place, :] = (prob * (off * HD**-0.5)).astype(bf16)
                off = inner_ref[1, place, :] - delta[rows, head : head + 1]
                prob = prow_ref[head, rows, :].astype(f32)
                score_ref[1, place, :] = (prob * (off * HD**-0.5)).astype(bf16)
        two = slice(2 * pair, 2 * pair + 2)
        kg_ref[:, lanes] = joined(dot(score_ref[0], qp))
        qg_ref[:, lanes] = joined(dot(score_ref[1], kp))
        vg_ref[:, lanes] = joined(dot(pcol_ref[two].reshape(2 * ROWS, L), agp))
    total = wide_ref[:ROWS, :]
    total += dot(qg_ref[...], wq_ref[...], NT)
    total += dot(kg_ref[...], wk_ref[...], NT)
    total += dot(vg_ref[...], wv_ref[...], NT)
    out_ref[...] = total.astype(bf16)


def backward(summed, got, kept, ln_gain, w_proj, w_out, w_query, w_key, w_value):
    q, k, v, att, prow, pcol, unit, inv, proj = kept
    width = HEADS * HD
    moved = (unit, w_out, att, v, k, q, prow, pcol, w_query, w_key, w_value)
    return call(
        backward_kernel,
        (shape((ROWS, D), bf16), shape((1,), f32)),
        [VMEM] * (6 + len(moved)),
        (VMEM, SMEM),
        [
            pltpu.VMEM((L, D), f32),
            pltpu.VMEM((L, D), bf16),
            pltpu.VMEM((L, width), bf16),
            pltpu.VMEM((ROWS, width), bf16),
            pltpu.VMEM((ROWS, width), bf16),
            pltpu.VMEM((ROWS, width), bf16),
            pltpu.VMEM((E, L), f32),
            pltpu.VMEM((2, 2 * ROWS, L), f32),
            pltpu.VMEM((2, 2 * ROWS, L), bf16),
        ],
        flops=3 * 10**9,
        limit=12,
    )(summed, got, proj, w_proj, inv, ln_gain[None], *moved)


def spread(x, axes):
    return lax.all_to_all(x, axes, 0, 0)


def body(
    hidden,
    doc_len,
    doc_keep,
    w_query,
    w_key,
    w_value,
    w_out,
    ln_gain,
    w_proj,
    queries,
    query_mask,
    positive,
):
    own = pack_hidden(hidden, doc_keep)
    by_core = lax.ppermute(own, "core", SWAP)
    by_yhi = lax.ppermute(own, "yhi", SWAP)
    line = spread(pack_query(positive, queries, query_mask, by_core), "z")
    by_both = lax.ppermute(by_yhi, "core", SWAP)
    blocks = (own, by_core, by_yhi, by_both)
    keep, bias = marks_call(doc_len, blocks)
    plane = spread(repack(line, keep), ("ylo", "x"))
    *kept, embed = forward(
        keep, bias, blocks, w_query, w_key, w_value, w_out, ln_gain, w_proj
    )
    send, sums, weight = sums_call(plane, embed)
    table = spread(send, DP)
    partial = grads_call(table, plane, embed, sums, weight)
    summed, half = add_call(partial, lax.ppermute(partial, "core", SWAP))
    got = lax.ppermute(half, "yhi", SWAP)
    out, loss = backward(summed, got, kept, ln_gain, w_proj, w_out, w_query, w_key, w_value)
    return (out, loss[0])


def solution(mesh):
    fine = Mesh(np.asarray(mesh.devices).reshape(SIZES), AXES)
    placed = (
        P(AXES, None),
        P(DP),
        P(AXES),
        P(),
        P(),
        P(),
        P(),
        P(),
        P(),
        P(AXES, None, None),
        P(AXES, None),
        P(AXES),
    )
    return jax.shard_map(
        body, mesh=fine, in_specs=placed, out_specs=(P(AXES, None), P()), check_vma=False
    )
```

time: 133 us -> 113 us (0.85)
  Pallas kernels: 39.9 us -> 25.1 us
  blocking collectives: 29.7 us -> 25.3 us
  waiting for transfers between devices: 14.4 us -> 18.2 us
  starting transfers between devices: 40.9 us -> 37.4 us
  local copies, waits for them, and re-layouts: 5.67 us -> 3.98 us
    pallas_call x5 -> x7, Pallas kernels: 34 us -> 22.2 us  [the longest x1 10.8 us: forward(): call(forward_kernel, outs, [ANY] * 6 + [HBM] * 6, tuple((HBM for _ in out...]
    all_to_all x2, waiting for transfers between devices: 0.98 us -> 11.7 us  [spread(): return lax.all_to_all(x, axes, 0, 0)]
    ppermute x1, waiting for transfers between devices: 6.34 us -> 0.01 us  [body(): by_yhi = lax.ppermute(own, 'yhi', SWAP)]
    ppermute x1, starting transfers between devices: 2.74 us -> 8.77 us  [body(): by_core = lax.ppermute(own, 'core', SWAP)]
    all_to_all x1, blocking collectives: 29.7 us -> 25.3 us  [spread(): return lax.all_to_all(x, axes, 0, 0)]
    all_to_all x2, starting transfers between devices: 20.9 us -> 16.6 us  [spread(): return lax.all_to_all(x, axes, 0, 0)]
    ppermute x1, starting transfers between devices: 4.82 us -> 1.92 us  [body(): by_yhi = lax.ppermute(own, 'yhi', SWAP)]
    pallas_call x1, Pallas kernels: 3.84 us -> 1.74 us  [sums_call(): call(sums_kernel, (shape((DOCS, QSET), f32), shape((QLEN, E), f32), shape...]
  transfers between devices with their start and end apart: 7 -> 7, of which waited for: 6 -> 5; matrix products, arithmetic and copies ran while one was open for 0% -> 0% of each run, Pallas kernels for 8% -> 11%
where the time goes in v4:
time: 113 us; the launch traced here: 112 us
  starting transfers between devices  37.4 us (33%)
  blocking collectives  25.3 us (22%)
  Pallas kernels  25.1 us (22%)
  waiting for transfers between devices  18.2 us (16%)
  local copies, waits for them, and re-layouts  3.98 us (4%)
  between operations  2.39 us (2%)
    all_to_all x1, blocking collectives, spread(): return lax.all_to_all(x, axes, 0, 0)  25.3 us
    all_to_all x2, starting transfers between devices, spread(): return lax.all_to_all(x, axes, 0, 0)  16.6 us
    all_to_all x2, waiting for transfers between devices, spread(): return lax.all_to_all(x, axes, 0, 0)  11.7 us
    pallas_call x1, Pallas kernels, forward(): call(forward_kernel, outs, [ANY] * 6 + [HBM] * 6, tuple((HBM for _ in out...  10.8 us
    ppermute x1, starting transfers between devices, body(): by_core = lax.ppermute(own, 'core', SWAP)  8.77 us
    pallas_call x1, Pallas kernels, backward(): call(backward_kernel, (shape((ROWS, D), bf16), shape((1,), f32)), [VMEM]...  5.26 us
    ppermute x1, waiting for transfers between devices, body(): got = lax.ppermute(half, 'yhi', SWAP)  4.81 us
    ppermute x1, starting transfers between devices, body(): summed, half = add_call(partial, lax.ppermute(partial, 'core', SWAP))  4.21 us
  transfers between devices with their start and end apart: 7, of which 5 were waited for; matrix products, arithmetic and copies ran while one was open for 0% of the time, Pallas kernels for 11%

profile of v4, /device:TPU:1, one launch (start us, length us, event | category | flops | bytes accessed | tf_op | source)
XLA Modules:
  0.0 112.4 jit_solution(16233147480051604068)
XLA Ops:
  0.6 1.7 %shard_map.131.x0_any = bf16[144,1024]{1,0:T(8,128)(2,1)} custom-call(bf16[128,1024]{1,0:T(8,128)(2,1)} %hidden_ref.1, s32[1,128]{1,0:T(1,128)} %bitcast.13), custom_call_target="tpu_custom_call" | custom-call | bytes 4194304 | tf_op jit(solution)/shard_map/pallas_call | solution.py:101
  2.3 8.8 %collective-permute-start = (bf16[144,1024]{1,0:T(8,128)(2,1)}, bf16[144,1024]{1,0:T(8,128)(2,1)S(1)}, u32[]{:S(2)}, u32[]{:S(2)}) collective-permute-start(bf16[144,1024]{1,0:T(8,128)(2,1)} %shard_map.131.x0_any), channel_id=1, source_target_pairs={{0,1},{1,0},{2,3},{3,2},{4,5},{5,4},{6,7},{7,6},{8,9},{9,8},{10,11... | collective-permute-start | bytes 884744 | tf_op jit(solution)/shard_map/ppermute | solution.py:579
  11.1 1.9 %collective-permute-start.1 = (bf16[144,1024]{1,0:T(8,128)(2,1)}, bf16[144,1024]{1,0:T(8,128)(2,1)S(1)}, u32[]{:S(2)}, u32[]{:S(2)}) collective-permute-start(bf16[144,1024]{1,0:T(8,128)(2,1)} %shard_map.131.x0_any), channel_id=1, source_target_pairs={{0,2},{2,0},{1,3},{3,1},{4,6},{6,4},{5,7},{7,5},{8,10},{10,8},{9,1... | collective-permute-start | bytes 884744 | tf_op jit(solution)/shard_map/ppermute | solution.py:580
  13.7 0.0 collective-permute-done.after_ref.x1_any
  13.7 0.0 copy-start.12
  13.7 0.7 copy-done.12
  14.4 1.5 %shard_map.132 = bf16[16,48,128]{2,1,0:T(8,128)(2,1)} custom-call(s32[1]{0:T(128)S(6)} %copy.16.pos_ref, bf16[32,128]{1,0:T(8,128)(2,1)} %bitcast.12, bf16[1,32]{1,0:T(2,128)(2,1)} %mask_ref.1, bf16[144,1024]{1,0:T(8,128)(2,1)} %copy-done.12), custom_call_target="tpu_custom_call" | custom-call | bytes 4194304 | tf_op jit(solution)/shard_map/pallas_call | solution.py:120
  15.9 12.4 %all-to-all-start = ((bf16[16,48,128]{2,1,0:T(8,128)(2,1)}), bf16[16,48,128]{2,1,0:T(8,128)(2,1)S(1)}, u32[]{:S(2)}, u32[]{:S(2)}) async-start(bf16[16,48,128]{2,1,0:T(8,128)(2,1)} %shard_map.132), calls=%async_computation | async-start | bytes 393216 | tf_op jit(solution)/shard_map/all_to_all | solution.py:561
  28.4 0.0 collective-permute-done.1.x2_any
  28.4 0.0 copy-start.19
  28.4 2.5 %collective-permute-start.2 = (bf16[144,1024]{1,0:T(8,128)(2,1)S(1)}, bf16[144,1024]{1,0:T(8,128)(2,1)S(1)}, u32[]{:S(2)}, u32[]{:S(2)}) collective-permute-start(bf16[144,1024]{1,0:T(8,128)(2,1)S(1)} %collective-permute-done.1.x2_any), channel_id=1, source_target_pairs={{0,1},{1,0},{2,3},{3,2},{4,5},{5,4},{6,7},{7,6},{8,9},{9,8},{10,11... | collective-permute-start | bytes 884744 | tf_op jit(solution)/shard_map/ppermute | solution.py:582
  31.5 0.5 collective-permute-done.2.x3_any
  32.1 0.0 copy-start.11
  32.1 1.0 copy-done.11
  33.0 0.0 copy-start.13
  33.0 1.0 copy-done.13
  34.0 0.0 copy-start.20
  34.0 0.4 shard_map.133
  34.4 0.0 copy-done.19
  34.5 0.3 copy-done.20
  34.7 0.0 copy-start.17
  34.7 0.0 copy-start.23
  34.7 6.6 %all-to-all-done.line_ref = bf16[16,48,128]{2,1,0:T(8,128)(2,1)S(1)} async-done(((bf16[16,48,128]{2,1,0:T(8,128)(2,1)}), bf16[16,48,128]{2,1,0:T(8,128)(2,1)S(1)}, u32[]{:S(2)}, u32[]{:S(2)}) %all-to-all-start) | async-done | bytes 196640 | tf_op jit(solution)/shard_map/all_to_all | solution.py:561
  41.4 1.2 %shard_map.134 = bf16[8,544,128]{2,1,0:T(8,128)(2,1)} custom-call(bf16[16,48,128]{2,1,0:T(8,128)(2,1)S(1)} %all-to-all-done.line_ref, bf16[512,128]{1,0:T(8,128)(2,1)S(1)} %get-tuple-element.21.after_ref.keep_any), custom_call_target="tpu_custom_call" | custom-call | bytes 4194304 | tf_op jit(solution)/shard_map/pallas_call | solution.py:141
  42.5 0.0 copy-done.17
  42.5 0.0 copy-done.23
  42.5 4.1 %all-to-all-start.1 = ((bf16[8,544,128]{2,1,0:T(8,128)(2,1)}), bf16[8,544,128]{2,1,0:T(8,128)(2,1)S(1)}, u32[]{:S(2)}, u32[]{:S(2)}) async-start(bf16[8,544,128]{2,1,0:T(8,128)(2,1)} %shard_map.134), calls=%async_computation.1 | async-start | bytes 2228224 | tf_op jit(solution)/shard_map/all_to_all | solution.py:561
  46.7 10.8 %shard_map.135 = (bf16[512,512]{1,0:T(8,128)(2,1)}, bf16[512,512]{1,0:T(8,128)(2,1)}, bf16[512,512]{1,0:T(8,128)(2,1)}, bf16[512,512]{1,0:T(8,128)(2,1)}, bf16[8...) custom-call(bf16[512,128]{1,0:T(8,128)(2,1)} %copy-done.17, ...), custom_call_target="tpu_custom_call" | custom-call | flops 4000000000 | bytes 4194304 | tf_op jit(solution)/shard_map/pallas_call | solution.py:328
  57.5 5.1 %all-to-all-done.1.plane_ref = bf16[8,544,128]{2,1,0:T(8,128)(2,1)S(1)} async-done(((bf16[8,544,128]{2,1,0:T(8,128)(2,1)}), bf16[8,544,128]{2,1,0:T(8,128)(2,1)S(1)}, u32[]{:S(2)}, u32[]{:S(2)}) %all-to-all-start.1) | async-done | bytes 1114144 | tf_op jit(solution)/shard_map/all_to_all | solution.py:561
  62.6 0.9 copy-done.21
  63.5 0.0 copy-start.10
  63.5 0.0 copy-start.14
  63.5 0.0 copy-start.15
  63.6 0.0 copy-start.16
  63.6 1.7 %shard_map.136 = (f32[128,128]{1,0:T(8,128)S(1)}, f32[32,128]{1,0:T(8,128)S(1)}, f32[32,128]{1,0:T(8,128)S(1)}) custom-call(bf16[8,544,128]{2,1,0:T(8,128)(2,1)S(1)} %all-to-all-done.1.plane_ref, bf16[1024,128]{1,0:T(8,128)(2,1)S(1)} %copy-done.21), custom_call_target="tpu_custom_call" | custom-call | flops 1000000000 | bytes 4194304 | tf_op jit(solution)/shard_map/pallas_call | solution.py:366
  65.3 25.3 %all_to_all.21 = f32[128,1,128]{2,1,0:T(1,128)S(1)} all-to-all(f32[128,1,128]{2,1,0:T(1,128)S(1)} %bitcast.9), channel_id=1, replica_groups=mesh['z'=16,'ylo'=2,'x'=4,'yhi'=2,'core'=2] {'z','ylo','x'}, dimensions={0} | all-to-all | bytes 131072 | tf_op jit(solution)/shard_map/all_to_all | solution.py:561
  90.6 0.0 copy-done.22
  90.6 0.0 copy-start.3
  90.6 0.0 copy-start.4
  90.6 0.0 copy-start.5
  90.6 0.0 copy-start.7
  90.6 0.0 copy-start.18
  90.7 2.4 %shard_map.137.own_ref = f32[520,128]{1,0:T(8,128)S(1)} custom-call(f32[128,128]{1,0:T(8,128)S(1)} %bitcast.8, f32[32,128]{1,0:T(8,128)S(1)} %get-tuple-element.25.sums_ref, f32[32,128]{1,0:T(8,128)S(1)} %get-tuple-element.26.weight_ref, bf16[8,544,128]{2,1,0:T(8,128)(2,1)S(1)} %all-to-all-done.1.plane_ref, bf16[1024,128]{1,0:T(8,128)(2,1)S(1)} %copy-done.22), custom_call_target="tpu_custom_call" | custom-call | flops 2000000000 | bytes 4194304 | tf_op jit(solution)/shard_map/pallas_call | solution.py:413
  93.1 4.2 %collective-permute-start.3 = (f32[520,128]{1,0:T(8,128)S(1)}, f32[520,128]{1,0:T(8,128)S(1)}, u32[]{:S(2)}, u32[]{:S(2)}) collective-permute-start(f32[520,128]{1,0:T(8,128)S(1)} %shard_map.137.own_ref), channel_id=1, source_target_pairs={{0,1},{1,0},{2,3},{3,2},{4,5},{5,4},{6,7},{7,6},{8,9},{9,8},{10,11... | collective-permute-start | bytes 798728 | tf_op jit(solution)/shard_map/ppermute | solution.py:592
  97.3 1.1 %collective-permute-done.3.got_ref = f32[520,128]{1,0:T(8,128)S(1)} collective-permute-done((f32[520,128]{1,0:T(8,128)S(1)}, f32[520,128]{1,0:T(8,128)S(1)}, u32[]{:S(2)}, u32[]{:S(2)}) %collective-permute-start.3) | collective-permute-done | bytes 266272 | tf_op jit(solution)/shard_map/ppermute | solution.py:592
  98.5 0.1 shard_map.138
  98.5 3.5 %collective-permute-start.4 = (bf16[544,128]{1,0:T(8,128)(2,1)S(1)}, bf16[544,128]{1,0:T(8,128)(2,1)S(1)}, u32[]{:S(2)}, u32[]{:S(2)}) collective-permute-start(bf16[544,128]{1,0:T(8,128)(2,1)S(1)} %get-tuple-element.28), channel_id=1, source_target_pairs={{0,2},{2,0},{1,3},{3,1},{4,6},{6,4},{5,7},{7,5},{8,10},{10,8},{9,1... | collective-permute-start | bytes 417800 | tf_op jit(solution)/shard_map/ppermute | solution.py:593
  102.0 4.8 %collective-permute-done.4.got_ref = bf16[544,128]{1,0:T(8,128)(2,1)S(1)} collective-permute-done((bf16[544,128]{1,0:T(8,128)(2,1)S(1)}, bf16[544,128]{1,0:T(8,128)(2,1)S(1)}, u32[]{:S(2)}, u32[]{:S(2)}) %collective-permute-start.4) | collective-permute-done | bytes 139296 | tf_op jit(solution)/shard_map/ppermute | solution.py:593
  106.8 0.0 copy-done.6
  106.8 0.0 copy-done.8
  106.8 0.0 copy-done.9
  106.8 0.0 copy-done.10
  106.8 0.0 copy-done.14
  106.8 0.0 copy-done.15
  106.8 0.0 copy-done.16
  106.8 0.0 copy-done
  106.9 0.0 copy-done.1
  106.9 0.0 copy-done.2
  106.9 0.0 copy-done.3
  106.9 0.0 copy-done.4
  106.9 0.0 copy-done.5
  106.9 0.0 copy-done.7
  106.9 0.0 copy-done.18
  106.9 5.3 %shard_map.139 = (bf16[128,1024]{1,0:T(8,128)(2,1)}, f32[1]{0:T(128)}) custom-call(f32[520,128]{1,0:T(8,128)S(1)} %get-tuple-element.27.sum_ref, bf16[544,128]{1,0:T(8,128)(2,1)S(1)} %collective-permute-done.4.got_ref, f32[512,128]{1,0:T(8,128)S(1)} %copy-done.16, bf16[1024,128]{1,0:T(8,128)(2,1)S(1)} %copy-done.14, f32[512,128]{1,0:T(8,128)S(1)} %copy-done.15, ...), custom_call_target="tpu_custom_call" | custom-call | flops 3000000000 | bytes 4194304 | tf_op jit(solution)/shard_map/pallas_call | solution.py:539
  (8 shorter events, 0.0 us)
Async XLA Ops:
  2.3 11.4 %collective-permute-start = (bf16[144,1024]{1,0:T(8,128)(2,1)}, bf16[144,1024]{1,0:T(8,128)(2,1)S(1)}, u32[]{:S(2)}, u32[]{:S(2)}) collective-permute-start(bf16[144,1024]{1,0:T(8,128)(2,1)} %shard_map.131.x0_any), channel_id=1, source_target_pairs={{0,1},{1,0},{2,3},{3,2},{4,5},{5,4},{6,7},{7,6},{8,9},{9,8},{10,11... | collective-permute-start | bytes 884744 | tf_op jit(solution)/shard_map/ppermute | solution.py:579
  11.1 17.3 %collective-permute-start.1 = (bf16[144,1024]{1,0:T(8,128)(2,1)}, bf16[144,1024]{1,0:T(8,128)(2,1)S(1)}, u32[]{:S(2)}, u32[]{:S(2)}) collective-permute-start(bf16[144,1024]{1,0:T(8,128)(2,1)} %shard_map.131.x0_any), channel_id=1, source_target_pairs={{0,2},{2,0},{1,3},{3,1},{4,6},{6,4},{5,7},{7,5},{8,10},{10,8},{9,1... | collective-permute-start | bytes 884744 | tf_op jit(solution)/shard_map/ppermute | solution.py:580
  13.7 0.7 copy-start.12
  15.9 25.5 %all-to-all-start = ((bf16[16,48,128]{2,1,0:T(8,128)(2,1)}), bf16[16,48,128]{2,1,0:T(8,128)(2,1)S(1)}, u32[]{:S(2)}, u32[]{:S(2)}) async-start(bf16[16,48,128]{2,1,0:T(8,128)(2,1)} %shard_map.132), calls=%async_computation | async-start | bytes 393216 | tf_op jit(solution)/shard_map/all_to_all | solution.py:561
  28.4 6.1 %copy-start.19 = (bf16[144,1024]{1,0:T(8,128)(2,1)}, bf16[144,1024]{1,0:T(8,128)(2,1)S(1)}, u32[]{:S(2)}) copy-start(bf16[144,1024]{1,0:T(8,128)(2,1)S(1)} %collective-permute-done.1.x2_any) | copy-start | bytes 884740
  28.4 3.7 %collective-permute-start.2 = (bf16[144,1024]{1,0:T(8,128)(2,1)S(1)}, bf16[144,1024]{1,0:T(8,128)(2,1)S(1)}, u32[]{:S(2)}, u32[]{:S(2)}) collective-permute-start(bf16[144,1024]{1,0:T(8,128)(2,1)S(1)} %collective-permute-done.1.x2_any), channel_id=1, source_target_pairs={{0,1},{1,0},{2,3},{3,2},{4,5},{5,4},{6,7},{7,6},{8,9},{9,8},{10,11... | collective-permute-start | bytes 884744 | tf_op jit(solution)/shard_map/ppermute | solution.py:582
  32.1 1.0 copy-start.11
  33.0 1.0 copy-start.13
  34.0 0.7 copy-start.20
  34.7 7.8 %copy-start.17 = (bf16[512,128]{1,0:T(8,128)(2,1)}, bf16[512,128]{1,0:T(8,128)(2,1)S(1)}, u32[]{:S(2)}) copy-start(bf16[512,128]{1,0:T(8,128)(2,1)S(1)} %get-tuple-element.21.after_ref.keep_any) | copy-start | bytes 393220
  34.7 7.8 %copy-start.23 = (f32[8,512]{1,0:T(8,128)}, f32[8,512]{1,0:T(8,128)S(1)}, u32[]{:S(2)}) copy-start(f32[8,512]{1,0:T(8,128)S(1)} %get-tuple-element.22.bias_any) | copy-start | bytes 49156
  42.5 20.0 %all-to-all-start.1 = ((bf16[8,544,128]{2,1,0:T(8,128)(2,1)}), bf16[8,544,128]{2,1,0:T(8,128)(2,1)S(1)}, u32[]{:S(2)}, u32[]{:S(2)}) async-start(bf16[8,544,128]{2,1,0:T(8,128)(2,1)} %shard_map.134), calls=%async_computation.1 | async-start | bytes 2228224 | tf_op jit(solution)/shard_map/all_to_all | solution.py:561
  62.6 1.0 copy-start.21
  63.5 27.1 %copy-start.22 = (bf16[1024,128]{1,0:T(8,128)(2,1)S(1)}, bf16[1024,128]{1,0:T(8,128)(2,1)}, u32[]{:S(2)}) copy-start(bf16[1024,128]{1,0:T(8,128)(2,1)} %get-tuple-element.23.embed_ref) | copy-start | bytes 786436
  63.5 43.3 %copy-start.6 = (bf16[8,128,512]{2,1,0:T(8,128)(2,1)S(1)}, bf16[8,128,512]{2,1,0:T(8,128)(2,1)}, u32[]{:S(2)}) copy-start(bf16[8,128,512]{2,1,0:T(8,128)(2,1)} %get-tuple-element.37.pcol_ref) | copy-start | bytes 3145732
  63.5 43.3 %copy-start.8 = (bf16[512,512]{1,0:T(8,128)(2,1)S(1)}, bf16[512,512]{1,0:T(8,128)(2,1)}, u32[]{:S(2)}) copy-start(bf16[512,512]{1,0:T(8,128)(2,1)} %get-tuple-element.34.k_ref) | copy-start | bytes 1572868
  63.5 43.3 %copy-start.9 = (bf16[512,512]{1,0:T(8,128)(2,1)S(1)}, bf16[512,512]{1,0:T(8,128)(2,1)}, u32[]{:S(2)}) copy-start(bf16[512,512]{1,0:T(8,128)(2,1)} %get-tuple-element.33.v_ref) | copy-start | bytes 1572868
  63.5 43.3 %copy-start.10 = (bf16[512,512]{1,0:T(8,128)(2,1)S(1)}, bf16[512,512]{1,0:T(8,128)(2,1)}, u32[]{:S(2)}) copy-start(bf16[512,512]{1,0:T(8,128)(2,1)} %get-tuple-element.32.att_ref) | copy-start | bytes 1572868
  63.5 43.3 %copy-start.14 = (bf16[1024,128]{1,0:T(8,128)(2,1)S(1)}, bf16[1024,128]{1,0:T(8,128)(2,1)}, u32[]{:S(2)}) copy-start(bf16[1024,128]{1,0:T(8,128)(2,1)} %wp_ref.1) | copy-start | bytes 786436
  63.5 43.3 %copy-start.15 = (f32[512,128]{1,0:T(8,128)S(1)}, f32[512,128]{1,0:T(8,128)}, u32[]{:S(2)}) copy-start(f32[512,128]{1,0:T(8,128)} %get-tuple-element.30.inv_ref) | copy-start | bytes 786436
  63.6 43.3 %copy-start.16 = (f32[512,128]{1,0:T(8,128)S(1)}, f32[512,128]{1,0:T(8,128)}, u32[]{:S(2)}) copy-start(f32[512,128]{1,0:T(8,128)} %get-tuple-element.29.proj_ref) | copy-start | bytes 786436
  90.6 16.3 %copy-start = (f32[512,1024]{1,0:T(8,128)S(1)}, f32[512,1024]{1,0:T(8,128)}, u32[]{:S(2)}) copy-start(f32[512,1024]{1,0:T(8,128)} %get-tuple-element.31.unit_ref) | copy-start | bytes 6291460
  90.6 16.3 %copy-start.1 = (bf16[1024,512]{1,0:T(8,128)(2,1)S(1)}, bf16[1024,512]{1,0:T(8,128)(2,1)}, u32[]{:S(2)}) copy-start(bf16[1024,512]{1,0:T(8,128)(2,1)} %wq_ref.1) | copy-start | bytes 3145732
  90.6 16.3 %copy-start.2 = (bf16[1024,512]{1,0:T(8,128)(2,1)S(1)}, bf16[1024,512]{1,0:T(8,128)(2,1)}, u32[]{:S(2)}) copy-start(bf16[1024,512]{1,0:T(8,128)(2,1)} %wk_ref.1) | copy-start | bytes 3145732
  90.6 16.3 %copy-start.3 = (bf16[1024,512]{1,0:T(8,128)(2,1)S(1)}, bf16[1024,512]{1,0:T(8,128)(2,1)}, u32[]{:S(2)}) copy-start(bf16[1024,512]{1,0:T(8,128)(2,1)} %wv_ref.1) | copy-start | bytes 3145732
  90.6 16.3 %copy-start.4 = (bf16[512,1024]{1,0:T(8,128)(2,1)S(1)}, bf16[512,1024]{1,0:T(8,128)(2,1)}, u32[]{:S(2)}) copy-start(bf16[512,1024]{1,0:T(8,128)(2,1)} %wo_ref.1) | copy-start | bytes 3145732
  90.6 16.3 %copy-start.5 = (bf16[8,128,512]{2,1,0:T(8,128)(2,1)S(1)}, bf16[8,128,512]{2,1,0:T(8,128)(2,1)}, u32[]{:S(2)}) copy-start(bf16[8,128,512]{2,1,0:T(8,128)(2,1)} %get-tuple-element.36.prow_ref) | copy-start | bytes 3145732
  90.6 16.3 %copy-start.7 = (bf16[512,512]{1,0:T(8,128)(2,1)S(1)}, bf16[512,512]{1,0:T(8,128)(2,1)}, u32[]{:S(2)}) copy-start(bf16[512,512]{1,0:T(8,128)(2,1)} %get-tuple-element.35.q_ref) | copy-start | bytes 1572868
  90.6 16.3 %copy-start.18 = (f32[1024]{0:T(1024)S(1)}, f32[1024]{0:T(1024)}, u32[]{:S(2)}) copy-start(f32[1024]{0:T(1024)} %param.19) | copy-start | bytes 12292
  93.1 5.4 %collective-permute-start.3 = (f32[520,128]{1,0:T(8,128)S(1)}, f32[520,128]{1,0:T(8,128)S(1)}, u32[]{:S(2)}, u32[]{:S(2)}) collective-permute-start(f32[520,128]{1,0:T(8,128)S(1)} %shard_map.137.own_ref), channel_id=1, source_target_pairs={{0,1},{1,0},{2,3},{3,2},{4,5},{5,4},{6,7},{7,6},{8,9},{9,8},{10,11... | collective-permute-start | bytes 798728 | tf_op jit(solution)/shard_map/ppermute | solution.py:592
  98.5 8.3 %collective-permute-start.4 = (bf16[544,128]{1,0:T(8,128)(2,1)S(1)}, bf16[544,128]{1,0:T(8,128)(2,1)S(1)}, u32[]{:S(2)}, u32[]{:S(2)}) collective-permute-start(bf16[544,128]{1,0:T(8,128)(2,1)S(1)} %get-tuple-element.28), channel_id=1, source_target_pairs={{0,2},{2,0},{1,3},{3,1},{4,6},{6,4},{5,7},{7,5},{8,10},{10,8},{9,1... | collective-permute-start | bytes 417800 | tf_op jit(solution)/shard_map/ppermute | solution.py:593

commit v5 on v4

--- a/solution.py
+++ b/solution.py
@@ -27,7 +27,7 @@
 CHUNK = LINE * QLEN
 STRIP = 64
 THIN = 32
-MARKS_FLOPS = 3 * 10**9
+MARKS_FLOPS = 10**8
 LOG2E = 1.4426950408889634
 SWAP = [(0, 1), (1, 0)]
 bf16 = jnp.bfloat16
@@ -103,7 +103,7 @@
     )
 
 
-def pack_query_kernel(pos_ref, queries_ref, mask_ref, after_ref, query_out):
+def pack_query_kernel(pos_ref, queries_ref, mask_ref, query_out):
     q = queries_ref[...].astype(f32)
     qn = (q * lax.rsqrt(jnp.sum(q * q, -1, keepdims=True) + 1e-06)).astype(bf16)
     repeat = (iota((QLEN, E), 1) % QLEN == iota((QLEN, E), 0)).astype(bf16)
@@ -116,13 +116,13 @@
         query_out[z, QLEN:, :] = aux
 
 
-def pack_query(positive, queries, query_mask, after):
+def pack_query(positive, queries, query_mask):
     return call(
         pack_query_kernel,
         shape((LINE, QLEN + AUX, E), bf16),
-        [SMEM, BLOCK, BLOCK, ANY],
+        [SMEM, BLOCK, BLOCK],
         limit=56,
-    )(positive, queries[0], query_mask, after)
+    )(positive, queries[0], query_mask)
 
 
 def repack_kernel(line_ref, after_ref, out_ref):
@@ -331,8 +331,8 @@
         [ANY] * 6 + [HBM] * 6,
         tuple(HBM for _ in outs),
         ins + [pltpu.VMEM(o.shape, o.dtype) for o in outs] + work,
-        flops=4 * 10**9,
-        limit=56,
+        flops=6 * 10**9,
+        limit=52,
     )(keep, bias, *blocks, w_query, w_key, w_value, w_out, ln_gain[None], w_proj)
 
 
@@ -578,11 +578,13 @@
     own = pack_hidden(hidden, doc_keep)
     by_core = lax.ppermute(own, "core", SWAP)
     by_yhi = lax.ppermute(own, "yhi", SWAP)
-    line = spread(pack_query(positive, queries, query_mask, by_core), "z")
+    line = spread(pack_query(positive, queries, query_mask), "z")
+    packed = repack(line, by_core)
+    plane = spread(packed, ("ylo", "x"))
+    by_yhi, _ = lax.optimization_barrier((by_yhi, packed))
     by_both = lax.ppermute(by_yhi, "core", SWAP)
     blocks = (own, by_core, by_yhi, by_both)
     keep, bias = marks_call(doc_len, blocks)
-    plane = spread(repack(line, keep), ("ylo", "x"))
     *kept, embed = forward(
         keep, bias, blocks, w_query, w_key, w_value, w_out, ln_gain, w_proj
     )

time: 113 us -> 106 us (0.938)
  waiting for transfers between devices: 18.2 us -> 8.58 us
  starting transfers between devices: 37.4 us -> 45.2 us
  local copies, waits for them, and re-layouts: 3.98 us -> 0.37 us
  blocking collectives: 25.3 us -> 24 us
    all_to_all x2, waiting for transfers between devices: 11.7 us -> 3.16 us  [spread(): return lax.all_to_all(x, axes, 0, 0)]
    ppermute x1, starting transfers between devices: 8.77 us -> 2.85 us  [body(): by_core = lax.ppermute(own, 'core', SWAP)]
    ppermute x1, starting transfers between devices: 2.48 us -> 7.15 us  [body(): by_both = lax.ppermute(by_yhi, 'core', SWAP)]
    all_to_all x2, starting transfers between devices: 16.6 us -> 20.9 us  [spread(): return lax.all_to_all(x, axes, 0, 0)]
    unnamed x48 -> x32, local copies, waits for them, and re-layouts: 3.98 us -> 0.37 us
    ppermute x1, starting transfers between devices: 1.92 us -> 4.82 us  [body(): by_yhi = lax.ppermute(own, 'yhi', SWAP)]
    ppermute x1, starting transfers between devices: 3.47 us -> 5.51 us  [body(): got = lax.ppermute(half, 'yhi', SWAP)]
    all_to_all x1, blocking collectives: 25.3 us -> 24 us  [spread(): return lax.all_to_all(x, axes, 0, 0)]
  transfers between devices with their start and end apart: 7 -> 7, of which waited for: 5 -> 4; matrix products, arithmetic and copies ran while one was open for 0% -> 0% of each run, Pallas kernels for 11% -> 13%
where the time goes in v5:
time: 106 us; the launch traced here: 105 us
  starting transfers between devices  45.2 us (43%)
  Pallas kernels  24.9 us (23%)
  blocking collectives  24 us (23%)
  waiting for transfers between devices  8.58 us (8%)
  between operations  2.34 us (2%)
    all_to_all x1, blocking collectives, spread(): return lax.all_to_all(x, axes, 0, 0)  24 us
    all_to_all x2, starting transfers between devices, spread(): return lax.all_to_all(x, axes, 0, 0)  20.9 us
    pallas_call x1, Pallas kernels, forward(): call(forward_kernel, outs, [ANY] * 6 + [HBM] * 6, tuple((HBM for _ in out...  10.5 us
    ppermute x1, starting transfers between devices, body(): by_both = lax.ppermute(by_yhi, 'core', SWAP)  7.15 us
    ppermute x1, starting transfers between devices, body(): got = lax.ppermute(half, 'yhi', SWAP)  5.51 us
    pallas_call x1, Pallas kernels, backward(): call(backward_kernel, (shape((ROWS, D), bf16), shape((1,), f32)), [VMEM]...  5.29 us
    ppermute x1, starting transfers between devices, body(): by_yhi = lax.ppermute(own, 'yhi', SWAP)  4.82 us
    ppermute x1, starting transfers between devices, body(): summed, half = add_call(partial, lax.ppermute(partial, 'core', SWAP))  3.93 us
  transfers between devices with their start and end apart: 7, of which 4 were waited for; matrix products, arithmetic and copies ran while one was open for 0% of the time, Pallas kernels for 13%

profile of v5, /device:TPU:1, one launch (start us, length us, event | category | flops | bytes accessed | tf_op | source)
XLA Modules:
  0.0 105.4 jit_solution(12518544657848021451)
XLA Ops:
  1.3 1.5 %shard_map.131 = bf16[16,48,128]{2,1,0:T(8,128)(2,1)} custom-call(s32[1]{0:T(128)S(6)} %copy.16.pos_ref, bf16[32,128]{1,0:T(8,128)(2,1)} %bitcast.12, bf16[1,32]{1,0:T(2,128)(2,1)} %mask_ref.1), custom_call_target="tpu_custom_call" | custom-call | bytes 4194304 | tf_op jit(solution)/shard_map/pallas_call | solution.py:120
  2.8 15.7 %all-to-all-start = ((bf16[16,48,128]{2,1,0:T(8,128)(2,1)}), bf16[16,48,128]{2,1,0:T(8,128)(2,1)S(1)}, u32[]{:S(2)}, u32[]{:S(2)}) async-start(bf16[16,48,128]{2,1,0:T(8,128)(2,1)} %shard_map.131), calls=%async_computation | async-start | bytes 393216 | tf_op jit(solution)/shard_map/all_to_all | solution.py:561
  18.5 1.7 %shard_map.132.x0_any = bf16[144,1024]{1,0:T(8,128)(2,1)} custom-call(bf16[128,1024]{1,0:T(8,128)(2,1)} %hidden_ref.1, s32[1,128]{1,0:T(1,128)} %bitcast.13), custom_call_target="tpu_custom_call" | custom-call | bytes 4194304 | tf_op jit(solution)/shard_map/pallas_call | solution.py:101
  20.2 2.9 %collective-permute-start = (bf16[144,1024]{1,0:T(8,128)(2,1)}, bf16[144,1024]{1,0:T(8,128)(2,1)S(1)}, u32[]{:S(2)}, u32[]{:S(2)}) collective-permute-start(bf16[144,1024]{1,0:T(8,128)(2,1)} %shard_map.132.x0_any), channel_id=1, source_target_pairs={{0,1},{1,0},{2,3},{3,2},{4,5},{5,4},{6,7},{7,6},{8,9},{9,8},{10,11... | collective-permute-start | bytes 884744 | tf_op jit(solution)/shard_map/ppermute | solution.py:579
  23.1 4.8 %collective-permute-start.1 = (bf16[144,1024]{1,0:T(8,128)(2,1)}, bf16[144,1024]{1,0:T(8,128)(2,1)S(1)}, u32[]{:S(2)}, u32[]{:S(2)}) collective-permute-start(bf16[144,1024]{1,0:T(8,128)(2,1)} %shard_map.132.x0_any), channel_id=1, source_target_pairs={{0,2},{2,0},{1,3},{3,1},{4,6},{6,4},{5,7},{7,5},{8,10},{10,8},{9,1... | collective-permute-start | bytes 884744 | tf_op jit(solution)/shard_map/ppermute | solution.py:580
  27.9 0.0 collective-permute-done.after_ref.x1_any
  27.9 3.2 %all-to-all-done.line_ref = bf16[16,48,128]{2,1,0:T(8,128)(2,1)S(1)} async-done(((bf16[16,48,128]{2,1,0:T(8,128)(2,1)}), bf16[16,48,128]{2,1,0:T(8,128)(2,1)S(1)}, u32[]{:S(2)}, u32[]{:S(2)}) %all-to-all-start) | async-done | bytes 196640 | tf_op jit(solution)/shard_map/all_to_all | solution.py:561
  31.1 1.1 %shard_map.133 = bf16[8,544,128]{2,1,0:T(8,128)(2,1)} custom-call(bf16[16,48,128]{2,1,0:T(8,128)(2,1)S(1)} %all-to-all-done.line_ref, bf16[144,1024]{1,0:T(8,128)(2,1)S(1)} %collective-permute-done.after_ref.x1_any), custom_call_target="tpu_custom_call" | custom-call | bytes 4194304 | tf_op jit(solution)/shard_map/pallas_call | solution.py:141
  32.2 0.0 copy-start.1
  32.2 5.2 %all-to-all-start.1 = ((bf16[8,544,128]{2,1,0:T(8,128)(2,1)}), bf16[8,544,128]{2,1,0:T(8,128)(2,1)S(1)}, u32[]{:S(2)}, u32[]{:S(2)}) async-start(bf16[8,544,128]{2,1,0:T(8,128)(2,1)} %shard_map.133), calls=%async_computation.1 | async-start | bytes 2228224 | tf_op jit(solution)/shard_map/all_to_all | solution.py:561
  37.4 0.0 copy-start.14
  37.4 0.0 copy-start.15
  37.4 0.0 collective-permute-done.1.x2_any
  37.4 0.0 copy-start.12
  37.4 7.2 %collective-permute-start.2 = (bf16[144,1024]{1,0:T(8,128)(2,1)S(1)}, bf16[144,1024]{1,0:T(8,128)(2,1)S(1)}, u32[]{:S(2)}, u32[]{:S(2)}) collective-permute-start(bf16[144,1024]{1,0:T(8,128)(2,1)S(1)} %collective-permute-done.1.x2_any), channel_id=1, source_target_pairs={{0,1},{1,0},{2,3},{3,2},{4,5},{5,4},{6,7},{7,6},{8,9},{9,8},{10,11... | collective-permute-start | bytes 884744 | tf_op jit(solution)/shard_map/ppermute | solution.py:585
  45.2 0.5 collective-permute-done.2.x3_any
  45.8 0.0 copy-done.1
  45.8 0.0 copy-start.13
  45.8 0.4 shard_map.134
  46.2 0.0 copy-done.12
  46.3 0.3 copy-done.13
  46.6 0.0 copy-done.14
  46.6 0.0 copy-done.15
  46.6 10.5 %shard_map.135 = (bf16[512,512]{1,0:T(8,128)(2,1)}, bf16[512,512]{1,0:T(8,128)(2,1)}, bf16[512,512]{1,0:T(8,128)(2,1)}, bf16[512,512]{1,0:T(8,128)(2,1)}, bf16[8...) custom-call(bf16[512,128]{1,0:T(8,128)(2,1)S(1)} %get-tuple-element., ...), custom_call_target="tpu_custom_call" | custom-call | flops 6000000000 | bytes 4194304 | tf_op jit(solution)/shard_map/pallas_call | solution.py:328
  57.0 0.0 all-to-all-done.1.plane_ref
  57.1 0.0 copy-start.7
  57.1 0.0 copy-start.9
  57.1 0.0 copy-start.10
  57.1 0.0 copy-start.11
  57.1 1.8 %shard_map.136 = (f32[128,128]{1,0:T(8,128)S(1)}, f32[32,128]{1,0:T(8,128)S(1)}, f32[32,128]{1,0:T(8,128)S(1)}) custom-call(bf16[8,544,128]{2,1,0:T(8,128)(2,1)S(1)} %all-to-all-done.1.plane_ref, bf16[1024,128]{1,0:T(8,128)(2,1)S(1)} %get-tuple-element.25.embed_ref), custom_call_target="tpu_custom_call" | custom-call | flops 1000000000 | bytes 4194304 | tf_op jit(solution)/shard_map/pallas_call | solution.py:366
  58.9 24.0 %all_to_all.21 = f32[128,1,128]{2,1,0:T(1,128)S(1)} all-to-all(f32[128,1,128]{2,1,0:T(1,128)S(1)} %bitcast.9), channel_id=1, replica_groups=mesh['z'=16,'ylo'=2,'x'=4,'yhi'=2,'core'=2] {'z','ylo','x'}, dimensions={0} | all-to-all | bytes 131072 | tf_op jit(solution)/shard_map/all_to_all | solution.py:561
  83.0 0.0 copy-start
  83.0 0.0 copy-start.2
  83.0 0.0 copy-start.3
  83.0 0.0 copy-start.4
  83.0 0.0 copy-start.5
  83.0 0.0 copy-start.6
  83.0 0.0 copy-start.8
  83.0 2.4 %shard_map.137.own_ref = f32[520,128]{1,0:T(8,128)S(1)} custom-call(f32[128,128]{1,0:T(8,128)S(1)} %bitcast.8, f32[32,128]{1,0:T(8,128)S(1)} %get-tuple-element.27.sums_ref, f32[32,128]{1,0:T(8,128)S(1)} %get-tuple-element.28.weight_ref, bf16[8,544,128]{2,1,0:T(8,128)(2,1)S(1)} %all-to-all-done.1.plane_ref, bf16[1024,128]{1,0:T(8,128)(2,1)S(1)} %get-tuple-element.25.embed_ref), custom_call_target="tpu_custom_call" | custom-call | flops 2000000000 | bytes 4194304 | tf_op jit(solution)/shard_map/pallas_call | solution.py:413
  85.5 3.9 %collective-permute-start.3 = (f32[520,128]{1,0:T(8,128)S(1)}, f32[520,128]{1,0:T(8,128)S(1)}, u32[]{:S(2)}, u32[]{:S(2)}) collective-permute-start(f32[520,128]{1,0:T(8,128)S(1)} %shard_map.137.own_ref), channel_id=1, source_target_pairs={{0,1},{1,0},{2,3},{3,2},{4,5},{5,4},{6,7},{7,6},{8,9},{9,8},{10,11... | collective-permute-start | bytes 798728 | tf_op jit(solution)/shard_map/ppermute | solution.py:594
  89.4 1.1 %collective-permute-done.3.got_ref = f32[520,128]{1,0:T(8,128)S(1)} collective-permute-done((f32[520,128]{1,0:T(8,128)S(1)}, f32[520,128]{1,0:T(8,128)S(1)}, u32[]{:S(2)}, u32[]{:S(2)}) %collective-permute-start.3) | collective-permute-done | bytes 266272 | tf_op jit(solution)/shard_map/ppermute | solution.py:594
  90.6 5.5 %collective-permute-start.4 = (bf16[544,128]{1,0:T(8,128)(2,1)S(1)}, bf16[544,128]{1,0:T(8,128)(2,1)S(1)}, u32[]{:S(2)}, u32[]{:S(2)}) collective-permute-start(bf16[544,128]{1,0:T(8,128)(2,1)S(1)} %get-tuple-element.30), channel_id=1, source_target_pairs={{0,2},{2,0},{1,3},{3,1},{4,6},{6,4},{5,7},{7,5},{8,10},{10,8},{9,1... | collective-permute-start | bytes 417800 | tf_op jit(solution)/shard_map/ppermute | solution.py:595
  96.1 3.7 %collective-permute-done.4.got_ref = bf16[544,128]{1,0:T(8,128)(2,1)S(1)} collective-permute-done((bf16[544,128]{1,0:T(8,128)(2,1)S(1)}, bf16[544,128]{1,0:T(8,128)(2,1)S(1)}, u32[]{:S(2)}, u32[]{:S(2)}) %collective-permute-start.4) | collective-permute-done | bytes 139296 | tf_op jit(solution)/shard_map/ppermute | solution.py:595
  99.8 0.0 copy-done.7
  99.8 0.0 copy-done.9
  99.8 0.0 copy-done.10
  99.8 0.0 copy-done.11
  99.9 0.0 copy-done
  99.9 0.0 copy-done.2
  99.9 0.0 copy-done.3
  99.9 0.0 copy-done.4
  99.9 0.0 copy-done.5
  99.9 0.0 copy-done.6
  99.9 0.0 copy-done.8
  99.9 5.3 %shard_map.139 = (bf16[128,1024]{1,0:T(8,128)(2,1)}, f32[1]{0:T(128)}) custom-call(f32[520,128]{1,0:T(8,128)S(1)} %get-tuple-element.29.sum_ref, bf16[544,128]{1,0:T(8,128)(2,1)S(1)} %collective-permute-done.4.got_ref, f32[512,128]{1,0:T(8,128)S(1)} %get-tuple-element.31.proj_ref, bf16[1024,128]{1,0:T(8,128)(2,1)S(1)} %copy-done.14, ...), custom_call_target="tpu_custom_call" | custom-call | flops 3000000000 | bytes 4194304 | tf_op jit(solution)/shard_map/pallas_call | solution.py:539
  (1 shorter events, 0.0 us)
Async XLA Ops:
  2.8 28.3 %all-to-all-start = ((bf16[16,48,128]{2,1,0:T(8,128)(2,1)}), bf16[16,48,128]{2,1,0:T(8,128)(2,1)S(1)}, u32[]{:S(2)}, u32[]{:S(2)}) async-start(bf16[16,48,128]{2,1,0:T(8,128)(2,1)} %shard_map.131), calls=%async_computation | async-start | bytes 393216 | tf_op jit(solution)/shard_map/all_to_all | solution.py:561
  20.2 7.7 %collective-permute-start = (bf16[144,1024]{1,0:T(8,128)(2,1)}, bf16[144,1024]{1,0:T(8,128)(2,1)S(1)}, u32[]{:S(2)}, u32[]{:S(2)}) collective-permute-start(bf16[144,1024]{1,0:T(8,128)(2,1)} %shard_map.132.x0_any), channel_id=1, source_target_pairs={{0,1},{1,0},{2,3},{3,2},{4,5},{5,4},{6,7},{7,6},{8,9},{9,8},{10,11... | collective-permute-start | bytes 884744 | tf_op jit(solution)/shard_map/ppermute | solution.py:579
  23.1 14.3 %collective-permute-start.1 = (bf16[144,1024]{1,0:T(8,128)(2,1)}, bf16[144,1024]{1,0:T(8,128)(2,1)S(1)}, u32[]{:S(2)}, u32[]{:S(2)}) collective-permute-start(bf16[144,1024]{1,0:T(8,128)(2,1)} %shard_map.132.x0_any), channel_id=1, source_target_pairs={{0,2},{2,0},{1,3},{3,1},{4,6},{6,4},{5,7},{7,5},{8,10},{10,8},{9,1... | collective-permute-start | bytes 884744 | tf_op jit(solution)/shard_map/ppermute | solution.py:580
  32.2 13.6 %copy-start.1 = (bf16[144,1024]{1,0:T(8,128)(2,1)S(1)}, bf16[144,1024]{1,0:T(8,128)(2,1)}, u32[]{:S(2)}) copy-start(bf16[144,1024]{1,0:T(8,128)(2,1)} %shard_map.132.x0_any) | copy-start | bytes 884740
  32.2 24.8 %all-to-all-start.1 = ((bf16[8,544,128]{2,1,0:T(8,128)(2,1)}), bf16[8,544,128]{2,1,0:T(8,128)(2,1)S(1)}, u32[]{:S(2)}, u32[]{:S(2)}) async-start(bf16[8,544,128]{2,1,0:T(8,128)(2,1)} %shard_map.133), calls=%async_computation.1 | async-start | bytes 2228224 | tf_op jit(solution)/shard_map/all_to_all | solution.py:561
  37.4 9.2 %copy-start.14 = (bf16[1024,128]{1,0:T(8,128)(2,1)S(1)}, bf16[1024,128]{1,0:T(8,128)(2,1)}, u32[]{:S(2)}) copy-start(bf16[1024,128]{1,0:T(8,128)(2,1)} %wp_ref.1) | copy-start | bytes 786436
  37.4 9.2 %copy-start.15 = (f32[1024]{0:T(1024)S(1)}, f32[1024]{0:T(1024)}, u32[]{:S(2)}) copy-start(f32[1024]{0:T(1024)} %param.19) | copy-start | bytes 12292
  37.4 8.8 %copy-start.12 = (bf16[144,1024]{1,0:T(8,128)(2,1)}, bf16[144,1024]{1,0:T(8,128)(2,1)S(1)}, u32[]{:S(2)}) copy-start(bf16[144,1024]{1,0:T(8,128)(2,1)S(1)} %collective-permute-done.1.x2_any) | copy-start | bytes 884740
  37.4 8.3 %collective-permute-start.2 = (bf16[144,1024]{1,0:T(8,128)(2,1)S(1)}, bf16[144,1024]{1,0:T(8,128)(2,1)S(1)}, u32[]{:S(2)}, u32[]{:S(2)}) collective-permute-start(bf16[144,1024]{1,0:T(8,128)(2,1)S(1)} %collective-permute-done.1.x2_any), channel_id=1, source_target_pairs={{0,1},{1,0},{2,3},{3,2},{4,5},{5,4},{6,7},{7,6},{8,9},{9,8},{10,11... | collective-permute-start | bytes 884744 | tf_op jit(solution)/shard_map/ppermute | solution.py:585
  45.8 0.8 copy-start.13
  57.1 42.8 %copy-start.7 = (bf16[8,128,512]{2,1,0:T(8,128)(2,1)S(1)}, bf16[8,128,512]{2,1,0:T(8,128)(2,1)}, u32[]{:S(2)}) copy-start(bf16[8,128,512]{2,1,0:T(8,128)(2,1)} %get-tuple-element.39.pcol_ref) | copy-start | bytes 3145732
  57.1 42.8 %copy-start.9 = (bf16[512,512]{1,0:T(8,128)(2,1)S(1)}, bf16[512,512]{1,0:T(8,128)(2,1)}, u32[]{:S(2)}) copy-start(bf16[512,512]{1,0:T(8,128)(2,1)} %get-tuple-element.36.k_ref) | copy-start | bytes 1572868
  57.1 42.8 %copy-start.10 = (bf16[512,512]{1,0:T(8,128)(2,1)S(1)}, bf16[512,512]{1,0:T(8,128)(2,1)}, u32[]{:S(2)}) copy-start(bf16[512,512]{1,0:T(8,128)(2,1)} %get-tuple-element.35.v_ref) | copy-start | bytes 1572868
  57.1 42.8 %copy-start.11 = (bf16[512,512]{1,0:T(8,128)(2,1)S(1)}, bf16[512,512]{1,0:T(8,128)(2,1)}, u32[]{:S(2)}) copy-start(bf16[512,512]{1,0:T(8,128)(2,1)} %get-tuple-element.34.att_ref) | copy-start | bytes 1572868
  83.0 16.9 %copy-start = (f32[512,1024]{1,0:T(8,128)S(1)}, f32[512,1024]{1,0:T(8,128)}, u32[]{:S(2)}) copy-start(f32[512,1024]{1,0:T(8,128)} %get-tuple-element.33.unit_ref) | copy-start | bytes 6291460
  83.0 16.9 %copy-start.2 = (bf16[1024,512]{1,0:T(8,128)(2,1)S(1)}, bf16[1024,512]{1,0:T(8,128)(2,1)}, u32[]{:S(2)}) copy-start(bf16[1024,512]{1,0:T(8,128)(2,1)} %wq_ref.1) | copy-start | bytes 3145732
  83.0 16.9 %copy-start.3 = (bf16[1024,512]{1,0:T(8,128)(2,1)S(1)}, bf16[1024,512]{1,0:T(8,128)(2,1)}, u32[]{:S(2)}) copy-start(bf16[1024,512]{1,0:T(8,128)(2,1)} %wk_ref.1) | copy-start | bytes 3145732
  83.0 16.9 %copy-start.4 = (bf16[1024,512]{1,0:T(8,128)(2,1)S(1)}, bf16[1024,512]{1,0:T(8,128)(2,1)}, u32[]{:S(2)}) copy-start(bf16[1024,512]{1,0:T(8,128)(2,1)} %wv_ref.1) | copy-start | bytes 3145732
  83.0 16.9 %copy-start.5 = (bf16[512,1024]{1,0:T(8,128)(2,1)S(1)}, bf16[512,1024]{1,0:T(8,128)(2,1)}, u32[]{:S(2)}) copy-start(bf16[512,1024]{1,0:T(8,128)(2,1)} %wo_ref.1) | copy-start | bytes 3145732
  83.0 16.9 %copy-start.6 = (bf16[8,128,512]{2,1,0:T(8,128)(2,1)S(1)}, bf16[8,128,512]{2,1,0:T(8,128)(2,1)}, u32[]{:S(2)}) copy-start(bf16[8,128,512]{2,1,0:T(8,128)(2,1)} %get-tuple-element.38.prow_ref) | copy-start | bytes 3145732
  83.0 16.9 %copy-start.8 = (bf16[512,512]{1,0:T(8,128)(2,1)S(1)}, bf16[512,512]{1,0:T(8,128)(2,1)}, u32[]{:S(2)}) copy-start(bf16[512,512]{1,0:T(8,128)(2,1)} %get-tuple-element.37.q_ref) | copy-start | bytes 1572868
  85.5 5.1 %collective-permute-start.3 = (f32[520,128]{1,0:T(8,128)S(1)}, f32[520,128]{1,0:T(8,128)S(1)}, u32[]{:S(2)}, u32[]{:S(2)}) collective-permute-start(f32[520,128]{1,0:T(8,128)S(1)} %shard_map.137.own_ref), channel_id=1, source_target_pairs={{0,1},{1,0},{2,3},{3,2},{4,5},{5,4},{6,7},{7,6},{8,9},{9,8},{10,11... | collective-permute-start | bytes 798728 | tf_op jit(solution)/shard_map/ppermute | solution.py:594
  90.6 9.2 %collective-permute-start.4 = (bf16[544,128]{1,0:T(8,128)(2,1)S(1)}, bf16[544,128]{1,0:T(8,128)(2,1)S(1)}, u32[]{:S(2)}, u32[]{:S(2)}) collective-permute-start(bf16[544,128]{1,0:T(8,128)(2,1)S(1)} %get-tuple-element.30), channel_id=1, source_target_pairs={{0,2},{2,0},{1,3},{3,1},{4,6},{6,4},{5,7},{7,5},{8,10},{10,8},{9,1... | collective-permute-start | bytes 417800 | tf_op jit(solution)/shard_map/ppermute | solution.py:595

commit v6 on v5

--- a/solution.py
+++ b/solution.py
@@ -16,6 +16,7 @@
 DOCS = 128
 QSET = 128
 AUX = 16
+TAIL = 8
 TAU = 0.05
 GRAD_SCALE = 1024.0
 NEG = -1e30
@@ -105,40 +106,37 @@
 
 def pack_query_kernel(pos_ref, queries_ref, mask_ref, query_out):
     q = queries_ref[...].astype(f32)
-    qn = (q * lax.rsqrt(jnp.sum(q * q, -1, keepdims=True) + 1e-06)).astype(bf16)
+    qn = q * lax.rsqrt(jnp.sum(q * q, -1, keepdims=True) + 1e-06)
     repeat = (iota((QLEN, E), 1) % QLEN == iota((QLEN, E), 0)).astype(bf16)
-    weights = dot(jnp.broadcast_to(mask_ref[...], (AUX, QLEN)), repeat)
-    target = pos_ref[0].astype(f32)
-    row = iota((AUX, E), 0)
-    aux = jnp.where(row == 0, weights, jnp.where(row == 1, target, 0.0)).astype(bf16)
-    for z in range(LINE):
-        query_out[z, :QLEN, :] = qn
-        query_out[z, QLEN:, :] = aux
+    weights = dot(jnp.broadcast_to(mask_ref[...], (16, QLEN)), repeat)[:TAIL]
+    target = jnp.broadcast_to(pos_ref[...], (TAIL, E)).astype(f32)
+    row = iota((TAIL, E), 0)
+    tail = jnp.where(row == 0, weights, jnp.where(row == 1, target, 0.0))
+    packet = jnp.concatenate([qn, tail], 0).astype(bf16)
+    query_out[...] = jnp.broadcast_to(packet[None], (LINE, QLEN + TAIL, E))
 
 
 def pack_query(positive, queries, query_mask):
     return call(
         pack_query_kernel,
-        shape((LINE, QLEN + AUX, E), bf16),
-        [SMEM, BLOCK, BLOCK],
+        shape((LINE, QLEN + TAIL, E), bf16),
+        [BLOCK] * 3,
+        VMEM,
         limit=56,
-    )(positive, queries[0], query_mask)
+    )(positive[None], queries[0], query_mask)
 
 
 def repack_kernel(line_ref, after_ref, out_ref):
-    aux = line_ref[:, QLEN:, :].astype(f32)
-    weights = aux[:, 0, :].astype(bf16)
-    target = aux[:, 1, :].astype(bf16)
+    line = line_ref[...].astype(f32)
+    queries = line[:, :QLEN, :].reshape(CHUNK, E)
+    packed = jnp.concatenate([queries, line[:, QLEN, :], line[:, QLEN + 1, :]], 0).astype(bf16)
     for p in range(PLANE):
-        for z in range(LINE):
-            out_ref[p, z * QLEN : (z + 1) * QLEN, :] = line_ref[z, :QLEN, :]
-        out_ref[p, CHUNK : CHUNK + LINE, :] = weights
-        out_ref[p, CHUNK + LINE :, :] = target
+        out_ref[p] = packed
 
 
 def repack(line, after):
     out = shape((PLANE, CHUNK + 2 * LINE, E), bf16)
-    return call(repack_kernel, out, [BLOCK, ANY])(line, after)
+    return call(repack_kernel, out, [VMEM, ANY], VMEM, limit=8)(line, after)
 
 
 def marks_kernel(length_ref, x0_any, x1_any, x2_any, x3_any, keep_ref, bias_ref, skip_ref, sems):
@@ -196,7 +194,7 @@
     unit_any,
     inv_any,
     proj_any,
-    embed_any,
+    embed_ref,
     x_ref,
     bias_ref,
     wq_ref,
@@ -214,7 +212,6 @@
     unit_ref,
     inv_ref,
     proj_ref,
-    embed_ref,
     score_ref,
     prob_ref,
     sems,
@@ -282,7 +279,9 @@
         unit_ref[rows, :] = unit
         inv_ref[rows, :] = jnp.broadcast_to(inv, (THIN, E))
         x_ref[rows, :] = (unit * gain_ref[...]).astype(bf16)
-    ends.append(moves.start(unit_ref, unit_any))
+        if (c + 1) * THIN % ROWS == 0:
+            done = pl.ds((c + 1) * THIN - ROWS, ROWS)
+            ends.append(moves.start(unit_ref.at[done], unit_any.at[done]))
     ends.append(moves.start(inv_ref, inv_any))
     at_p.wait()
     proj = dot(x_ref[...], wp_ref[...])
@@ -290,7 +289,6 @@
     ends.append(moves.start(proj_ref, proj_any))
     scale = lax.rsqrt(jnp.sum(proj * proj, -1, keepdims=True) + 1e-06)
     embed_ref[:L, :] = (proj * scale).astype(bf16)
-    ends.append(moves.start(embed_ref, embed_any))
     for copy in ends:
         copy.wait()
 
@@ -329,8 +327,8 @@
         forward_kernel,
         outs,
         [ANY] * 6 + [HBM] * 6,
-        tuple(HBM for _ in outs),
-        ins + [pltpu.VMEM(o.shape, o.dtype) for o in outs] + work,
+        tuple(HBM for _ in outs[:-1]) + (VMEM,),
+        ins + [pltpu.VMEM(o.shape, o.dtype) for o in outs[:-1]] + work,
         flops=6 * 10**9,
         limit=52,
     )(keep, bias, *blocks, w_query, w_key, w_value, w_out, ln_gain[None], w_proj)

time: 106 us -> 113 us (1.066)
  blocking collectives: 24 us -> 32.3 us
    all_to_all x1, blocking collectives: 24 us -> 32.3 us  [spread(): return lax.all_to_all(x, axes, 0, 0)]
  transfers between devices with their start and end apart: 7 -> 7, of which waited for: 4 -> 4; matrix products, arithmetic and copies ran while one was open for 0% -> 0% of each run, Pallas kernels for 13% -> 12%
where the time goes in v6:
time: 113 us
  starting transfers between devices  44.9 us (40%)
  blocking collectives  32.3 us (29%)
  Pallas kernels  24.7 us (22%)
  waiting for transfers between devices  8.25 us (7%)
  between operations  2.34 us (2%)
    all_to_all x1, blocking collectives, spread(): return lax.all_to_all(x, axes, 0, 0)  32.3 us
    all_to_all x2, starting transfers between devices, spread(): return lax.all_to_all(x, axes, 0, 0)  20.9 us
    pallas_call x1, Pallas kernels, forward(): call(forward_kernel, outs, [ANY] * 6 + [HBM] * 6, tuple((HBM for _ in out...  10.3 us
    ppermute x1, starting transfers between devices, body(): by_both = lax.ppermute(by_yhi, 'core', SWAP)  6.69 us
    ppermute x1, starting transfers between devices, body(): got = lax.ppermute(half, 'yhi', SWAP)  5.66 us
    pallas_call x1, Pallas kernels, backward(): call(backward_kernel, (shape((ROWS, D), bf16), shape((1,), f32)), [VMEM]...  5.29 us
    ppermute x1, starting transfers between devices, body(): by_yhi = lax.ppermute(own, 'yhi', SWAP)  4.82 us
    ppermute x1, starting transfers between devices, body(): summed, half = add_call(partial, lax.ppermute(partial, 'core', SWAP))  3.94 us
  transfers between devices with their start and end apart: 7, of which 4 were waited for; matrix products, arithmetic and copies ran while one was open for 0% of the time, Pallas kernels for 12%

profile of v6, /device:TPU:1, one launch (start us, length us, event | category | flops | bytes accessed | tf_op | source)
XLA Modules:
  0.0 112.9 jit_solution(18213531326520881576)
XLA Ops:
  1.3 1.5 %shard_map.131 = bf16[16,40,128]{2,1,0:T(8,128)(2,1)} custom-call(s32[1,1]{1,0:T(1,128)} %bitcast.9.pos_ref, bf16[32,128]{1,0:T(8,128)(2,1)} %bitcast.14, bf16[1,32]{1,0:T(2,128)(2,1)} %mask_ref.1), custom_call_target="tpu_custom_call" | custom-call | bytes 4194304 | tf_op jit(solution)/shard_map/pallas_call | solution.py:120
  2.8 15.7 %all-to-all-start = ((bf16[16,40,128]{2,1,0:T(8,128)(2,1)}), bf16[16,40,128]{2,1,0:T(8,128)(2,1)S(1)}, u32[]{:S(2)}, u32[]{:S(2)}) async-start(bf16[16,40,128]{2,1,0:T(8,128)(2,1)} %shard_map.131), calls=%async_computation | async-start | bytes 327680 | tf_op jit(solution)/shard_map/all_to_all | solution.py:559
  18.5 1.7 %shard_map.132.x0_any = bf16[144,1024]{1,0:T(8,128)(2,1)} custom-call(bf16[128,1024]{1,0:T(8,128)(2,1)} %hidden_ref.1, s32[1,128]{1,0:T(1,128)} %bitcast.15), custom_call_target="tpu_custom_call" | custom-call | bytes 4194304 | tf_op jit(solution)/shard_map/pallas_call | solution.py:102
  20.2 2.9 %collective-permute-start = (bf16[144,1024]{1,0:T(8,128)(2,1)}, bf16[144,1024]{1,0:T(8,128)(2,1)S(1)}, u32[]{:S(2)}, u32[]{:S(2)}) collective-permute-start(bf16[144,1024]{1,0:T(8,128)(2,1)} %shard_map.132.x0_any), channel_id=1, source_target_pairs={{0,1},{1,0},{2,3},{3,2},{4,5},{5,4},{6,7},{7,6},{8,9},{9,8},{10,11... | collective-permute-start | bytes 884744 | tf_op jit(solution)/shard_map/ppermute | solution.py:577
  23.1 4.8 %collective-permute-start.1 = (bf16[144,1024]{1,0:T(8,128)(2,1)}, bf16[144,1024]{1,0:T(8,128)(2,1)S(1)}, u32[]{:S(2)}, u32[]{:S(2)}) collective-permute-start(bf16[144,1024]{1,0:T(8,128)(2,1)} %shard_map.132.x0_any), channel_id=1, source_target_pairs={{0,2},{2,0},{1,3},{3,1},{4,6},{6,4},{5,7},{7,5},{8,10},{10,8},{9,1... | collective-permute-start | bytes 884744 | tf_op jit(solution)/shard_map/ppermute | solution.py:578
  27.9 0.0 collective-permute-done.after_ref.x1_any
  27.9 2.8 %all-to-all-done.line_ref = bf16[16,40,128]{2,1,0:T(8,128)(2,1)S(1)} async-done(((bf16[16,40,128]{2,1,0:T(8,128)(2,1)}), bf16[16,40,128]{2,1,0:T(8,128)(2,1)S(1)}, u32[]{:S(2)}, u32[]{:S(2)}) %all-to-all-start) | async-done | bytes 163872 | tf_op jit(solution)/shard_map/all_to_all | solution.py:559
  30.8 1.2 %shard_map.133 = bf16[8,544,128]{2,1,0:T(8,128)(2,1)} custom-call(bf16[16,40,128]{2,1,0:T(8,128)(2,1)S(1)} %all-to-all-done.line_ref, bf16[144,1024]{1,0:T(8,128)(2,1)S(1)} %collective-permute-done.after_ref.x1_any), custom_call_target="tpu_custom_call" | custom-call | bytes 4194304 | tf_op jit(solution)/shard_map/pallas_call | solution.py:139
  31.9 0.0 copy-start.1
  31.9 5.2 %all-to-all-start.1 = ((bf16[8,544,128]{2,1,0:T(8,128)(2,1)}), bf16[8,544,128]{2,1,0:T(8,128)(2,1)S(1)}, u32[]{:S(2)}, u32[]{:S(2)}) async-start(bf16[8,544,128]{2,1,0:T(8,128)(2,1)} %shard_map.133), calls=%async_computation.1 | async-start | bytes 2228224 | tf_op jit(solution)/shard_map/all_to_all | solution.py:559
  37.1 0.0 copy-start.14
  37.1 0.0 copy-start.15
  37.1 0.0 collective-permute-done.1.x2_any
  37.1 0.0 copy-start.12
  37.1 6.7 %collective-permute-start.2 = (bf16[144,1024]{1,0:T(8,128)(2,1)S(1)}, bf16[144,1024]{1,0:T(8,128)(2,1)S(1)}, u32[]{:S(2)}, u32[]{:S(2)}) collective-permute-start(bf16[144,1024]{1,0:T(8,128)(2,1)S(1)} %collective-permute-done.1.x2_any), channel_id=1, source_target_pairs={{0,1},{1,0},{2,3},{3,2},{4,5},{5,4},{6,7},{7,6},{8,9},{9,8},{10,11... | collective-permute-start | bytes 884744 | tf_op jit(solution)/shard_map/ppermute | solution.py:583
  44.5 0.5 collective-permute-done.2.x3_any
  45.0 0.0 copy-done.1
  45.0 0.0 copy-start.13
  45.0 0.4 shard_map.134
  45.5 0.0 copy-done.12
  45.5 0.3 copy-done.13
  45.8 0.0 copy-done.14
  45.8 0.0 copy-done.15
  45.8 10.3 %shard_map.135 = (bf16[512,512]{1,0:T(8,128)(2,1)}, bf16[512,512]{1,0:T(8,128)(2,1)}, bf16[512,512]{1,0:T(8,128)(2,1)}, bf16[512,512]{1,0:T(8,128)(2,1)}, bf16[8...) custom-call(bf16[512,128]{1,0:T(8,128)(2,1)S(1)} %get-tuple-element., ...), custom_call_target="tpu_custom_call" | custom-call | flops 6000000000 | bytes 4194304 | tf_op jit(solution)/shard_map/pallas_call | solution.py:326
  56.1 0.0 all-to-all-done.1.plane_ref
  56.1 0.0 copy-start.7
  56.1 0.0 copy-start.9
  56.1 0.0 copy-start.10
  56.1 0.0 copy-start.11
  56.1 1.8 %shard_map.136 = (f32[128,128]{1,0:T(8,128)S(1)}, f32[32,128]{1,0:T(8,128)S(1)}, f32[32,128]{1,0:T(8,128)S(1)}) custom-call(bf16[8,544,128]{2,1,0:T(8,128)(2,1)S(1)} %all-to-all-done.1.plane_ref, bf16[1024,128]{1,0:T(8,128)(2,1)S(1)} %get-tuple-element.25.embed_ref), custom_call_target="tpu_custom_call" | custom-call | flops 1000000000 | bytes 4194304 | tf_op jit(solution)/shard_map/pallas_call | solution.py:364
  58.0 32.3 %all_to_all.21 = f32[128,1,128]{2,1,0:T(1,128)S(1)} all-to-all(f32[128,1,128]{2,1,0:T(1,128)S(1)} %bitcast.11), channel_id=1, replica_groups=mesh['z'=16,'ylo'=2,'x'=4,'yhi'=2,'core'=2] {'z','ylo','x'}, dimensions={0} | all-to-all | bytes 131072 | tf_op jit(solution)/shard_map/all_to_all | solution.py:559
  90.3 0.0 copy-start
  90.3 0.0 copy-start.2
  90.3 0.0 copy-start.3
  90.3 0.0 copy-start.4
  90.3 0.0 copy-start.5
  90.3 0.0 copy-start.6
  90.3 0.0 copy-start.8
  90.3 2.4 %shard_map.137.own_ref = f32[520,128]{1,0:T(8,128)S(1)} custom-call(f32[128,128]{1,0:T(8,128)S(1)} %bitcast.10, f32[32,128]{1,0:T(8,128)S(1)} %get-tuple-element.27.sums_ref, f32[32,128]{1,0:T(8,128)S(1)} %get-tuple-element.28.weight_ref, bf16[8,544,128]{2,1,0:T(8,128)(2,1)S(1)} %all-to-all-done.1.plane_ref, bf16[1024,128]{1,0:T(8,128)(2,1)S(1)} %get-tuple-element.25.embed_ref), custom_call_target="tpu_custom_call" | custom-call | flops 2000000000 | bytes 4194304 | tf_op jit(solution)/shard_map/pallas_call | solution.py:411
  92.8 3.9 %collective-permute-start.3 = (f32[520,128]{1,0:T(8,128)S(1)}, f32[520,128]{1,0:T(8,128)S(1)}, u32[]{:S(2)}, u32[]{:S(2)}) collective-permute-start(f32[520,128]{1,0:T(8,128)S(1)} %shard_map.137.own_ref), channel_id=1, source_target_pairs={{0,1},{1,0},{2,3},{3,2},{4,5},{5,4},{6,7},{7,6},{8,9},{9,8},{10,11... | collective-permute-start | bytes 798728 | tf_op jit(solution)/shard_map/ppermute | solution.py:592
  96.7 1.1 %collective-permute-done.3.got_ref = f32[520,128]{1,0:T(8,128)S(1)} collective-permute-done((f32[520,128]{1,0:T(8,128)S(1)}, f32[520,128]{1,0:T(8,128)S(1)}, u32[]{:S(2)}, u32[]{:S(2)}) %collective-permute-start.3) | collective-permute-done | bytes 266272 | tf_op jit(solution)/shard_map/ppermute | solution.py:592
  97.9 5.7 %collective-permute-start.4 = (bf16[544,128]{1,0:T(8,128)(2,1)S(1)}, bf16[544,128]{1,0:T(8,128)(2,1)S(1)}, u32[]{:S(2)}, u32[]{:S(2)}) collective-permute-start(bf16[544,128]{1,0:T(8,128)(2,1)S(1)} %get-tuple-element.30), channel_id=1, source_target_pairs={{0,2},{2,0},{1,3},{3,1},{4,6},{6,4},{5,7},{7,5},{8,10},{10,8},{9,1... | collective-permute-start | bytes 417800 | tf_op jit(solution)/shard_map/ppermute | solution.py:593
  103.6 3.7 %collective-permute-done.4.got_ref = bf16[544,128]{1,0:T(8,128)(2,1)S(1)} collective-permute-done((bf16[544,128]{1,0:T(8,128)(2,1)S(1)}, bf16[544,128]{1,0:T(8,128)(2,1)S(1)}, u32[]{:S(2)}, u32[]{:S(2)}) %collective-permute-start.4) | collective-permute-done | bytes 139296 | tf_op jit(solution)/shard_map/ppermute | solution.py:593
  107.3 0.0 copy-done.7
  107.3 0.0 copy-done.9
  107.3 0.0 copy-done.10
  107.3 0.0 copy-done.11
  107.3 0.0 copy-done
  107.3 0.0 copy-done.2
  107.4 0.0 copy-done.3
  107.4 0.0 copy-done.4
  107.4 0.0 copy-done.5
  107.4 0.0 copy-done.6
  107.4 0.0 copy-done.8
  107.4 5.3 %shard_map.139 = (bf16[128,1024]{1,0:T(8,128)(2,1)}, f32[1]{0:T(128)}) custom-call(f32[520,128]{1,0:T(8,128)S(1)} %get-tuple-element.29.sum_ref, bf16[544,128]{1,0:T(8,128)(2,1)S(1)} %collective-permute-done.4.got_ref, f32[512,128]{1,0:T(8,128)S(1)} %get-tuple-element.31.proj_ref, bf16[1024,128]{1,0:T(8,128)(2,1)S(1)} %copy-done.14, ...), custom_call_target="tpu_custom_call" | custom-call | flops 3000000000 | bytes 4194304 | tf_op jit(solution)/shard_map/pallas_call | solution.py:537
  (1 shorter events, 0.0 us)
Async XLA Ops:
  2.8 28.0 %all-to-all-start = ((bf16[16,40,128]{2,1,0:T(8,128)(2,1)}), bf16[16,40,128]{2,1,0:T(8,128)(2,1)S(1)}, u32[]{:S(2)}, u32[]{:S(2)}) async-start(bf16[16,40,128]{2,1,0:T(8,128)(2,1)} %shard_map.131), calls=%async_computation | async-start | bytes 327680 | tf_op jit(solution)/shard_map/all_to_all | solution.py:559
  20.2 7.7 %collective-permute-start = (bf16[144,1024]{1,0:T(8,128)(2,1)}, bf16[144,1024]{1,0:T(8,128)(2,1)S(1)}, u32[]{:S(2)}, u32[]{:S(2)}) collective-permute-start(bf16[144,1024]{1,0:T(8,128)(2,1)} %shard_map.132.x0_any), channel_id=1, source_target_pairs={{0,1},{1,0},{2,3},{3,2},{4,5},{5,4},{6,7},{7,6},{8,9},{9,8},{10,11... | collective-permute-start | bytes 884744 | tf_op jit(solution)/shard_map/ppermute | solution.py:577
  23.1 14.0 %collective-permute-start.1 = (bf16[144,1024]{1,0:T(8,128)(2,1)}, bf16[144,1024]{1,0:T(8,128)(2,1)S(1)}, u32[]{:S(2)}, u32[]{:S(2)}) collective-permute-start(bf16[144,1024]{1,0:T(8,128)(2,1)} %shard_map.132.x0_any), channel_id=1, source_target_pairs={{0,2},{2,0},{1,3},{3,1},{4,6},{6,4},{5,7},{7,5},{8,10},{10,8},{9,1... | collective-permute-start | bytes 884744 | tf_op jit(solution)/shard_map/ppermute | solution.py:578
  31.9 13.1 %copy-start.1 = (bf16[144,1024]{1,0:T(8,128)(2,1)S(1)}, bf16[144,1024]{1,0:T(8,128)(2,1)}, u32[]{:S(2)}) copy-start(bf16[144,1024]{1,0:T(8,128)(2,1)} %shard_map.132.x0_any) | copy-start | bytes 884740
  31.9 24.2 %all-to-all-start.1 = ((bf16[8,544,128]{2,1,0:T(8,128)(2,1)}), bf16[8,544,128]{2,1,0:T(8,128)(2,1)S(1)}, u32[]{:S(2)}, u32[]{:S(2)}) async-start(bf16[8,544,128]{2,1,0:T(8,128)(2,1)} %shard_map.133), calls=%async_computation.1 | async-start | bytes 2228224 | tf_op jit(solution)/shard_map/all_to_all | solution.py:559
  37.1 8.7 %copy-start.14 = (bf16[1024,128]{1,0:T(8,128)(2,1)S(1)}, bf16[1024,128]{1,0:T(8,128)(2,1)}, u32[]{:S(2)}) copy-start(bf16[1024,128]{1,0:T(8,128)(2,1)} %wp_ref.1) | copy-start | bytes 786436
  37.1 8.7 %copy-start.15 = (f32[1024]{0:T(1024)S(1)}, f32[1024]{0:T(1024)}, u32[]{:S(2)}) copy-start(f32[1024]{0:T(1024)} %param.19) | copy-start | bytes 12292
  37.1 8.4 %copy-start.12 = (bf16[144,1024]{1,0:T(8,128)(2,1)}, bf16[144,1024]{1,0:T(8,128)(2,1)S(1)}, u32[]{:S(2)}) copy-start(bf16[144,1024]{1,0:T(8,128)(2,1)S(1)} %collective-permute-done.1.x2_any) | copy-start | bytes 884740
  37.1 7.9 %collective-permute-start.2 = (bf16[144,1024]{1,0:T(8,128)(2,1)S(1)}, bf16[144,1024]{1,0:T(8,128)(2,1)S(1)}, u32[]{:S(2)}, u32[]{:S(2)}) collective-permute-start(bf16[144,1024]{1,0:T(8,128)(2,1)S(1)} %collective-permute-done.1.x2_any), channel_id=1, source_target_pairs={{0,1},{1,0},{2,3},{3,2},{4,5},{5,4},{6,7},{7,6},{8,9},{9,8},{10,11... | collective-permute-start | bytes 884744 | tf_op jit(solution)/shard_map/ppermute | solution.py:583
  45.0 0.8 copy-start.13
  56.1 51.2 %copy-start.7 = (bf16[8,128,512]{2,1,0:T(8,128)(2,1)S(1)}, bf16[8,128,512]{2,1,0:T(8,128)(2,1)}, u32[]{:S(2)}) copy-start(bf16[8,128,512]{2,1,0:T(8,128)(2,1)} %get-tuple-element.39.pcol_ref) | copy-start | bytes 3145732
  56.1 51.2 %copy-start.9 = (bf16[512,512]{1,0:T(8,128)(2,1)S(1)}, bf16[512,512]{1,0:T(8,128)(2,1)}, u32[]{:S(2)}) copy-start(bf16[512,512]{1,0:T(8,128)(2,1)} %get-tuple-element.36.k_ref) | copy-start | bytes 1572868
  56.1 51.2 %copy-start.10 = (bf16[512,512]{1,0:T(8,128)(2,1)S(1)}, bf16[512,512]{1,0:T(8,128)(2,1)}, u32[]{:S(2)}) copy-start(bf16[512,512]{1,0:T(8,128)(2,1)} %get-tuple-element.35.v_ref) | copy-start | bytes 1572868
  56.1 51.2 %copy-start.11 = (bf16[512,512]{1,0:T(8,128)(2,1)S(1)}, bf16[512,512]{1,0:T(8,128)(2,1)}, u32[]{:S(2)}) copy-start(bf16[512,512]{1,0:T(8,128)(2,1)} %get-tuple-element.34.att_ref) | copy-start | bytes 1572868
  90.3 17.0 %copy-start = (f32[512,1024]{1,0:T(8,128)S(1)}, f32[512,1024]{1,0:T(8,128)}, u32[]{:S(2)}) copy-start(f32[512,1024]{1,0:T(8,128)} %get-tuple-element.33.unit_ref) | copy-start | bytes 6291460
  90.3 17.0 %copy-start.2 = (bf16[1024,512]{1,0:T(8,128)(2,1)S(1)}, bf16[1024,512]{1,0:T(8,128)(2,1)}, u32[]{:S(2)}) copy-start(bf16[1024,512]{1,0:T(8,128)(2,1)} %wq_ref.1) | copy-start | bytes 3145732
  90.3 17.1 %copy-start.3 = (bf16[1024,512]{1,0:T(8,128)(2,1)S(1)}, bf16[1024,512]{1,0:T(8,128)(2,1)}, u32[]{:S(2)}) copy-start(bf16[1024,512]{1,0:T(8,128)(2,1)} %wk_ref.1) | copy-start | bytes 3145732
  90.3 17.1 %copy-start.4 = (bf16[1024,512]{1,0:T(8,128)(2,1)S(1)}, bf16[1024,512]{1,0:T(8,128)(2,1)}, u32[]{:S(2)}) copy-start(bf16[1024,512]{1,0:T(8,128)(2,1)} %wv_ref.1) | copy-start | bytes 3145732
  90.3 17.1 %copy-start.5 = (bf16[512,1024]{1,0:T(8,128)(2,1)S(1)}, bf16[512,1024]{1,0:T(8,128)(2,1)}, u32[]{:S(2)}) copy-start(bf16[512,1024]{1,0:T(8,128)(2,1)} %wo_ref.1) | copy-start | bytes 3145732
  90.3 17.1 %copy-start.6 = (bf16[8,128,512]{2,1,0:T(8,128)(2,1)S(1)}, bf16[8,128,512]{2,1,0:T(8,128)(2,1)}, u32[]{:S(2)}) copy-start(bf16[8,128,512]{2,1,0:T(8,128)(2,1)} %get-tuple-element.38.prow_ref) | copy-start | bytes 3145732
  90.3 17.1 %copy-start.8 = (bf16[512,512]{1,0:T(8,128)(2,1)S(1)}, bf16[512,512]{1,0:T(8,128)(2,1)}, u32[]{:S(2)}) copy-start(bf16[512,512]{1,0:T(8,128)(2,1)} %get-tuple-element.37.q_ref) | copy-start | bytes 1572868
  92.8 5.1 %collective-permute-start.3 = (f32[520,128]{1,0:T(8,128)S(1)}, f32[520,128]{1,0:T(8,128)S(1)}, u32[]{:S(2)}, u32[]{:S(2)}) collective-permute-start(f32[520,128]{1,0:T(8,128)S(1)} %shard_map.137.own_ref), channel_id=1, source_target_pairs={{0,1},{1,0},{2,3},{3,2},{4,5},{5,4},{6,7},{7,6},{8,9},{9,8},{10,11... | collective-permute-start | bytes 798728 | tf_op jit(solution)/shard_map/ppermute | solution.py:592
  97.9 9.4 %collective-permute-start.4 = (bf16[544,128]{1,0:T(8,128)(2,1)S(1)}, bf16[544,128]{1,0:T(8,128)(2,1)S(1)}, u32[]{:S(2)}, u32[]{:S(2)}) collective-permute-start(bf16[544,128]{1,0:T(8,128)(2,1)S(1)} %get-tuple-element.30), channel_id=1, source_target_pairs={{0,2},{2,0},{1,3},{3,1},{4,6},{6,4},{5,7},{7,5},{8,10},{10,8},{9,1... | collective-permute-start | bytes 417800 | tf_op jit(solution)/shard_map/ppermute | solution.py:593

commit v7 on v6

--- a/solution.py
+++ b/solution.py
@@ -92,19 +92,11 @@
     return jax.ShapeDtypeStruct(dims, kind)
 
 
-def pack_hidden_kernel(hidden_ref, skip_ref, own_out):
-    own_out[:ROWS, :] = hidden_ref[...]
+def pack_kernel(pos_ref, queries_ref, mask_ref, skip_ref, hidden_any, query_out, own_out, sems):
+    moves = Moves(sems)
+    copy = moves.start(hidden_any, own_out.at[pl.ds(0, ROWS)])
     own_out[ROWS:, :] = jnp.zeros((AUX, D), bf16)
     own_out[ROWS:, :ROWS] = jnp.broadcast_to(skip_ref[...], (AUX, ROWS)).astype(f32).astype(bf16)
-
-
-def pack_hidden(hidden, doc_keep):
-    return call(pack_hidden_kernel, shape((ROWS + AUX, D), bf16), [BLOCK] * 2, limit=56)(
-        hidden, doc_keep[None]
-    )
-
-
-def pack_query_kernel(pos_ref, queries_ref, mask_ref, query_out):
     q = queries_ref[...].astype(f32)
     qn = q * lax.rsqrt(jnp.sum(q * q, -1, keepdims=True) + 1e-06)
     repeat = (iota((QLEN, E), 1) % QLEN == iota((QLEN, E), 0)).astype(bf16)
@@ -114,16 +106,18 @@
     tail = jnp.where(row == 0, weights, jnp.where(row == 1, target, 0.0))
     packet = jnp.concatenate([qn, tail], 0).astype(bf16)
     query_out[...] = jnp.broadcast_to(packet[None], (LINE, QLEN + TAIL, E))
-
-
-def pack_query(positive, queries, query_mask):
+    copy.wait()
+
+
+def pack(positive, queries, query_mask, hidden, doc_keep):
     return call(
-        pack_query_kernel,
-        shape((LINE, QLEN + TAIL, E), bf16),
-        [BLOCK] * 3,
-        VMEM,
+        pack_kernel,
+        (shape((LINE, QLEN + TAIL, E), bf16), shape((ROWS + AUX, D), bf16)),
+        [BLOCK] * 4 + [ANY],
+        (VMEM, VMEM),
+        [pltpu.SemaphoreType.DMA((1,))],
         limit=56,
-    )(positive[None], queries[0], query_mask)
+    )(positive[None], queries[0], query_mask, doc_keep[None], hidden)
 
 
 def repack_kernel(line_ref, after_ref, out_ref):
@@ -573,10 +567,10 @@
     query_mask,
     positive,
 ):
-    own = pack_hidden(hidden, doc_keep)
+    query_send, own = pack(positive, queries, query_mask, hidden, doc_keep)
     by_core = lax.ppermute(own, "core", SWAP)
     by_yhi = lax.ppermute(own, "yhi", SWAP)
-    line = spread(pack_query(positive, queries, query_mask), "z")
+    line = spread(query_send, "z")
     packed = repack(line, by_core)
     plane = spread(packed, ("ylo", "x"))
     by_yhi, _ = lax.optimization_barrier((by_yhi, packed))

time: 113 us -> 104 us (0.920)
  blocking collectives: 32.3 us -> 23.3 us
  waiting for transfers between devices: 8.25 us -> 9.95 us
    all_to_all x1, blocking collectives: 32.3 us -> 23.3 us  [spread(): return lax.all_to_all(x, axes, 0, 0)]
    all_to_all x2, waiting for transfers between devices: 2.83 us -> 4.51 us  [spread(): return lax.all_to_all(x, axes, 0, 0)]
    ppermute x1, starting transfers between devices: 5.66 us -> 4.52 us  [body(): got = lax.ppermute(half, 'yhi', SWAP)]
    pallas_call x2 -> x1, Pallas kernels: 3.2 us -> 2.44 us  [pack(): call(pack_kernel, (shape((LINE, QLEN + TAIL, E), bf16), shape((ROWS + AUX...]
  transfers between devices with their start and end apart: 7 -> 7, of which waited for: 4 -> 4; matrix products, arithmetic and copies ran while one was open for 0% -> 0% of each run, Pallas kernels for 12% -> 11%
where the time goes in v7:
time: 104 us
  starting transfers between devices  43.8 us (42%)
  Pallas kernels  24.2 us (23%)
  blocking collectives  23.3 us (22%)
  waiting for transfers between devices  9.95 us (10%)
  between operations  2.35 us (2%)
    all_to_all x1, blocking collectives, spread(): return lax.all_to_all(x, axes, 0, 0)  23.3 us
    all_to_all x2, starting transfers between devices, spread(): return lax.all_to_all(x, axes, 0, 0)  20.9 us
    pallas_call x1, Pallas kernels, forward(): call(forward_kernel, outs, [ANY] * 6 + [HBM] * 6, tuple((HBM for _ in out...  10.3 us
    ppermute x1, starting transfers between devices, body(): by_both = lax.ppermute(by_yhi, 'core', SWAP)  6.69 us
    pallas_call x1, Pallas kernels, backward(): call(backward_kernel, (shape((ROWS, D), bf16), shape((1,), f32)), [VMEM]...  5.55 us
    ppermute x1, starting transfers between devices, body(): by_yhi = lax.ppermute(own, 'yhi', SWAP)  4.82 us
    ppermute x1, starting transfers between devices, body(): got = lax.ppermute(half, 'yhi', SWAP)  4.52 us
    all_to_all x2, waiting for transfers between devices, spread(): return lax.all_to_all(x, axes, 0, 0)  4.51 us
  transfers between devices with their start and end apart: 7, of which 4 were waited for; matrix products, arithmetic and copies ran while one was open for 0% of the time, Pallas kernels for 11%

profile of v7, /device:TPU:1, one launch (start us, length us, event | category | flops | bytes accessed | tf_op | source)
XLA Modules:
  0.0 103.9 jit_solution(2088915262272378789)
XLA Ops:
  1.3 2.4 %shard_map.131 = (bf16[16,40,128]{2,1,0:T(8,128)(2,1)}, bf16[144,1024]{1,0:T(8,128)(2,1)}) custom-call(s32[1,1]{1,0:T(1,128)} %bitcast.9.pos_ref, bf16[32,128]{1,0:T(8,128)(2,1)} %bitcast.14, bf16[1,32]{1,0:T(2,128)(2,1)} %mask_ref.1, s32[1,128]{1,0:T(1,128)} %bitcast.15, bf16[128,1024]{1,0:T(8,128)(2,1)} %hidden_any.1), custom_call_target="tpu_custom_call" | custom-call | bytes 4194304 | tf_op jit(solution)/shard_map/pallas_call | solution.py:113
  3.7 15.8 %all-to-all-start = ((bf16[16,40,128]{2,1,0:T(8,128)(2,1)}), bf16[16,40,128]{2,1,0:T(8,128)(2,1)S(1)}, u32[]{:S(2)}, u32[]{:S(2)}) async-start(bf16[16,40,128]{2,1,0:T(8,128)(2,1)} %get-tuple-element.24), calls=%async_computation | async-start | bytes 327680 | tf_op jit(solution)/shard_map/all_to_all | solution.py:553
  19.5 2.9 %collective-permute-start = (bf16[144,1024]{1,0:T(8,128)(2,1)}, bf16[144,1024]{1,0:T(8,128)(2,1)S(1)}, u32[]{:S(2)}, u32[]{:S(2)}) collective-permute-start(bf16[144,1024]{1,0:T(8,128)(2,1)} %get-tuple-element.25.x0_any), channel_id=1, source_target_pairs={{0,1},{1,0},{2,3},{3,2},{4,5},{5,4},{6,7},{7,6},{8,9},{9,8},{10,11... | collective-permute-start | bytes 884744 | tf_op jit(solution)/shard_map/ppermute | solution.py:571
  22.4 4.8 %collective-permute-start.1 = (bf16[144,1024]{1,0:T(8,128)(2,1)}, bf16[144,1024]{1,0:T(8,128)(2,1)S(1)}, u32[]{:S(2)}, u32[]{:S(2)}) collective-permute-start(bf16[144,1024]{1,0:T(8,128)(2,1)} %get-tuple-element.25.x0_any), channel_id=1, source_target_pairs={{0,2},{2,0},{1,3},{3,1},{4,6},{6,4},{5,7},{7,5},{8,10},{10,8},{9,1... | collective-permute-start | bytes 884744 | tf_op jit(solution)/shard_map/ppermute | solution.py:572
  27.2 0.0 collective-permute-done.after_ref.x1_any
  27.2 4.5 %all-to-all-done.line_ref = bf16[16,40,128]{2,1,0:T(8,128)(2,1)S(1)} async-done(((bf16[16,40,128]{2,1,0:T(8,128)(2,1)}), bf16[16,40,128]{2,1,0:T(8,128)(2,1)S(1)}, u32[]{:S(2)}, u32[]{:S(2)}) %all-to-all-start) | async-done | bytes 163872 | tf_op jit(solution)/shard_map/all_to_all | solution.py:553
  31.7 1.2 %shard_map.132 = bf16[8,544,128]{2,1,0:T(8,128)(2,1)} custom-call(bf16[16,40,128]{2,1,0:T(8,128)(2,1)S(1)} %all-to-all-done.line_ref, bf16[144,1024]{1,0:T(8,128)(2,1)S(1)} %collective-permute-done.after_ref.x1_any), custom_call_target="tpu_custom_call" | custom-call | bytes 4194304 | tf_op jit(solution)/shard_map/pallas_call | solution.py:133
  32.9 0.0 copy-start.11
  32.9 5.2 %all-to-all-start.1 = ((bf16[8,544,128]{2,1,0:T(8,128)(2,1)}), bf16[8,544,128]{2,1,0:T(8,128)(2,1)S(1)}, u32[]{:S(2)}, u32[]{:S(2)}) async-start(bf16[8,544,128]{2,1,0:T(8,128)(2,1)} %shard_map.132), calls=%async_computation.1 | async-start | bytes 2228224 | tf_op jit(solution)/shard_map/all_to_all | solution.py:553
  38.0 0.0 copy-start.14
  38.0 0.0 copy-start.15
  38.1 0.0 collective-permute-done.1.x2_any
  38.1 0.0 copy-start.12
  38.1 6.7 %collective-permute-start.2 = (bf16[144,1024]{1,0:T(8,128)(2,1)S(1)}, bf16[144,1024]{1,0:T(8,128)(2,1)S(1)}, u32[]{:S(2)}, u32[]{:S(2)}) collective-permute-start(bf16[144,1024]{1,0:T(8,128)(2,1)S(1)} %collective-permute-done.1.x2_any), channel_id=1, source_target_pairs={{0,1},{1,0},{2,3},{3,2},{4,5},{5,4},{6,7},{7,6},{8,9},{9,8},{10,11... | collective-permute-start | bytes 884744 | tf_op jit(solution)/shard_map/ppermute | solution.py:577
  45.4 0.5 collective-permute-done.2.x3_any
  46.0 0.0 copy-done.11
  46.0 0.0 copy-start.13
  46.0 0.4 shard_map.133
  46.4 0.0 copy-done.12
  46.4 0.3 copy-done.13
  46.7 0.0 copy-done.14
  46.7 0.0 copy-done.15
  46.7 10.3 %shard_map.134 = (bf16[512,512]{1,0:T(8,128)(2,1)}, bf16[512,512]{1,0:T(8,128)(2,1)}, bf16[512,512]{1,0:T(8,128)(2,1)}, bf16[512,512]{1,0:T(8,128)(2,1)}, bf16[8...) custom-call(bf16[512,128]{1,0:T(8,128)(2,1)S(1)} %get-tuple-element., ...), custom_call_target="tpu_custom_call" | custom-call | flops 6000000000 | bytes 4194304 | tf_op jit(solution)/shard_map/pallas_call | solution.py:320
  57.0 0.0 all-to-all-done.1.plane_ref
  57.1 0.0 copy-start.6
  57.1 0.0 copy-start.8
  57.1 0.0 copy-start.9
  57.1 0.0 copy-start.10
  57.1 1.8 %shard_map.135 = (f32[128,128]{1,0:T(8,128)S(1)}, f32[32,128]{1,0:T(8,128)S(1)}, f32[32,128]{1,0:T(8,128)S(1)}) custom-call(bf16[8,544,128]{2,1,0:T(8,128)(2,1)S(1)} %all-to-all-done.1.plane_ref, bf16[1024,128]{1,0:T(8,128)(2,1)S(1)} %get-tuple-element.29.embed_ref), custom_call_target="tpu_custom_call" | custom-call | flops 1000000000 | bytes 4194304 | tf_op jit(solution)/shard_map/pallas_call | solution.py:358
  58.9 23.3 %all_to_all.21 = f32[128,1,128]{2,1,0:T(1,128)S(1)} all-to-all(f32[128,1,128]{2,1,0:T(1,128)S(1)} %bitcast.11), channel_id=1, replica_groups=mesh['z'=16,'ylo'=2,'x'=4,'yhi'=2,'core'=2] {'z','ylo','x'}, dimensions={0} | all-to-all | bytes 131072 | tf_op jit(solution)/shard_map/all_to_all | solution.py:553
  82.2 0.0 copy-start
  82.2 0.0 copy-start.1
  82.2 0.0 copy-start.2
  82.2 0.0 copy-start.3
  82.2 0.0 copy-start.4
  82.2 0.0 copy-start.5
  82.2 0.0 copy-start.7
  82.2 2.4 %shard_map.136.own_ref = f32[520,128]{1,0:T(8,128)S(1)} custom-call(f32[128,128]{1,0:T(8,128)S(1)} %bitcast.10, f32[32,128]{1,0:T(8,128)S(1)} %get-tuple-element.31.sums_ref, f32[32,128]{1,0:T(8,128)S(1)} %get-tuple-element.32.weight_ref, bf16[8,544,128]{2,1,0:T(8,128)(2,1)S(1)} %all-to-all-done.1.plane_ref, bf16[1024,128]{1,0:T(8,128)(2,1)S(1)} %get-tuple-element.29.embed_ref), custom_call_target="tpu_custom_call" | custom-call | flops 2000000000 | bytes 4194304 | tf_op jit(solution)/shard_map/pallas_call | solution.py:405
  84.7 3.9 %collective-permute-start.3 = (f32[520,128]{1,0:T(8,128)S(1)}, f32[520,128]{1,0:T(8,128)S(1)}, u32[]{:S(2)}, u32[]{:S(2)}) collective-permute-start(f32[520,128]{1,0:T(8,128)S(1)} %shard_map.136.own_ref), channel_id=1, source_target_pairs={{0,1},{1,0},{2,3},{3,2},{4,5},{5,4},{6,7},{7,6},{8,9},{9,8},{10,11... | collective-permute-start | bytes 798728 | tf_op jit(solution)/shard_map/ppermute | solution.py:586
  88.6 1.1 %collective-permute-done.3.got_ref = f32[520,128]{1,0:T(8,128)S(1)} collective-permute-done((f32[520,128]{1,0:T(8,128)S(1)}, f32[520,128]{1,0:T(8,128)S(1)}, u32[]{:S(2)}, u32[]{:S(2)}) %collective-permute-start.3) | collective-permute-done | bytes 266272 | tf_op jit(solution)/shard_map/ppermute | solution.py:586
  89.8 4.5 %collective-permute-start.4 = (bf16[544,128]{1,0:T(8,128)(2,1)S(1)}, bf16[544,128]{1,0:T(8,128)(2,1)S(1)}, u32[]{:S(2)}, u32[]{:S(2)}) collective-permute-start(bf16[544,128]{1,0:T(8,128)(2,1)S(1)} %get-tuple-element.34), channel_id=1, source_target_pairs={{0,2},{2,0},{1,3},{3,1},{4,6},{6,4},{5,7},{7,5},{8,10},{10,8},{9,1... | collective-permute-start | bytes 417800 | tf_op jit(solution)/shard_map/ppermute | solution.py:587
  94.3 3.8 %collective-permute-done.4.got_ref = bf16[544,128]{1,0:T(8,128)(2,1)S(1)} collective-permute-done((bf16[544,128]{1,0:T(8,128)(2,1)S(1)}, bf16[544,128]{1,0:T(8,128)(2,1)S(1)}, u32[]{:S(2)}, u32[]{:S(2)}) %collective-permute-start.4) | collective-permute-done | bytes 139296 | tf_op jit(solution)/shard_map/ppermute | solution.py:587
  98.1 0.0 copy-done.6
  98.1 0.0 copy-done.8
  98.1 0.0 copy-done.9
  98.1 0.0 copy-done.10
  98.1 0.0 copy-done
  98.1 0.0 copy-done.1
  98.1 0.0 copy-done.2
  98.1 0.0 copy-done.3
  98.1 0.0 copy-done.4
  98.1 0.0 copy-done.5
  98.2 0.0 copy-done.7
  98.2 5.6 %shard_map.138 = (bf16[128,1024]{1,0:T(8,128)(2,1)}, f32[1]{0:T(128)}) custom-call(f32[520,128]{1,0:T(8,128)S(1)} %get-tuple-element.33.sum_ref, bf16[544,128]{1,0:T(8,128)(2,1)S(1)} %collective-permute-done.4.got_ref, f32[512,128]{1,0:T(8,128)S(1)} %get-tuple-element.35.proj_ref, bf16[1024,128]{1,0:T(8,128)(2,1)S(1)} %copy-done.14, ...), custom_call_target="tpu_custom_call" | custom-call | flops 3000000000 | bytes 4194304 | tf_op jit(solution)/shard_map/pallas_call | solution.py:531
  (1 shorter events, 0.0 us)
Async XLA Ops:
  3.7 28.0 %all-to-all-start = ((bf16[16,40,128]{2,1,0:T(8,128)(2,1)}), bf16[16,40,128]{2,1,0:T(8,128)(2,1)S(1)}, u32[]{:S(2)}, u32[]{:S(2)}) async-start(bf16[16,40,128]{2,1,0:T(8,128)(2,1)} %get-tuple-element.24), calls=%async_computation | async-start | bytes 327680 | tf_op jit(solution)/shard_map/all_to_all | solution.py:553
  19.5 7.7 %collective-permute-start = (bf16[144,1024]{1,0:T(8,128)(2,1)}, bf16[144,1024]{1,0:T(8,128)(2,1)S(1)}, u32[]{:S(2)}, u32[]{:S(2)}) collective-permute-start(bf16[144,1024]{1,0:T(8,128)(2,1)} %get-tuple-element.25.x0_any), channel_id=1, source_target_pairs={{0,1},{1,0},{2,3},{3,2},{4,5},{5,4},{6,7},{7,6},{8,9},{9,8},{10,11... | collective-permute-start | bytes 884744 | tf_op jit(solution)/shard_map/ppermute | solution.py:571
  22.4 15.7 %collective-permute-start.1 = (bf16[144,1024]{1,0:T(8,128)(2,1)}, bf16[144,1024]{1,0:T(8,128)(2,1)S(1)}, u32[]{:S(2)}, u32[]{:S(2)}) collective-permute-start(bf16[144,1024]{1,0:T(8,128)(2,1)} %get-tuple-element.25.x0_any), channel_id=1, source_target_pairs={{0,2},{2,0},{1,3},{3,1},{4,6},{6,4},{5,7},{7,5},{8,10},{10,8},{9,1... | collective-permute-start | bytes 884744 | tf_op jit(solution)/shard_map/ppermute | solution.py:572
  32.9 13.1 %copy-start.11 = (bf16[144,1024]{1,0:T(8,128)(2,1)S(1)}, bf16[144,1024]{1,0:T(8,128)(2,1)}, u32[]{:S(2)}) copy-start(bf16[144,1024]{1,0:T(8,128)(2,1)} %get-tuple-element.25.x0_any) | copy-start | bytes 884740
  32.9 24.2 %all-to-all-start.1 = ((bf16[8,544,128]{2,1,0:T(8,128)(2,1)}), bf16[8,544,128]{2,1,0:T(8,128)(2,1)S(1)}, u32[]{:S(2)}, u32[]{:S(2)}) async-start(bf16[8,544,128]{2,1,0:T(8,128)(2,1)} %shard_map.132), calls=%async_computation.1 | async-start | bytes 2228224 | tf_op jit(solution)/shard_map/all_to_all | solution.py:553
  38.0 8.7 %copy-start.14 = (bf16[1024,128]{1,0:T(8,128)(2,1)S(1)}, bf16[1024,128]{1,0:T(8,128)(2,1)}, u32[]{:S(2)}) copy-start(bf16[1024,128]{1,0:T(8,128)(2,1)} %wp_ref.1) | copy-start | bytes 786436
  38.0 8.7 %copy-start.15 = (f32[1024]{0:T(1024)S(1)}, f32[1024]{0:T(1024)}, u32[]{:S(2)}) copy-start(f32[1024]{0:T(1024)} %param.19) | copy-start | bytes 12292
  38.1 8.4 %copy-start.12 = (bf16[144,1024]{1,0:T(8,128)(2,1)}, bf16[144,1024]{1,0:T(8,128)(2,1)S(1)}, u32[]{:S(2)}) copy-start(bf16[144,1024]{1,0:T(8,128)(2,1)S(1)} %collective-permute-done.1.x2_any) | copy-start | bytes 884740
  38.1 7.9 %collective-permute-start.2 = (bf16[144,1024]{1,0:T(8,128)(2,1)S(1)}, bf16[144,1024]{1,0:T(8,128)(2,1)S(1)}, u32[]{:S(2)}, u32[]{:S(2)}) collective-permute-start(bf16[144,1024]{1,0:T(8,128)(2,1)S(1)} %collective-permute-done.1.x2_any), channel_id=1, source_target_pairs={{0,1},{1,0},{2,3},{3,2},{4,5},{5,4},{6,7},{7,6},{8,9},{9,8},{10,11... | collective-permute-start | bytes 884744 | tf_op jit(solution)/shard_map/ppermute | solution.py:577
  46.0 0.8 copy-start.13
  57.1 41.0 %copy-start.6 = (bf16[8,128,512]{2,1,0:T(8,128)(2,1)S(1)}, bf16[8,128,512]{2,1,0:T(8,128)(2,1)}, u32[]{:S(2)}) copy-start(bf16[8,128,512]{2,1,0:T(8,128)(2,1)} %get-tuple-element.43.pcol_ref) | copy-start | bytes 3145732
  57.1 41.0 %copy-start.8 = (bf16[512,512]{1,0:T(8,128)(2,1)S(1)}, bf16[512,512]{1,0:T(8,128)(2,1)}, u32[]{:S(2)}) copy-start(bf16[512,512]{1,0:T(8,128)(2,1)} %get-tuple-element.40.k_ref) | copy-start | bytes 1572868
  57.1 41.0 %copy-start.9 = (bf16[512,512]{1,0:T(8,128)(2,1)S(1)}, bf16[512,512]{1,0:T(8,128)(2,1)}, u32[]{:S(2)}) copy-start(bf16[512,512]{1,0:T(8,128)(2,1)} %get-tuple-element.39.v_ref) | copy-start | bytes 1572868
  57.1 41.0 %copy-start.10 = (bf16[512,512]{1,0:T(8,128)(2,1)S(1)}, bf16[512,512]{1,0:T(8,128)(2,1)}, u32[]{:S(2)}) copy-start(bf16[512,512]{1,0:T(8,128)(2,1)} %get-tuple-element.38.att_ref) | copy-start | bytes 1572868
  82.2 15.9 %copy-start = (f32[512,1024]{1,0:T(8,128)S(1)}, f32[512,1024]{1,0:T(8,128)}, u32[]{:S(2)}) copy-start(f32[512,1024]{1,0:T(8,128)} %get-tuple-element.37.unit_ref) | copy-start | bytes 6291460
  82.2 15.9 %copy-start.1 = (bf16[1024,512]{1,0:T(8,128)(2,1)S(1)}, bf16[1024,512]{1,0:T(8,128)(2,1)}, u32[]{:S(2)}) copy-start(bf16[1024,512]{1,0:T(8,128)(2,1)} %wq_ref.1) | copy-start | bytes 3145732
  82.2 15.9 %copy-start.2 = (bf16[1024,512]{1,0:T(8,128)(2,1)S(1)}, bf16[1024,512]{1,0:T(8,128)(2,1)}, u32[]{:S(2)}) copy-start(bf16[1024,512]{1,0:T(8,128)(2,1)} %wk_ref.1) | copy-start | bytes 3145732
  82.2 15.9 %copy-start.3 = (bf16[1024,512]{1,0:T(8,128)(2,1)S(1)}, bf16[1024,512]{1,0:T(8,128)(2,1)}, u32[]{:S(2)}) copy-start(bf16[1024,512]{1,0:T(8,128)(2,1)} %wv_ref.1) | copy-start | bytes 3145732
  82.2 15.9 %copy-start.4 = (bf16[512,1024]{1,0:T(8,128)(2,1)S(1)}, bf16[512,1024]{1,0:T(8,128)(2,1)}, u32[]{:S(2)}) copy-start(bf16[512,1024]{1,0:T(8,128)(2,1)} %wo_ref.1) | copy-start | bytes 3145732
  82.2 15.9 %copy-start.5 = (bf16[8,128,512]{2,1,0:T(8,128)(2,1)S(1)}, bf16[8,128,512]{2,1,0:T(8,128)(2,1)}, u32[]{:S(2)}) copy-start(bf16[8,128,512]{2,1,0:T(8,128)(2,1)} %get-tuple-element.42.prow_ref) | copy-start | bytes 3145732
  82.2 15.9 %copy-start.7 = (bf16[512,512]{1,0:T(8,128)(2,1)S(1)}, bf16[512,512]{1,0:T(8,128)(2,1)}, u32[]{:S(2)}) copy-start(bf16[512,512]{1,0:T(8,128)(2,1)} %get-tuple-element.41.q_ref) | copy-start | bytes 1572868
  84.7 5.1 %collective-permute-start.3 = (f32[520,128]{1,0:T(8,128)S(1)}, f32[520,128]{1,0:T(8,128)S(1)}, u32[]{:S(2)}, u32[]{:S(2)}) collective-permute-start(f32[520,128]{1,0:T(8,128)S(1)} %shard_map.136.own_ref), channel_id=1, source_target_pairs={{0,1},{1,0},{2,3},{3,2},{4,5},{5,4},{6,7},{7,6},{8,9},{9,8},{10,11... | collective-permute-start | bytes 798728 | tf_op jit(solution)/shard_map/ppermute | solution.py:586
  89.8 8.3 %collective-permute-start.4 = (bf16[544,128]{1,0:T(8,128)(2,1)S(1)}, bf16[544,128]{1,0:T(8,128)(2,1)S(1)}, u32[]{:S(2)}, u32[]{:S(2)}) collective-permute-start(bf16[544,128]{1,0:T(8,128)(2,1)S(1)} %get-tuple-element.34), channel_id=1, source_target_pairs={{0,2},{2,0},{1,3},{3,1},{4,6},{6,4},{5,7},{7,5},{8,10},{10,8},{9,1... | collective-permute-start | bytes 417800 | tf_op jit(solution)/shard_map/ppermute | solution.py:587

commit v8 on v7

--- a/solution.py
+++ b/solution.py
@@ -92,9 +92,8 @@
     return jax.ShapeDtypeStruct(dims, kind)
 
 
-def pack_kernel(pos_ref, queries_ref, mask_ref, skip_ref, hidden_any, query_out, own_out, sems):
-    moves = Moves(sems)
-    copy = moves.start(hidden_any, own_out.at[pl.ds(0, ROWS)])
+def pack_kernel(pos_ref, queries_ref, mask_ref, skip_ref, hidden_ref, query_out, own_out):
+    own_out[:ROWS, :] = hidden_ref[...]
     own_out[ROWS:, :] = jnp.zeros((AUX, D), bf16)
     own_out[ROWS:, :ROWS] = jnp.broadcast_to(skip_ref[...], (AUX, ROWS)).astype(f32).astype(bf16)
     q = queries_ref[...].astype(f32)
@@ -106,16 +105,14 @@
     tail = jnp.where(row == 0, weights, jnp.where(row == 1, target, 0.0))
     packet = jnp.concatenate([qn, tail], 0).astype(bf16)
     query_out[...] = jnp.broadcast_to(packet[None], (LINE, QLEN + TAIL, E))
-    copy.wait()
 
 
 def pack(positive, queries, query_mask, hidden, doc_keep):
     return call(
         pack_kernel,
         (shape((LINE, QLEN + TAIL, E), bf16), shape((ROWS + AUX, D), bf16)),
-        [BLOCK] * 4 + [ANY],
+        [BLOCK] * 5,
         (VMEM, VMEM),
-        [pltpu.SemaphoreType.DMA((1,))],
         limit=56,
     )(positive[None], queries[0], query_mask, doc_keep[None], hidden)
 

time: 104 us -> 104 us (level)
  transfers between devices with their start and end apart: 7 -> 7, of which waited for: 4 -> 4; matrix products, arithmetic and copies ran while one was open for 0% -> 0% of each run, Pallas kernels for 11% -> 12%
where the time goes in v8:
time: 104 us; the launch traced here: 103 us
  starting transfers between devices  43.7 us (42%)
  Pallas kernels  23.6 us (23%)
  blocking collectives  23.3 us (22%)
  waiting for transfers between devices  9.95 us (10%)
  between operations  2.34 us (2%)
    all_to_all x1, blocking collectives, spread(): return lax.all_to_all(x, axes, 0, 0)  23.3 us
    all_to_all x2, starting transfers between devices, spread(): return lax.all_to_all(x, axes, 0, 0)  20.9 us
    pallas_call x1, Pallas kernels, forward(): call(forward_kernel, outs, [ANY] * 6 + [HBM] * 6, tuple((HBM for _ in out...  10.3 us
    ppermute x1, starting transfers between devices, body(): by_both = lax.ppermute(by_yhi, 'core', SWAP)  6.69 us
    pallas_call x1, Pallas kernels, backward(): call(backward_kernel, (shape((ROWS, D), bf16), shape((1,), f32)), [VMEM]...  5.55 us
    ppermute x1, starting transfers between devices, body(): by_yhi = lax.ppermute(own, 'yhi', SWAP)  4.82 us
    ppermute x1, starting transfers between devices, body(): got = lax.ppermute(half, 'yhi', SWAP)  4.52 us
    all_to_all x2, waiting for transfers between devices, spread(): return lax.all_to_all(x, axes, 0, 0)  4.51 us
  transfers between devices with their start and end apart: 7, of which 4 were waited for; matrix products, arithmetic and copies ran while one was open for 0% of the time, Pallas kernels for 12%

profile of v8, /device:TPU:1, one launch (start us, length us, event | category | flops | bytes accessed | tf_op | source)
XLA Modules:
  0.0 103.2 jit_solution(13325864497822592847)
XLA Ops:
  1.3 1.8 %shard_map.131 = (bf16[16,40,128]{2,1,0:T(8,128)(2,1)}, bf16[144,1024]{1,0:T(8,128)(2,1)}) custom-call(s32[1,1]{1,0:T(1,128)} %bitcast.9.pos_ref, bf16[32,128]{1,0:T(8,128)(2,1)} %bitcast.14, bf16[1,32]{1,0:T(2,128)(2,1)} %mask_ref.1, s32[1,128]{1,0:T(1,128)} %bitcast.15, bf16[128,1024]{1,0:T(8,128)(2,1)} %hidden_ref.1), custom_call_target="tpu_custom_call" | custom-call | bytes 4194304 | tf_op jit(solution)/shard_map/pallas_call | solution.py:111
  3.1 15.7 %all-to-all-start = ((bf16[16,40,128]{2,1,0:T(8,128)(2,1)}), bf16[16,40,128]{2,1,0:T(8,128)(2,1)S(1)}, u32[]{:S(2)}, u32[]{:S(2)}) async-start(bf16[16,40,128]{2,1,0:T(8,128)(2,1)} %get-tuple-element.24), calls=%async_computation | async-start | bytes 327680 | tf_op jit(solution)/shard_map/all_to_all | solution.py:550
  18.8 2.9 %collective-permute-start = (bf16[144,1024]{1,0:T(8,128)(2,1)}, bf16[144,1024]{1,0:T(8,128)(2,1)S(1)}, u32[]{:S(2)}, u32[]{:S(2)}) collective-permute-start(bf16[144,1024]{1,0:T(8,128)(2,1)} %get-tuple-element.25.x0_any), channel_id=1, source_target_pairs={{0,1},{1,0},{2,3},{3,2},{4,5},{5,4},{6,7},{7,6},{8,9},{9,8},{10,11... | collective-permute-start | bytes 884744 | tf_op jit(solution)/shard_map/ppermute | solution.py:568
  21.7 4.8 %collective-permute-start.1 = (bf16[144,1024]{1,0:T(8,128)(2,1)}, bf16[144,1024]{1,0:T(8,128)(2,1)S(1)}, u32[]{:S(2)}, u32[]{:S(2)}) collective-permute-start(bf16[144,1024]{1,0:T(8,128)(2,1)} %get-tuple-element.25.x0_any), channel_id=1, source_target_pairs={{0,2},{2,0},{1,3},{3,1},{4,6},{6,4},{5,7},{7,5},{8,10},{10,8},{9,1... | collective-permute-start | bytes 884744 | tf_op jit(solution)/shard_map/ppermute | solution.py:569
  26.5 0.0 collective-permute-done.after_ref.x1_any
  26.6 4.5 %all-to-all-done.line_ref = bf16[16,40,128]{2,1,0:T(8,128)(2,1)S(1)} async-done(((bf16[16,40,128]{2,1,0:T(8,128)(2,1)}), bf16[16,40,128]{2,1,0:T(8,128)(2,1)S(1)}, u32[]{:S(2)}, u32[]{:S(2)}) %all-to-all-start) | async-done | bytes 163872 | tf_op jit(solution)/shard_map/all_to_all | solution.py:550
  31.1 1.2 %shard_map.132 = bf16[8,544,128]{2,1,0:T(8,128)(2,1)} custom-call(bf16[16,40,128]{2,1,0:T(8,128)(2,1)S(1)} %all-to-all-done.line_ref, bf16[144,1024]{1,0:T(8,128)(2,1)S(1)} %collective-permute-done.after_ref.x1_any), custom_call_target="tpu_custom_call" | custom-call | bytes 4194304 | tf_op jit(solution)/shard_map/pallas_call | solution.py:130
  32.2 0.0 copy-start.11
  32.2 5.2 %all-to-all-start.1 = ((bf16[8,544,128]{2,1,0:T(8,128)(2,1)}), bf16[8,544,128]{2,1,0:T(8,128)(2,1)S(1)}, u32[]{:S(2)}, u32[]{:S(2)}) async-start(bf16[8,544,128]{2,1,0:T(8,128)(2,1)} %shard_map.132), calls=%async_computation.1 | async-start | bytes 2228224 | tf_op jit(solution)/shard_map/all_to_all | solution.py:550
  37.4 0.0 copy-start.14
  37.4 0.0 copy-start.15
  37.4 0.0 collective-permute-done.1.x2_any
  37.4 0.0 copy-start.12
  37.4 6.7 %collective-permute-start.2 = (bf16[144,1024]{1,0:T(8,128)(2,1)S(1)}, bf16[144,1024]{1,0:T(8,128)(2,1)S(1)}, u32[]{:S(2)}, u32[]{:S(2)}) collective-permute-start(bf16[144,1024]{1,0:T(8,128)(2,1)S(1)} %collective-permute-done.1.x2_any), channel_id=1, source_target_pairs={{0,1},{1,0},{2,3},{3,2},{4,5},{5,4},{6,7},{7,6},{8,9},{9,8},{10,11... | collective-permute-start | bytes 884744 | tf_op jit(solution)/shard_map/ppermute | solution.py:574
  44.8 0.5 collective-permute-done.2.x3_any
  45.3 0.0 copy-done.11
  45.3 0.0 copy-start.13
  45.3 0.4 shard_map.133
  45.8 0.0 copy-done.12
  45.8 0.3 copy-done.13
  46.1 0.0 copy-done.14
  46.1 0.0 copy-done.15
  46.1 10.3 %shard_map.134 = (bf16[512,512]{1,0:T(8,128)(2,1)}, bf16[512,512]{1,0:T(8,128)(2,1)}, bf16[512,512]{1,0:T(8,128)(2,1)}, bf16[512,512]{1,0:T(8,128)(2,1)}, bf16[8...) custom-call(bf16[512,128]{1,0:T(8,128)(2,1)S(1)} %get-tuple-element., ...), custom_call_target="tpu_custom_call" | custom-call | flops 6000000000 | bytes 4194304 | tf_op jit(solution)/shard_map/pallas_call | solution.py:317
  56.4 0.0 all-to-all-done.1.plane_ref
  56.4 0.0 copy-start.6
  56.4 0.0 copy-start.8
  56.4 0.0 copy-start.9
  56.5 0.0 copy-start.10
  56.5 1.8 %shard_map.135 = (f32[128,128]{1,0:T(8,128)S(1)}, f32[32,128]{1,0:T(8,128)S(1)}, f32[32,128]{1,0:T(8,128)S(1)}) custom-call(bf16[8,544,128]{2,1,0:T(8,128)(2,1)S(1)} %all-to-all-done.1.plane_ref, bf16[1024,128]{1,0:T(8,128)(2,1)S(1)} %get-tuple-element.29.embed_ref), custom_call_target="tpu_custom_call" | custom-call | flops 1000000000 | bytes 4194304 | tf_op jit(solution)/shard_map/pallas_call | solution.py:355
  58.3 23.3 %all_to_all.21 = f32[128,1,128]{2,1,0:T(1,128)S(1)} all-to-all(f32[128,1,128]{2,1,0:T(1,128)S(1)} %bitcast.11), channel_id=1, replica_groups=mesh['z'=16,'ylo'=2,'x'=4,'yhi'=2,'core'=2] {'z','ylo','x'}, dimensions={0} | all-to-all | bytes 131072 | tf_op jit(solution)/shard_map/all_to_all | solution.py:550
  81.5 0.0 copy-start
  81.5 0.0 copy-start.1
  81.5 0.0 copy-start.2
  81.5 0.0 copy-start.3
  81.5 0.0 copy-start.4
  81.6 0.0 copy-start.5
  81.6 0.0 copy-start.7
  81.6 2.4 %shard_map.136.own_ref = f32[520,128]{1,0:T(8,128)S(1)} custom-call(f32[128,128]{1,0:T(8,128)S(1)} %bitcast.10, f32[32,128]{1,0:T(8,128)S(1)} %get-tuple-element.31.sums_ref, f32[32,128]{1,0:T(8,128)S(1)} %get-tuple-element.32.weight_ref, bf16[8,544,128]{2,1,0:T(8,128)(2,1)S(1)} %all-to-all-done.1.plane_ref, bf16[1024,128]{1,0:T(8,128)(2,1)S(1)} %get-tuple-element.29.embed_ref), custom_call_target="tpu_custom_call" | custom-call | flops 2000000000 | bytes 4194304 | tf_op jit(solution)/shard_map/pallas_call | solution.py:402
  84.0 3.9 %collective-permute-start.3 = (f32[520,128]{1,0:T(8,128)S(1)}, f32[520,128]{1,0:T(8,128)S(1)}, u32[]{:S(2)}, u32[]{:S(2)}) collective-permute-start(f32[520,128]{1,0:T(8,128)S(1)} %shard_map.136.own_ref), channel_id=1, source_target_pairs={{0,1},{1,0},{2,3},{3,2},{4,5},{5,4},{6,7},{7,6},{8,9},{9,8},{10,11... | collective-permute-start | bytes 798728 | tf_op jit(solution)/shard_map/ppermute | solution.py:583
  88.0 1.1 %collective-permute-done.3.got_ref = f32[520,128]{1,0:T(8,128)S(1)} collective-permute-done((f32[520,128]{1,0:T(8,128)S(1)}, f32[520,128]{1,0:T(8,128)S(1)}, u32[]{:S(2)}, u32[]{:S(2)}) %collective-permute-start.3) | collective-permute-done | bytes 266272 | tf_op jit(solution)/shard_map/ppermute | solution.py:583
  89.1 4.5 %collective-permute-start.4 = (bf16[544,128]{1,0:T(8,128)(2,1)S(1)}, bf16[544,128]{1,0:T(8,128)(2,1)S(1)}, u32[]{:S(2)}, u32[]{:S(2)}) collective-permute-start(bf16[544,128]{1,0:T(8,128)(2,1)S(1)} %get-tuple-element.34), channel_id=1, source_target_pairs={{0,2},{2,0},{1,3},{3,1},{4,6},{6,4},{5,7},{7,5},{8,10},{10,8},{9,1... | collective-permute-start | bytes 417800 | tf_op jit(solution)/shard_map/ppermute | solution.py:584
  93.7 3.8 %collective-permute-done.4.got_ref = bf16[544,128]{1,0:T(8,128)(2,1)S(1)} collective-permute-done((bf16[544,128]{1,0:T(8,128)(2,1)S(1)}, bf16[544,128]{1,0:T(8,128)(2,1)S(1)}, u32[]{:S(2)}, u32[]{:S(2)}) %collective-permute-start.4) | collective-permute-done | bytes 139296 | tf_op jit(solution)/shard_map/ppermute | solution.py:584
  97.4 0.0 copy-done.6
  97.4 0.0 copy-done.8
  97.4 0.0 copy-done.9
  97.4 0.0 copy-done.10
  97.4 0.0 copy-done
  97.5 0.0 copy-done.1
  97.5 0.0 copy-done.2
  97.5 0.0 copy-done.3
  97.5 0.0 copy-done.4
  97.5 0.0 copy-done.5
  97.5 0.0 copy-done.7
  97.5 5.5 %shard_map.138 = (bf16[128,1024]{1,0:T(8,128)(2,1)}, f32[1]{0:T(128)}) custom-call(f32[520,128]{1,0:T(8,128)S(1)} %get-tuple-element.33.sum_ref, bf16[544,128]{1,0:T(8,128)(2,1)S(1)} %collective-permute-done.4.got_ref, f32[512,128]{1,0:T(8,128)S(1)} %get-tuple-element.35.proj_ref, bf16[1024,128]{1,0:T(8,128)(2,1)S(1)} %copy-done.14, ...), custom_call_target="tpu_custom_call" | custom-call | flops 3000000000 | bytes 4194304 | tf_op jit(solution)/shard_map/pallas_call | solution.py:528
  (1 shorter events, 0.0 us)
Async XLA Ops:
  3.1 28.0 %all-to-all-start = ((bf16[16,40,128]{2,1,0:T(8,128)(2,1)}), bf16[16,40,128]{2,1,0:T(8,128)(2,1)S(1)}, u32[]{:S(2)}, u32[]{:S(2)}) async-start(bf16[16,40,128]{2,1,0:T(8,128)(2,1)} %get-tuple-element.24), calls=%async_computation | async-start | bytes 327680 | tf_op jit(solution)/shard_map/all_to_all | solution.py:550
  18.8 7.7 %collective-permute-start = (bf16[144,1024]{1,0:T(8,128)(2,1)}, bf16[144,1024]{1,0:T(8,128)(2,1)S(1)}, u32[]{:S(2)}, u32[]{:S(2)}) collective-permute-start(bf16[144,1024]{1,0:T(8,128)(2,1)} %get-tuple-element.25.x0_any), channel_id=1, source_target_pairs={{0,1},{1,0},{2,3},{3,2},{4,5},{5,4},{6,7},{7,6},{8,9},{9,8},{10,11... | collective-permute-start | bytes 884744 | tf_op jit(solution)/shard_map/ppermute | solution.py:568
  21.7 15.7 %collective-permute-start.1 = (bf16[144,1024]{1,0:T(8,128)(2,1)}, bf16[144,1024]{1,0:T(8,128)(2,1)S(1)}, u32[]{:S(2)}, u32[]{:S(2)}) collective-permute-start(bf16[144,1024]{1,0:T(8,128)(2,1)} %get-tuple-element.25.x0_any), channel_id=1, source_target_pairs={{0,2},{2,0},{1,3},{3,1},{4,6},{6,4},{5,7},{7,5},{8,10},{10,8},{9,1... | collective-permute-start | bytes 884744 | tf_op jit(solution)/shard_map/ppermute | solution.py:569
  32.2 13.1 %copy-start.11 = (bf16[144,1024]{1,0:T(8,128)(2,1)S(1)}, bf16[144,1024]{1,0:T(8,128)(2,1)}, u32[]{:S(2)}) copy-start(bf16[144,1024]{1,0:T(8,128)(2,1)} %get-tuple-element.25.x0_any) | copy-start | bytes 884740
  32.2 24.2 %all-to-all-start.1 = ((bf16[8,544,128]{2,1,0:T(8,128)(2,1)}), bf16[8,544,128]{2,1,0:T(8,128)(2,1)S(1)}, u32[]{:S(2)}, u32[]{:S(2)}) async-start(bf16[8,544,128]{2,1,0:T(8,128)(2,1)} %shard_map.132), calls=%async_computation.1 | async-start | bytes 2228224 | tf_op jit(solution)/shard_map/all_to_all | solution.py:550
  37.4 8.7 %copy-start.14 = (bf16[1024,128]{1,0:T(8,128)(2,1)S(1)}, bf16[1024,128]{1,0:T(8,128)(2,1)}, u32[]{:S(2)}) copy-start(bf16[1024,128]{1,0:T(8,128)(2,1)} %wp_ref.1) | copy-start | bytes 786436
  37.4 8.7 %copy-start.15 = (f32[1024]{0:T(1024)S(1)}, f32[1024]{0:T(1024)}, u32[]{:S(2)}) copy-start(f32[1024]{0:T(1024)} %param.19) | copy-start | bytes 12292
  37.4 8.4 %copy-start.12 = (bf16[144,1024]{1,0:T(8,128)(2,1)}, bf16[144,1024]{1,0:T(8,128)(2,1)S(1)}, u32[]{:S(2)}) copy-start(bf16[144,1024]{1,0:T(8,128)(2,1)S(1)} %collective-permute-done.1.x2_any) | copy-start | bytes 884740
  37.4 7.9 %collective-permute-start.2 = (bf16[144,1024]{1,0:T(8,128)(2,1)S(1)}, bf16[144,1024]{1,0:T(8,128)(2,1)S(1)}, u32[]{:S(2)}, u32[]{:S(2)}) collective-permute-start(bf16[144,1024]{1,0:T(8,128)(2,1)S(1)} %collective-permute-done.1.x2_any), channel_id=1, source_target_pairs={{0,1},{1,0},{2,3},{3,2},{4,5},{5,4},{6,7},{7,6},{8,9},{9,8},{10,11... | collective-permute-start | bytes 884744 | tf_op jit(solution)/shard_map/ppermute | solution.py:574
  45.3 0.8 copy-start.13
  56.4 41.0 %copy-start.6 = (bf16[8,128,512]{2,1,0:T(8,128)(2,1)S(1)}, bf16[8,128,512]{2,1,0:T(8,128)(2,1)}, u32[]{:S(2)}) copy-start(bf16[8,128,512]{2,1,0:T(8,128)(2,1)} %get-tuple-element.43.pcol_ref) | copy-start | bytes 3145732
  56.4 41.0 %copy-start.8 = (bf16[512,512]{1,0:T(8,128)(2,1)S(1)}, bf16[512,512]{1,0:T(8,128)(2,1)}, u32[]{:S(2)}) copy-start(bf16[512,512]{1,0:T(8,128)(2,1)} %get-tuple-element.40.k_ref) | copy-start | bytes 1572868
  56.4 41.0 %copy-start.9 = (bf16[512,512]{1,0:T(8,128)(2,1)S(1)}, bf16[512,512]{1,0:T(8,128)(2,1)}, u32[]{:S(2)}) copy-start(bf16[512,512]{1,0:T(8,128)(2,1)} %get-tuple-element.39.v_ref) | copy-start | bytes 1572868
  56.5 41.0 %copy-start.10 = (bf16[512,512]{1,0:T(8,128)(2,1)S(1)}, bf16[512,512]{1,0:T(8,128)(2,1)}, u32[]{:S(2)}) copy-start(bf16[512,512]{1,0:T(8,128)(2,1)} %get-tuple-element.38.att_ref) | copy-start | bytes 1572868
  81.5 15.9 %copy-start = (f32[512,1024]{1,0:T(8,128)S(1)}, f32[512,1024]{1,0:T(8,128)}, u32[]{:S(2)}) copy-start(f32[512,1024]{1,0:T(8,128)} %get-tuple-element.37.unit_ref) | copy-start | bytes 6291460
  81.5 15.9 %copy-start.1 = (bf16[1024,512]{1,0:T(8,128)(2,1)S(1)}, bf16[1024,512]{1,0:T(8,128)(2,1)}, u32[]{:S(2)}) copy-start(bf16[1024,512]{1,0:T(8,128)(2,1)} %wq_ref.1) | copy-start | bytes 3145732
  81.5 15.9 %copy-start.2 = (bf16[1024,512]{1,0:T(8,128)(2,1)S(1)}, bf16[1024,512]{1,0:T(8,128)(2,1)}, u32[]{:S(2)}) copy-start(bf16[1024,512]{1,0:T(8,128)(2,1)} %wk_ref.1) | copy-start | bytes 3145732
  81.5 15.9 %copy-start.3 = (bf16[1024,512]{1,0:T(8,128)(2,1)S(1)}, bf16[1024,512]{1,0:T(8,128)(2,1)}, u32[]{:S(2)}) copy-start(bf16[1024,512]{1,0:T(8,128)(2,1)} %wv_ref.1) | copy-start | bytes 3145732
  81.5 15.9 %copy-start.4 = (bf16[512,1024]{1,0:T(8,128)(2,1)S(1)}, bf16[512,1024]{1,0:T(8,128)(2,1)}, u32[]{:S(2)}) copy-start(bf16[512,1024]{1,0:T(8,128)(2,1)} %wo_ref.1) | copy-start | bytes 3145732
  81.6 15.9 %copy-start.5 = (bf16[8,128,512]{2,1,0:T(8,128)(2,1)S(1)}, bf16[8,128,512]{2,1,0:T(8,128)(2,1)}, u32[]{:S(2)}) copy-start(bf16[8,128,512]{2,1,0:T(8,128)(2,1)} %get-tuple-element.42.prow_ref) | copy-start | bytes 3145732
  81.6 15.9 %copy-start.7 = (bf16[512,512]{1,0:T(8,128)(2,1)S(1)}, bf16[512,512]{1,0:T(8,128)(2,1)}, u32[]{:S(2)}) copy-start(bf16[512,512]{1,0:T(8,128)(2,1)} %get-tuple-element.41.q_ref) | copy-start | bytes 1572868
  84.0 5.1 %collective-permute-start.3 = (f32[520,128]{1,0:T(8,128)S(1)}, f32[520,128]{1,0:T(8,128)S(1)}, u32[]{:S(2)}, u32[]{:S(2)}) collective-permute-start(f32[520,128]{1,0:T(8,128)S(1)} %shard_map.136.own_ref), channel_id=1, source_target_pairs={{0,1},{1,0},{2,3},{3,2},{4,5},{5,4},{6,7},{7,6},{8,9},{9,8},{10,11... | collective-permute-start | bytes 798728 | tf_op jit(solution)/shard_map/ppermute | solution.py:583
  89.1 8.3 %collective-permute-start.4 = (bf16[544,128]{1,0:T(8,128)(2,1)S(1)}, bf16[544,128]{1,0:T(8,128)(2,1)S(1)}, u32[]{:S(2)}, u32[]{:S(2)}) collective-permute-start(bf16[544,128]{1,0:T(8,128)(2,1)S(1)} %get-tuple-element.34), channel_id=1, source_target_pairs={{0,2},{2,0},{1,3},{3,1},{4,6},{6,4},{5,7},{7,5},{8,10},{10,8},{9,1... | collective-permute-start | bytes 417800 | tf_op jit(solution)/shard_map/ppermute | solution.py:584

commit v9 on v8

--- a/solution.py
+++ b/solution.py
@@ -251,7 +251,7 @@
                 probs = expo * (1.0 / jnp.sum(expo, -1, keepdims=True))
                 prob_ref[half, rows, :] = probs.astype(bf16)
             prow_ref[head] = prob_ref[half, :ROWS, :]
-            pcol_ref[head] = jnp.transpose(prob_ref[half, :, :ROWS])
+            pcol_ref[head] = prob_ref[half, :, :ROWS]
             mixes.append(dot(prob_ref[half], v_ref[:, lanes]))
         att_ref[:, lanes] = jnp.where(first, mixes[0], mixes[1]).astype(bf16)
         two = pl.ds(2 * pair, 2)
@@ -293,7 +293,7 @@
         square,
         square,
         shape((HEADS, ROWS, L), bf16),
-        shape((HEADS, ROWS, L), bf16),
+        shape((HEADS, L, ROWS), bf16),
         shape((L, D), f32),
         shape((L, E), f32),
         shape((L, E), f32),
@@ -323,6 +323,15 @@
         flops=6 * 10**9,
         limit=52,
     )(keep, bias, *blocks, w_query, w_key, w_value, w_out, ln_gain[None], w_proj)
+
+
+def turn_kernel(in_ref, out_ref):
+    for head in range(HEADS):
+        out_ref[head] = jnp.transpose(in_ref[head])
+
+
+def turn(pcol):
+    return call(turn_kernel, shape((HEADS, ROWS, L), bf16), [BLOCK], flops=5 * 10**9, limit=56)(pcol)
 
 
 def sums_kernel(plane_ref, embed_ref, send_ref, sums_ref, weight_ref, keep_ref):
@@ -578,6 +587,7 @@
         keep, bias, blocks, w_query, w_key, w_value, w_out, ln_gain, w_proj
     )
     send, sums, weight = sums_call(plane, embed)
+    kept[5] = turn(kept[5])
     table = spread(send, DP)
     partial = grads_call(table, plane, embed, sums, weight)
     summed, half = add_call(partial, lax.ppermute(partial, "core", SWAP))

time: 104 us -> 113 us (1.087)
  local copies, waits for them, and re-layouts: 0.36 us -> 8.94 us
  Pallas kernels: 23.6 us -> 27 us
  waiting for transfers between devices: 9.95 us -> 7.39 us
    unnamed x32 -> x42, local copies, waits for them, and re-layouts: 0.36 us -> 8.94 us
    pallas_call x0 -> x1, Pallas kernels: none -> 2.69 us  [turn(): call(turn_kernel, shape((HEADS, ROWS, L), bf16), [BLOCK], flops=5 * 10 **...]
    ppermute x1, waiting for transfers between devices: 3.75 us -> 1.19 us  [body(): got = lax.ppermute(half, 'yhi', SWAP)]
  transfers between devices with their start and end apart: 7 -> 7, of which waited for: 4 -> 4; matrix products, arithmetic and copies ran while one was open for 0% -> 0% of each run, Pallas kernels for 12% -> 13%
where the time goes in v9:
time: 113 us
  starting transfers between devices  43.7 us (39%)
  Pallas kernels  27 us (24%)
  blocking collectives  23.3 us (21%)
  local copies, waits for them, and re-layouts  8.94 us (8%)
  waiting for transfers between devices  7.39 us (7%)
  between operations  2.33 us (2%)
    all_to_all x1, blocking collectives, spread(): return lax.all_to_all(x, axes, 0, 0)  23.3 us
    all_to_all x2, starting transfers between devices, spread(): return lax.all_to_all(x, axes, 0, 0)  20.9 us
    pallas_call x1, Pallas kernels, forward(): call(forward_kernel, outs, [ANY] * 6 + [HBM] * 6, tuple((HBM for _ in out...  10.7 us
    unnamed x42, local copies, waits for them, and re-layouts  8.94 us
    ppermute x1, starting transfers between devices, body(): by_both = lax.ppermute(by_yhi, 'core', SWAP)  6.69 us
    pallas_call x1, Pallas kernels, backward(): call(backward_kernel, (shape((ROWS, D), bf16), shape((1,), f32)), [VMEM]...  5.33 us
    ppermute x1, starting transfers between devices, body(): by_yhi = lax.ppermute(own, 'yhi', SWAP)  4.82 us
    ppermute x1, starting transfers between devices, body(): got = lax.ppermute(half, 'yhi', SWAP)  4.52 us
  transfers between devices with their start and end apart: 7, of which 4 were waited for; matrix products, arithmetic and copies ran while one was open for 0% of the time, Pallas kernels for 13%

profile of v9, /device:TPU:1, one launch (start us, length us, event | category | flops | bytes accessed | tf_op | source)
XLA Modules:
  0.0 112.6 jit_solution(10824011123887112873)
XLA Ops:
  1.3 1.8 %shard_map.131 = (bf16[16,40,128]{2,1,0:T(8,128)(2,1)}, bf16[144,1024]{1,0:T(8,128)(2,1)}) custom-call(s32[1,1]{1,0:T(1,128)} %bitcast.9.pos_ref, bf16[32,128]{1,0:T(8,128)(2,1)} %bitcast.14, bf16[1,32]{1,0:T(2,128)(2,1)} %mask_ref.1, s32[1,128]{1,0:T(1,128)} %bitcast.15, bf16[128,1024]{1,0:T(8,128)(2,1)} %hidden_ref.1), custom_call_target="tpu_custom_call" | custom-call | bytes 4194304 | tf_op jit(solution)/shard_map/pallas_call | solution.py:111
  3.1 15.7 %all-to-all-start = ((bf16[16,40,128]{2,1,0:T(8,128)(2,1)}), bf16[16,40,128]{2,1,0:T(8,128)(2,1)S(1)}, u32[]{:S(2)}, u32[]{:S(2)}) async-start(bf16[16,40,128]{2,1,0:T(8,128)(2,1)} %get-tuple-element.24), calls=%async_computation | async-start | bytes 327680 | tf_op jit(solution)/shard_map/all_to_all | solution.py:559
  18.8 2.9 %collective-permute-start = (bf16[144,1024]{1,0:T(8,128)(2,1)}, bf16[144,1024]{1,0:T(8,128)(2,1)S(1)}, u32[]{:S(2)}, u32[]{:S(2)}) collective-permute-start(bf16[144,1024]{1,0:T(8,128)(2,1)} %get-tuple-element.25.x0_any), channel_id=1, source_target_pairs={{0,1},{1,0},{2,3},{3,2},{4,5},{5,4},{6,7},{7,6},{8,9},{9,8},{10,11... | collective-permute-start | bytes 884744 | tf_op jit(solution)/shard_map/ppermute | solution.py:577
  21.7 4.8 %collective-permute-start.1 = (bf16[144,1024]{1,0:T(8,128)(2,1)}, bf16[144,1024]{1,0:T(8,128)(2,1)S(1)}, u32[]{:S(2)}, u32[]{:S(2)}) collective-permute-start(bf16[144,1024]{1,0:T(8,128)(2,1)} %get-tuple-element.25.x0_any), channel_id=1, source_target_pairs={{0,2},{2,0},{1,3},{3,1},{4,6},{6,4},{5,7},{7,5},{8,10},{10,8},{9,1... | collective-permute-start | bytes 884744 | tf_op jit(solution)/shard_map/ppermute | solution.py:578
  26.5 0.0 collective-permute-done.after_ref.x1_any
  26.6 4.5 %all-to-all-done.line_ref = bf16[16,40,128]{2,1,0:T(8,128)(2,1)S(1)} async-done(((bf16[16,40,128]{2,1,0:T(8,128)(2,1)}), bf16[16,40,128]{2,1,0:T(8,128)(2,1)S(1)}, u32[]{:S(2)}, u32[]{:S(2)}) %all-to-all-start) | async-done | bytes 163872 | tf_op jit(solution)/shard_map/all_to_all | solution.py:559
  31.1 1.2 %shard_map.132 = bf16[8,544,128]{2,1,0:T(8,128)(2,1)} custom-call(bf16[16,40,128]{2,1,0:T(8,128)(2,1)S(1)} %all-to-all-done.line_ref, bf16[144,1024]{1,0:T(8,128)(2,1)S(1)} %collective-permute-done.after_ref.x1_any), custom_call_target="tpu_custom_call" | custom-call | bytes 4194304 | tf_op jit(solution)/shard_map/pallas_call | solution.py:130
  32.2 0.0 copy-start.11
  32.2 5.2 %all-to-all-start.1 = ((bf16[8,544,128]{2,1,0:T(8,128)(2,1)}), bf16[8,544,128]{2,1,0:T(8,128)(2,1)S(1)}, u32[]{:S(2)}, u32[]{:S(2)}) async-start(bf16[8,544,128]{2,1,0:T(8,128)(2,1)} %shard_map.132), calls=%async_computation.1 | async-start | bytes 2228224 | tf_op jit(solution)/shard_map/all_to_all | solution.py:559
  37.4 0.0 copy-start.14
  37.4 0.0 copy-start.20
  37.4 0.0 collective-permute-done.1.x2_any
  37.4 0.0 copy-start.12
  37.4 6.7 %collective-permute-start.2 = (bf16[144,1024]{1,0:T(8,128)(2,1)S(1)}, bf16[144,1024]{1,0:T(8,128)(2,1)S(1)}, u32[]{:S(2)}, u32[]{:S(2)}) collective-permute-start(bf16[144,1024]{1,0:T(8,128)(2,1)S(1)} %collective-permute-done.1.x2_any), channel_id=1, source_target_pairs={{0,1},{1,0},{2,3},{3,2},{4,5},{5,4},{6,7},{7,6},{8,9},{9,8},{10,11... | collective-permute-start | bytes 884744 | tf_op jit(solution)/shard_map/ppermute | solution.py:583
  44.8 0.5 collective-permute-done.2.x3_any
  45.3 0.0 copy-done.11
  45.3 0.0 copy-start.13
  45.3 0.4 shard_map.133
  45.8 0.0 copy-done.12
  45.8 0.3 copy-done.13
  46.1 0.0 copy-done.14
  46.1 0.0 copy-done.20
  46.1 10.7 %shard_map.134 = (bf16[512,512]{1,0:T(8,128)(2,1)}, bf16[512,512]{1,0:T(8,128)(2,1)}, bf16[512,512]{1,0:T(8,128)(2,1)}, bf16[512,512]{1,0:T(8,128)(2,1)}, bf16[8...) custom-call(bf16[512,128]{1,0:T(8,128)(2,1)S(1)} %get-tuple-element., ...), custom_call_target="tpu_custom_call" | custom-call | flops 6000000000 | bytes 4194304 | tf_op jit(solution)/shard_map/pallas_call | solution.py:317
  56.7 0.0 copy-start.16
  56.8 0.7 copy-done.16
  57.4 0.0 copy-start.18
  57.4 0.7 copy-done.18
  58.1 0.0 all-to-all-done.1.plane_ref
  58.2 1.7 %shard_map.135 = (f32[128,128]{1,0:T(8,128)S(1)}, f32[32,128]{1,0:T(8,128)S(1)}, f32[32,128]{1,0:T(8,128)S(1)}) custom-call(bf16[8,544,128]{2,1,0:T(8,128)(2,1)S(1)} %all-to-all-done.1.plane_ref, bf16[1024,128]{1,0:T(8,128)(2,1)S(1)} %get-tuple-element.29.embed_ref), custom_call_target="tpu_custom_call" | custom-call | flops 1000000000 | bytes 4194304 | tf_op jit(solution)/shard_map/pallas_call | solution.py:364
  59.9 23.3 %all_to_all.21 = f32[128,1,128]{2,1,0:T(1,128)S(1)} all-to-all(f32[128,1,128]{2,1,0:T(1,128)S(1)} %bitcast.11), channel_id=1, replica_groups=mesh['z'=16,'ylo'=2,'x'=4,'yhi'=2,'core'=2] {'z','ylo','x'}, dimensions={0} | all-to-all | bytes 131072 | tf_op jit(solution)/shard_map/all_to_all | solution.py:559
  83.1 2.4 %shard_map.136.own_ref = f32[520,128]{1,0:T(8,128)S(1)} custom-call(f32[128,128]{1,0:T(8,128)S(1)} %bitcast.10, f32[32,128]{1,0:T(8,128)S(1)} %get-tuple-element.31.sums_ref, f32[32,128]{1,0:T(8,128)S(1)} %get-tuple-element.32.weight_ref, bf16[8,544,128]{2,1,0:T(8,128)(2,1)S(1)} %all-to-all-done.1.plane_ref, bf16[1024,128]{1,0:T(8,128)(2,1)S(1)} %get-tuple-element.29.embed_ref), custom_call_target="tpu_custom_call" | custom-call | flops 2000000000 | bytes 4194304 | tf_op jit(solution)/shard_map/pallas_call | solution.py:411
  85.6 3.9 %collective-permute-start.3 = (f32[520,128]{1,0:T(8,128)S(1)}, f32[520,128]{1,0:T(8,128)S(1)}, u32[]{:S(2)}, u32[]{:S(2)}) collective-permute-start(f32[520,128]{1,0:T(8,128)S(1)} %shard_map.136.own_ref), channel_id=1, source_target_pairs={{0,1},{1,0},{2,3},{3,2},{4,5},{5,4},{6,7},{7,6},{8,9},{9,8},{10,11... | collective-permute-start | bytes 798728 | tf_op jit(solution)/shard_map/ppermute | solution.py:593
  89.5 1.1 %collective-permute-done.3.got_ref = f32[520,128]{1,0:T(8,128)S(1)} collective-permute-done((f32[520,128]{1,0:T(8,128)S(1)}, f32[520,128]{1,0:T(8,128)S(1)}, u32[]{:S(2)}, u32[]{:S(2)}) %collective-permute-start.3) | collective-permute-done | bytes 266272 | tf_op jit(solution)/shard_map/ppermute | solution.py:593
  90.7 0.7 shard_map.137
  91.4 4.5 %collective-permute-start.4 = (bf16[544,128]{1,0:T(8,128)(2,1)}, bf16[544,128]{1,0:T(8,128)(2,1)S(1)}, u32[]{:S(2)}, u32[]{:S(2)}) collective-permute-start(bf16[544,128]{1,0:T(8,128)(2,1)} %get-tuple-element.34), channel_id=1, source_target_pairs={{0,2},{2,0},{1,3},{3,1},{4,6},{6,4},{5,7},{7,5},{8,10},{10,8},{9,1... | collective-permute-start | bytes 417800 | tf_op jit(solution)/shard_map/ppermute | solution.py:594
  95.9 0.0 copy-start
  95.9 0.0 copy-start.1
  95.9 0.0 copy-start.2
  95.9 0.0 copy-start.3
  95.9 0.0 copy-start.4
  96.0 0.0 copy-start.5
  96.0 0.0 copy-start.7
  96.0 2.7 %shard_map.138.pcol_ref = bf16[8,128,512]{2,1,0:T(8,128)(2,1)} custom-call(bf16[8,512,128]{2,1,0:T(8,128)(2,1)} %get-tuple-element.43.in_ref), custom_call_target="tpu_custom_call" | custom-call | flops 5000000000 | bytes 4194304 | tf_op jit(solution)/shard_map/pallas_call | solution.py:334
  98.7 1.2 %collective-permute-done.4.got_ref = bf16[544,128]{1,0:T(8,128)(2,1)S(1)} collective-permute-done((bf16[544,128]{1,0:T(8,128)(2,1)}, bf16[544,128]{1,0:T(8,128)(2,1)S(1)}, u32[]{:S(2)}, u32[]{:S(2)}) %collective-permute-start.4) | collective-permute-done | bytes 139296 | tf_op jit(solution)/shard_map/ppermute | solution.py:594
  99.9 0.0 copy-done
  99.9 0.0 copy-done.1
  99.9 0.0 copy-done.2
  99.9 0.0 copy-done.3
  99.9 0.0 copy-done.4
  99.9 0.0 copy-done.5
  99.9 0.0 copy-done.7
  99.9 0.0 copy-start.6
  99.9 1.2 %copy-done.6 = bf16[8,128,512]{2,1,0:T(8,128)(2,1)S(1)} copy-done((bf16[8,128,512]{2,1,0:T(8,128)(2,1)S(1)}, bf16[8,128,512]{2,1,0:T(8,128)(2,1)}, u32[]{:S(2)}) %copy-start.6) | copy-done | bytes 1048600
  101.1 0.0 copy-start.8
  101.1 1.0 copy-done.8
  102.2 1.0 copy-done.9
  103.2 0.0 copy-start.10
  103.2 1.0 copy-done.10
  104.3 0.0 copy-start.15
  104.3 0.9 copy-done.15
  105.2 0.0 copy-start.17
  105.2 0.9 copy-done.17
  106.2 0.9 copy-done.19
  107.1 5.3 %shard_map.139 = (bf16[128,1024]{1,0:T(8,128)(2,1)}, f32[1]{0:T(128)}) custom-call(f32[520,128]{1,0:T(8,128)S(1)} %get-tuple-element.33.sum_ref, bf16[544,128]{1,0:T(8,128)(2,1)S(1)} %collective-permute-done.4.got_ref, f32[512,128]{1,0:T(8,128)S(1)} %copy-done.19, bf16[1024,128]{1,0:T(8,128)(2,1)S(1)} %copy-done.15, f32[512,128]{1,0:T(8,128)S(1)} %copy-done.17, ...), custom_call_target="tpu_custom_call" | custom-call | flops 3000000000 | bytes 4194304 | tf_op jit(solution)/shard_map/pallas_call | solution.py:537
  (2 shorter events, 0.0 us)
Async XLA Ops:
  3.1 28.0 %all-to-all-start = ((bf16[16,40,128]{2,1,0:T(8,128)(2,1)}), bf16[16,40,128]{2,1,0:T(8,128)(2,1)S(1)}, u32[]{:S(2)}, u32[]{:S(2)}) async-start(bf16[16,40,128]{2,1,0:T(8,128)(2,1)} %get-tuple-element.24), calls=%async_computation | async-start | bytes 327680 | tf_op jit(solution)/shard_map/all_to_all | solution.py:559
  18.8 7.7 %collective-permute-start = (bf16[144,1024]{1,0:T(8,128)(2,1)}, bf16[144,1024]{1,0:T(8,128)(2,1)S(1)}, u32[]{:S(2)}, u32[]{:S(2)}) collective-permute-start(bf16[144,1024]{1,0:T(8,128)(2,1)} %get-tuple-element.25.x0_any), channel_id=1, source_target_pairs={{0,1},{1,0},{2,3},{3,2},{4,5},{5,4},{6,7},{7,6},{8,9},{9,8},{10,11... | collective-permute-start | bytes 884744 | tf_op jit(solution)/shard_map/ppermute | solution.py:577
  21.7 15.7 %collective-permute-start.1 = (bf16[144,1024]{1,0:T(8,128)(2,1)}, bf16[144,1024]{1,0:T(8,128)(2,1)S(1)}, u32[]{:S(2)}, u32[]{:S(2)}) collective-permute-start(bf16[144,1024]{1,0:T(8,128)(2,1)} %get-tuple-element.25.x0_any), channel_id=1, source_target_pairs={{0,2},{2,0},{1,3},{3,1},{4,6},{6,4},{5,7},{7,5},{8,10},{10,8},{9,1... | collective-permute-start | bytes 884744 | tf_op jit(solution)/shard_map/ppermute | solution.py:578
  32.2 13.1 %copy-start.11 = (bf16[144,1024]{1,0:T(8,128)(2,1)S(1)}, bf16[144,1024]{1,0:T(8,128)(2,1)}, u32[]{:S(2)}) copy-start(bf16[144,1024]{1,0:T(8,128)(2,1)} %get-tuple-element.25.x0_any) | copy-start | bytes 884740
  32.2 25.9 %all-to-all-start.1 = ((bf16[8,544,128]{2,1,0:T(8,128)(2,1)}), bf16[8,544,128]{2,1,0:T(8,128)(2,1)S(1)}, u32[]{:S(2)}, u32[]{:S(2)}) async-start(bf16[8,544,128]{2,1,0:T(8,128)(2,1)} %shard_map.132), calls=%async_computation.1 | async-start | bytes 2228224 | tf_op jit(solution)/shard_map/all_to_all | solution.py:559
  37.4 8.7 %copy-start.14 = (bf16[1024,128]{1,0:T(8,128)(2,1)S(1)}, bf16[1024,128]{1,0:T(8,128)(2,1)}, u32[]{:S(2)}) copy-start(bf16[1024,128]{1,0:T(8,128)(2,1)} %wp_ref.1) | copy-start | bytes 786436
  37.4 8.7 %copy-start.20 = (f32[1024]{0:T(1024)S(1)}, f32[1024]{0:T(1024)}, u32[]{:S(2)}) copy-start(f32[1024]{0:T(1024)} %param.19) | copy-start | bytes 12292
  37.4 8.4 %copy-start.12 = (bf16[144,1024]{1,0:T(8,128)(2,1)}, bf16[144,1024]{1,0:T(8,128)(2,1)S(1)}, u32[]{:S(2)}) copy-start(bf16[144,1024]{1,0:T(8,128)(2,1)S(1)} %collective-permute-done.1.x2_any) | copy-start | bytes 884740
  37.4 7.9 %collective-permute-start.2 = (bf16[144,1024]{1,0:T(8,128)(2,1)S(1)}, bf16[144,1024]{1,0:T(8,128)(2,1)S(1)}, u32[]{:S(2)}, u32[]{:S(2)}) collective-permute-start(bf16[144,1024]{1,0:T(8,128)(2,1)S(1)} %collective-permute-done.1.x2_any), channel_id=1, source_target_pairs={{0,1},{1,0},{2,3},{3,2},{4,5},{5,4},{6,7},{7,6},{8,9},{9,8},{10,11... | collective-permute-start | bytes 884744 | tf_op jit(solution)/shard_map/ppermute | solution.py:583
  45.3 0.8 copy-start.13
  56.7 0.7 copy-start.16
  57.4 0.7 copy-start.18
  85.6 5.1 %collective-permute-start.3 = (f32[520,128]{1,0:T(8,128)S(1)}, f32[520,128]{1,0:T(8,128)S(1)}, u32[]{:S(2)}, u32[]{:S(2)}) collective-permute-start(f32[520,128]{1,0:T(8,128)S(1)} %shard_map.136.own_ref), channel_id=1, source_target_pairs={{0,1},{1,0},{2,3},{3,2},{4,5},{5,4},{6,7},{7,6},{8,9},{9,8},{10,11... | collective-permute-start | bytes 798728 | tf_op jit(solution)/shard_map/ppermute | solution.py:593
  91.4 8.5 %collective-permute-start.4 = (bf16[544,128]{1,0:T(8,128)(2,1)}, bf16[544,128]{1,0:T(8,128)(2,1)S(1)}, u32[]{:S(2)}, u32[]{:S(2)}) collective-permute-start(bf16[544,128]{1,0:T(8,128)(2,1)} %get-tuple-element.34), channel_id=1, source_target_pairs={{0,2},{2,0},{1,3},{3,1},{4,6},{6,4},{5,7},{7,5},{8,10},{10,8},{9,1... | collective-permute-start | bytes 417800 | tf_op jit(solution)/shard_map/ppermute | solution.py:594
  95.9 4.0 %copy-start = (f32[512,1024]{1,0:T(8,128)S(1)}, f32[512,1024]{1,0:T(8,128)}, u32[]{:S(2)}) copy-start(f32[512,1024]{1,0:T(8,128)} %get-tuple-element.37.unit_ref) | copy-start | bytes 6291460
  95.9 4.0 %copy-start.1 = (bf16[1024,512]{1,0:T(8,128)(2,1)S(1)}, bf16[1024,512]{1,0:T(8,128)(2,1)}, u32[]{:S(2)}) copy-start(bf16[1024,512]{1,0:T(8,128)(2,1)} %wq_ref.1) | copy-start | bytes 3145732
  95.9 3.9 %copy-start.2 = (bf16[1024,512]{1,0:T(8,128)(2,1)S(1)}, bf16[1024,512]{1,0:T(8,128)(2,1)}, u32[]{:S(2)}) copy-start(bf16[1024,512]{1,0:T(8,128)(2,1)} %wk_ref.1) | copy-start | bytes 3145732
  95.9 3.9 %copy-start.3 = (bf16[1024,512]{1,0:T(8,128)(2,1)S(1)}, bf16[1024,512]{1,0:T(8,128)(2,1)}, u32[]{:S(2)}) copy-start(bf16[1024,512]{1,0:T(8,128)(2,1)} %wv_ref.1) | copy-start | bytes 3145732
  95.9 3.9 %copy-start.4 = (bf16[512,1024]{1,0:T(8,128)(2,1)S(1)}, bf16[512,1024]{1,0:T(8,128)(2,1)}, u32[]{:S(2)}) copy-start(bf16[512,1024]{1,0:T(8,128)(2,1)} %wo_ref.1) | copy-start | bytes 3145732
  96.0 3.9 %copy-start.5 = (bf16[8,128,512]{2,1,0:T(8,128)(2,1)S(1)}, bf16[8,128,512]{2,1,0:T(8,128)(2,1)}, u32[]{:S(2)}) copy-start(bf16[8,128,512]{2,1,0:T(8,128)(2,1)} %get-tuple-element.42.prow_ref) | copy-start | bytes 3145732
  96.0 3.9 %copy-start.7 = (bf16[512,512]{1,0:T(8,128)(2,1)S(1)}, bf16[512,512]{1,0:T(8,128)(2,1)}, u32[]{:S(2)}) copy-start(bf16[512,512]{1,0:T(8,128)(2,1)} %get-tuple-element.41.q_ref) | copy-start | bytes 1572868
  99.9 1.2 %copy-start.6 = (bf16[8,128,512]{2,1,0:T(8,128)(2,1)S(1)}, bf16[8,128,512]{2,1,0:T(8,128)(2,1)}, u32[]{:S(2)}) copy-start(bf16[8,128,512]{2,1,0:T(8,128)(2,1)} %shard_map.138.pcol_ref) | copy-start | bytes 3145732
  101.1 1.0 copy-start.8
  102.2 1.0 copy-start.9
  103.2 1.0 copy-start.10
  104.3 0.9 copy-start.15
  105.2 0.9 copy-start.17
  106.2 0.9 copy-start.19
